TPU v7x, 128 devices: a whole 4x4x4 slice. The times are simulated.
128 devices in a mesh: fsdp: 2 (over core), dp: 64 (over z, y, x).
Axes of the slice: x: 4, y: 4, z: 4, core: 2. Of those that a mesh axis runs over, the one named last changes fastest.
Arguments:
- grad_parts: bfloat16 [64, 8, 64, 8, 512], P('dp', None, None, 'fsdp'), may hold values from -0.1875 to 0.1875
- slot_block: int32 [2, 8], replicated, may hold values from -1 to 7, as said below
- gram_left: float32 [16, 512, 512], P('fsdp', 'dp'), may hold values from -1.2 to 1.2
- gram_right: float32 [16, 512, 512], P('fsdp', 'dp'), may hold values from -1.2 to 1.2
- left_basis_t: bfloat16 [16, 512, 512], P('fsdp', 'dp'), may hold values from -0.25 to 0.25
- right_basis: bfloat16 [16, 512, 512], P('fsdp', 'dp'), may hold values from -0.25 to 0.25
- moment_first: float32 [16, 512, 512], P('fsdp', 'dp'), may hold values from -0.3 to 0.3
- moment_second: float32 [16, 512, 512], P('fsdp', 'dp'), may hold values from 0.002 to 0.05
Outputs:
- gram_left_new: float32 [16, 512, 512], P('fsdp', 'dp')
- gram_right_new: float32 [16, 512, 512], P('fsdp', 'dp')
- moment_first_new: float32 [16, 512, 512], P('fsdp', 'dp')
- moment_second_new: float32 [16, 512, 512], P('fsdp', 'dp')
- direction: bfloat16 [8, 64, 8, 512], P(None, 'dp', 'fsdp')
Inputs may be any that keep to these rules, and one draw needn't show every extreme that they name: `slot_block`: every block 0 to 7 stands in exactly one slot; an owner's filled slots come first and the rest hold -1; some owner has all 8 slots filled.
All inputs are finite; a program needn't handle non-finite values.
Results may differ from a plain program's by a relative error of at most 0.0065.
Values may be sent and summed in bfloat16 or wider, within the bound.
No kernel may reach another device: no remote copies, remote signals or barrier semaphores. Data moves between devices by JAX's collectives and lax.ppermute only.
A program may use at most 64 MiB of HBM per device.

v0:
```python
import jax
import jax.numpy as jnp
from jax import lax
from jax.sharding import PartitionSpec as P

shampoo_beta = 0.9
adam_first = 0.95
adam_second = 0.95
epsilon = 1e-08


def shards(
    grad_parts,
    slot_block,
    gram_left,
    gram_right,
    left_basis_t,
    right_basis,
    moment_first,
    moment_second,
):
    partial_terms = grad_parts[0].astype(jnp.float32)
    summed = lax.psum_scatter(partial_terms, "dp", scatter_dimension=1, tiled=True)
    grad_rows = summed[:, 0].astype(jnp.bfloat16)
    block_total = grad_rows.shape[0]
    owner_count = slot_block.shape[0]
    capacity = slot_block.shape[1]
    slot_order = slot_block.T
    occupied = slot_order >= 0
    picked = grad_rows[jnp.maximum(slot_order, 0)]
    outgoing = jnp.where(occupied[:, :, None, None], picked, jnp.zeros((), jnp.bfloat16))
    arrived = lax.all_to_all(outgoing, "fsdp", split_axis=1, concat_axis=1, tiled=True)
    row_span = arrived.shape[1] * arrived.shape[2]
    width = arrived.shape[3]
    local_grad = arrived.reshape(capacity, row_span, width)
    full_grad = lax.all_gather(local_grad, "dp", axis=1, tiled=True)
    row_start = lax.axis_index("dp") * row_span
    gram_l_new = shampoo_beta * gram_left + (1.0 - shampoo_beta) * jnp.einsum(
        "crk,cjk->crj", local_grad, full_grad, preferred_element_type=jnp.float32
    )
    grad_cols = lax.dynamic_slice_in_dim(full_grad, row_start, row_span, 2)
    gram_r_new = shampoo_beta * gram_right + (1.0 - shampoo_beta) * jnp.einsum(
        "cki,ckj->cij", grad_cols, full_grad, preferred_element_type=jnp.float32
    )
    half_rot = jnp.einsum(
        "crk,ckj->crj", left_basis_t, full_grad, preferred_element_type=jnp.float32
    ).astype(jnp.bfloat16)
    rotated = jnp.einsum(
        "crk,ckj->crj",
        half_rot,
        lax.all_gather(right_basis, "dp", axis=1, tiled=True),
        preferred_element_type=jnp.float32,
    )
    first_new = adam_first * moment_first + (1.0 - adam_first) * rotated
    second_new = adam_second * moment_second + (1.0 - adam_second) * rotated * rotated
    scaled = (first_new / (jnp.sqrt(second_new) + epsilon)).astype(jnp.bfloat16)
    back_right = jnp.einsum(
        "crk,cjk->crj",
        scaled,
        lax.all_gather(right_basis, "dp", axis=1, tiled=True),
        preferred_element_type=jnp.float32,
    ).astype(jnp.bfloat16)
    update_rows = lax.psum_scatter(
        jnp.einsum("cri,crj->icj", left_basis_t, back_right, preferred_element_type=jnp.float32),
        "dp",
        scatter_dimension=0,
        tiled=True,
    )
    outgoing_update = update_rows.astype(jnp.bfloat16).reshape(
        owner_count, row_span // owner_count, capacity, width
    )
    returned = lax.all_to_all(outgoing_update, "fsdp", split_axis=0, concat_axis=0, tiled=True)
    values = jnp.swapaxes(returned, 1, 2)
    target = jnp.where(slot_block >= 0, slot_block, block_total)
    placed = (
        jnp.zeros((block_total, row_span // owner_count, width), jnp.bfloat16)
        .at[target]
        .set(values, mode="drop")
    )
    return (gram_l_new, gram_r_new, first_new, second_new, placed[:, None])


def solution(mesh):
    return jax.shard_map(
        shards,
        mesh=mesh,
        in_specs=(
            P("dp", None, None, "fsdp", None),
            P(),
            P("fsdp", "dp", None),
            P("fsdp", "dp", None),
            P("fsdp", "dp", None),
            P("fsdp", "dp", None),
            P("fsdp", "dp", None),
            P("fsdp", "dp", None),
        ),
        out_specs=(
            P("fsdp", "dp", None),
            P("fsdp", "dp", None),
            P("fsdp", "dp", None),
            P("fsdp", "dp", None),
            P(None, "dp", "fsdp", None),
        ),
        check_vma=False,
    )
```

profile of v0, /device:TPU:0, one launch (start us, length us, event | category | flops | bytes accessed | tf_op | source)
XLA Modules:
  0.0 922.7 jit_solution(16699421896116061129)
XLA Ops:
  7.2 0.0 reduce-scatter.3.cloned.1.call-start
  7.3 6.1 bitcast_convert_fusion
  13.4 0.0 reduce-scatter.3.cloned.1.call-update
  13.4 0.0 all-gather.5.cloned.1.call-start
  13.4 0.7 all-gather.5.cloned.1.call-update
  14.1 0.0 all-gather.3.cloned.1.call-start
  14.2 0.1 copy.44
  14.3 0.1 reshape.25
  14.4 359.6 %reduce-scatter.3.cloned.1.call-done = f32[8,1,4,512]{3,0,2,1:T(8,128)} async-done(((f32[8,64,4,512]{3,0,2,1:T(8,128)}), f32[8,1,4,512]{3,0,2,1:T(8,128)}) %reduce-scatter.3.cloned.1.call-update) | async-done | bytes 65552 | tf_op jit(solution)/shard_map/reduce_scatter | solution.py:23
  374.0 0.8 convert_element_type.34
  374.8 0.6 gather_fusion
  375.4 0.1 copy_select_fusion
  375.6 3.8 all_to_all.10
  379.4 0.6 reshape.20
  380.0 0.0 all-gather.3.cloned.1.call-update
  380.0 0.0 reduce-scatter.5.cloned.1.call-start
  380.1 64.4 %all-gather.5.cloned.1.call-done = bf16[8,512,512]{2,1,0:T(8,128)(2,1)} async-done(((bf16[8,8,512]{2,1,0:T(8,128)(2,1)}), bf16[8,512,512]{2,1,0:T(8,128)(2,1)}) %all-gather.5.cloned.1.call-update) | async-done | bytes 4194320 | tf_op jit(solution)/shard_map/all_gather | solution.py:51
  444.5 75.1 %all-gather.3.cloned.1.call-done = bf16[8,512,512]{2,1,0:T(8,128)(2,1)} async-done(((bf16[8,8,512]{2,1,0:T(8,128)(2,1)}), bf16[8,512,512]{2,1,0:T(8,128)(2,1)}) %all-gather.3.cloned.1.call-update) | async-done | bytes 4194320 | tf_op jit(solution)/shard_map/all_gather | solution.py:36
  519.6 4.7 fusion.4
  524.3 7.8 convolution_bitcast_fusion
  532.1 10.5 %copy.48 = f32[512,8,512]{2,1,0:T(8,128)} copy(f32[512,8,512]{0,2,1:T(8,128)} %convolution_bitcast_fusion) | data formatting | bytes 16777216 | tf_op jit(solution)/shard_map/cri,crj->icj/transpose | solution.py:64
  542.7 0.0 reduce-scatter.5.cloned.1.call-update
  542.7 0.1 reshape.33
  542.8 0.8 copy-done.8
  543.6 4.4 fusion
  547.9 1.9 fusion.1
  549.8 359.9 %reduce-scatter.5.cloned.1.call-done = f32[8,8,512]{2,1,0:T(8,128)} async-done(((f32[512,8,512]{2,1,0:T(8,128)}), f32[8,8,512]{2,1,0:T(8,128)}) %reduce-scatter.5.cloned.1.call-update) | async-done | bytes 131088 | tf_op jit(solution)/shard_map/reduce_scatter | solution.py:63
  909.7 0.9 convert_element_type.32
  910.6 3.8 all_to_all.11
  914.4 0.1 copy.50
  914.5 1.0 scatter_fusion
  915.5 0.6 copy-done.5
  (27 shorter events, 0.1 us)
Async XLA Ops:
  7.2 512.5 %copy-start = (bf16[8,8,512]{2,1,0:T(8,128)(2,1)S(1)}, bf16[8,8,512]{2,1,0:T(8,128)(2,1)}, u32[]{:S(2)}) copy-start(bf16[8,8,512]{2,1,0:T(8,128)(2,1)} %param.12) | copy-start | bytes 196612
  7.2 7.0 copy-start.10
  7.2 512.4 %copy-start.6 = (f32[8,8,512]{2,1,0:T(8,128)S(1)}, f32[8,8,512]{2,1,0:T(8,128)}, u32[]{:S(2)}) copy-start(f32[8,8,512]{2,1,0:T(8,128)} %param.15) | copy-start | bytes 393220
  7.2 512.4 %copy-start.7 = (f32[8,8,512]{2,1,0:T(8,128)S(1)}, f32[8,8,512]{2,1,0:T(8,128)}, u32[]{:S(2)}) copy-start(f32[8,8,512]{2,1,0:T(8,128)} %param.14) | copy-start | bytes 393220
  7.2 366.8 %reduce-scatter.3.cloned.1.call-start = ((), (), s32[]{:S(2)}) async-start(), calls=%async_computation.4 | async-start | bytes 4259840 | tf_op jit(solution)/shard_map/reduce_scatter | solution.py:23
  13.4 431.1 %all-gather.5.cloned.1.call-start = ((), (), s32[]{:S(2)}) async-start(), calls=%async_computation.6 | async-start | bytes 4259840 | tf_op jit(solution)/shard_map/all_gather | solution.py:51
  14.1 505.5 %all-gather.3.cloned.1.call-start = ((), (), s32[]{:S(2)}) async-start(), calls=%async_computation.5 | async-start | bytes 4259840 | tf_op jit(solution)/shard_map/all_gather | solution.py:36
  380.0 529.6 %reduce-scatter.5.cloned.1.call-start = ((), (), s32[]{:S(2)}) async-start(), calls=%async_computation.7 | async-start | bytes 8519680 | tf_op jit(solution)/shard_map/reduce_scatter | solution.py:63
  524.3 7.9 copy-start.3
  524.3 7.9 copy-start.4
  542.6 0.9 copy-start.8
  542.7 5.2 copy-start.2
  542.7 5.2 copy-start.9
  543.6 4.4 copy-start.1
  915.5 0.6 copy-start.5
Sparse Core Ops, SparseCore 0:
  13.5 360.4 reduce-scatter.2
  377.0 67.4 all-gather.4
  448.1 71.4 all-gather.2
  542.8 366.8 reduce-scatter.4
where the time goes:
time: 924 us; the launch traced here: 923 us
  waiting for transfers between devices  860 us (93%)
  matrix products  18.7 us (2%)
  local copies, waits for them, and re-layouts  14.6 us (2%)
  between operations  13.9 us (2%)
    reduce_scatter x1, waiting for transfers between devices, shards(): lax.psum_scatter(jnp.einsum('cri,crj->icj', left_basis_t, back_right, pre...  360 us
    reduce_scatter x1, waiting for transfers between devices, shards(): lax.psum_scatter(partial_terms, 'dp', scatter_dimension=1, tiled=True)  360 us
    all_gather x1, waiting for transfers between devices, shards(): full_grad = lax.all_gather(local_grad, 'dp', axis=1, tiled=True)  75.1 us
    all_gather x1, waiting for transfers between devices, shards(): lax.all_gather(right_basis, 'dp', axis=1, tiled=True)  64.4 us
  transfers between devices with their start and end apart: 4, of which 4 were waited for; matrix products, arithmetic and copies ran while one was open for 1% of the time, Pallas kernels for 0%

commit v1 on v0

v1 whole, which is shorter than its diff:
```python
import jax
import jax.numpy as jnp
from jax import lax
from jax.experimental import pallas as pl
from jax.experimental.pallas import tpu as pltpu
from jax.sharding import PartitionSpec as P

shampoo_beta = 0.9
adam_first = 0.95
adam_second = 0.95
epsilon = 1e-08

GROUP = 8
AXES = ("fsdp", "dp")


def number(dp):
    b = g = 0
    for axis in range(3):
        place = (dp >> (2 * axis)) & 3
        wrap, inner = place >> 1, (place ^ (place >> 1)) & 1
        b += (inner if axis == 0 else wrap) << axis
        g += (wrap if axis == 0 else inner) << axis
    return b, g


PLACE = {number(dp): dp for dp in range(GROUP * GROUP)}
EIGHT = range(GROUP)


def device(c, b, g):
    return c * GROUP * GROUP + PLACE[b, g]


OVER_B = [[[device(c, b, g) for b in EIGHT] for g in EIGHT] for c in range(2)]
OVER_G = [[[device(c, b, g) for g in EIGHT] for b in EIGHT] for c in range(2)]
FIRST = OVER_B[0] + OVER_G[1]
SECOND = OVER_G[0] + OVER_B[1]
BLOCK = OVER_G[0] + OVER_G[1]
ALL = [[device(c, b, g) for b in EIGHT for g in EIGHT] for c in range(2)]


def exchange(x, groups):
    return lax.all_to_all(x, AXES, 0, 0, axis_index_groups=groups, tiled=True)


def swap_cores(x):
    return lax.ppermute(x, "fsdp", [(0, 1), (1, 0)])


def dot(a, b, ca=1, cb=0):
    return lax.dot_general(a, b, (((ca,), (cb,)), ((), ())), preferred_element_type=jnp.float32)


def iota(shape, axis):
    return lax.broadcasted_iota(jnp.int32, shape, axis)


def one_hot(hit):
    return jnp.where(hit, 1.0, 0.0).astype(jnp.bfloat16)


WHOLE = pl.BlockSpec(memory_space=pltpu.VMEM)
SCALARS = pl.BlockSpec(memory_space=pltpu.SMEM)
FAR = pl.BlockSpec(memory_space=pltpu.HBM)


def local_call(kernel, name, out_shape, in_specs, scratch=(), vmem=40, out=WHOLE):
    return pl.pallas_call(
        kernel,
        out_shape=out_shape,
        in_specs=in_specs,
        out_specs=jax.tree.map(lambda _: out, out_shape),
        scratch_shapes=list(scratch),
        compiler_params=pltpu.CompilerParams(vmem_limit_bytes=vmem * 2**20),
        name=name,
    )


def chain_kernel(raw, swapped, right, left_t, first, second, out):
    bf16 = jnp.bfloat16
    core = lax.axis_index("fsdp")
    lane = number(lax.axis_index("dp"))[1]
    size = raw.shape[1]
    picks = size // 8

    n = iota((256, 256), 0)
    at = ((n >> 2) & 1) * 128 + (n >> 6) * 32 + ((n >> 3) & 7) * 4 + (n & 3)
    pick = one_hot(iota((256, 256), 1) == at)
    low = jnp.where(core == 0, raw[...], swapped[...])
    high = jnp.where(core == 0, swapped[...], raw[...])
    block = []
    for i in range(0, size // 2, 128):
        rows = jnp.concatenate([low[i : i + 128], high[i : i + 128]], axis=0)
        block.append(dot(pick, rows).astype(bf16))
    block = jnp.concatenate(block, axis=0)

    half_rot = dot(left_t[...], block).astype(bf16)
    rotated = dot(half_rot, right[...])
    new_first = adam_first * first[...] + (1.0 - adam_first) * rotated
    new_second = adam_second * second[...] + (1.0 - adam_second) * rotated * rotated
    scaled = (new_first / (jnp.sqrt(new_second) + epsilon)).astype(bf16)
    back = dot(scaled, right[...], 1, 1).astype(bf16)
    update = dot(left_t[...], back, 0, 0)

    own = one_hot(iota((picks, size), 1) == iota((picks, size), 0) * 8 + lane)
    gram_l = dot(dot(own, block).astype(bf16), block, 1, 1).astype(bf16)
    gram_r = dot(dot(block, own, 1, 1).astype(bf16), block, 0, 0).astype(bf16)

    upper = rotated.astype(bf16)
    lower = (rotated - upper.astype(jnp.float32)).astype(bf16)
    rows = jnp.concatenate([gram_l, gram_r, upper, lower], axis=0)
    n, col = iota((size, 4 * picks), 0), iota((size, 4 * picks), 1)
    spread = one_hot(col == ((n & 7) - 4 * (1 - core)) * picks + (n >> 3))
    kept = (iota((size, size), 0) & 4) == 4 * core
    result = jnp.where(kept, update, dot(spread, rows))
    order = [PLACE[b, g] * 8 for b in EIGHT for g in EIGHT]
    out[...] = jnp.concatenate([result[at : at + 8] for at in order], axis=0).astype(bf16)


def chain(raw, *others):
    width = raw.shape[1]
    out = jax.ShapeDtypeStruct((width, width), jnp.bfloat16)
    return local_call(chain_kernel, "block_chain", out, [WHOLE] * 6)(raw, *others)


def finish_kernel(slot_block, home, gram_l, gram_r, first, second, *outs):
    gram_l_new, gram_r_new, first_new, second_new, direction = outs
    core = lax.axis_index("fsdp")
    n, col = iota((32, 64), 0), iota((32, 64), 1)
    kind, chip, row = n >> 3, col >> 3, col & 7
    other = row - 4 * (1 - core)
    product = (chip == (n & 7)) & ((other == kind) | ((kind == 2) & (other == 3)))
    hit = ((kind == 3) & (row - 4 * core == (n & 7))) | ((kind < 3) & product)
    take = one_hot(hit)
    for b in range(home.shape[0]):
        direction[b] = dot(take[24:], home[b])[:4].astype(jnp.bfloat16)
    share = jnp.where(slot_block[core, 0] >= 0, 1.0, 0.0)
    for slot in range(home.shape[0]):
        block = jnp.maximum(slot_block[core, slot], 0)
        rows = dot(take, home[block]) * share
        rotated = rows[16:24]
        gram_l_new[slot] = shampoo_beta * gram_l[slot] + (1.0 - shampoo_beta) * rows[:8]
        gram_r_new[slot] = shampoo_beta * gram_r[slot] + (1.0 - shampoo_beta) * rows[8:16]
        first_new[slot] = adam_first * first[slot] + (1.0 - adam_first) * rotated
        second_new[slot] = (
            adam_second * second[slot] + (1.0 - adam_second) * rotated * rotated
        )


def finish(slot_block, home, states):
    blocks, width = home.shape[0], home.shape[2]
    outs = [jax.ShapeDtypeStruct(x.shape, x.dtype) for x in states]
    outs.append(jax.ShapeDtypeStruct((blocks, 4, width), jnp.bfloat16))
    return local_call(finish_kernel, "new_state", outs, [SCALARS] + [WHOLE] * 5)(
        slot_block, home, *states
    )


def on_core(zero, one):
    core = lax.axis_index("fsdp")
    pl.when(core == 0)(zero)
    pl.when(core != 0)(one)


def half_rows(left_t, right, moment):
    upper = moment.astype(jnp.bfloat16).astype(jnp.float32)
    rows = [right.astype(jnp.float32), left_t.astype(jnp.float32), upper, moment - upper]
    return jnp.concatenate(rows, axis=0)


def give_kernel(left_t, right, first, second, out, left_here, right_here, moment, done):
    copies = [
        pltpu.make_async_copy(left_t, left_here, done.at[0]),
        pltpu.make_async_copy(right, right_here, done.at[1]),
    ]
    first_copy = pltpu.make_async_copy(first, moment, done.at[2])
    second_copy = pltpu.make_async_copy(second, moment, done.at[2])
    on_core(second_copy.start, first_copy.start)
    for copy in copies:
        copy.start()
    for copy in copies:
        copy.wait()
    on_core(second_copy.wait, first_copy.wait)
    for slot in range(out.shape[0]):
        rows = half_rows(left_here[slot], right_here[slot], moment[slot])
        out[slot] = rows.astype(jnp.bfloat16)


def give_half(*states):
    blocks, rows, width = states[0].shape
    return local_call(
        give_kernel,
        "state_half",
        jax.ShapeDtypeStruct((blocks, 4 * rows, width), jnp.bfloat16),
        [FAR] * 4,
        [pltpu.VMEM(x.shape, x.dtype) for x in states[:3]] + [pltpu.SemaphoreType.DMA((3,))],
        vmem=60,
    )(*states)


def pack_kernel(slot_block, terms, given, left_t, right, first, second, out, *scratch):
    built, brought, left_here, right_here, moment, done, sent = scratch
    core = lax.axis_index("fsdp")
    blocks, span = terms.shape[0], terms.shape[2]
    units = pl.ds(0, span)
    fetch = [
        pltpu.make_async_copy(given, brought, done.at[blocks]),
        pltpu.make_async_copy(left_t, left_here, done.at[blocks + 1]),
        pltpu.make_async_copy(right, right_here, done.at[blocks + 2]),
    ]
    first_copy = pltpu.make_async_copy(first, moment, done.at[blocks + 3])
    second_copy = pltpu.make_async_copy(second, moment, done.at[blocks + 3])
    for copy in fetch:
        copy.start()
    on_core(first_copy.start, second_copy.start)
    near = [
        pltpu.make_async_copy(terms.at[b], built.at[b, :, units], done.at[b])
        for b in range(blocks)
    ]
    cross = [
        pltpu.make_async_copy(terms.at[b], built.at[:, b, units], done.at[b])
        for b in range(blocks)
    ]
    near_out = [pltpu.make_async_copy(built.at[b], out.at[b], sent.at[b]) for b in range(blocks)]
    cross_out = [
        pltpu.make_async_copy(built.at[:, b], out.at[:, b], sent.at[b]) for b in range(blocks)
    ]
    for b in range(blocks):
        on_core(near[b].start, cross[b].start)

    mine = slot_block[core, 0] >= 0
    n, col = iota((32, 32), 0), iota((32, 32), 1)
    turn = one_hot(col == (((n & 3) + 1) & 3) * 8 + (n >> 2))
    for copy in fetch:
        copy.wait()
    on_core(first_copy.wait, second_copy.wait)
    for b in range(blocks):
        at = 0
        for owner in range(slot_block.shape[0]):
            for slot in range(blocks):
                at += jnp.where(slot_block[owner, slot] == b, slot, 0)
        rows = half_rows(left_here[at], right_here[at], moment[at])
        rows = jnp.where(mine, rows, brought[at].astype(jnp.float32))
        half = jnp.where(core == 0, rows[:4], rows[4:8]).astype(jnp.bfloat16)
        singles = dot(turn, rows.astype(jnp.bfloat16)).astype(jnp.bfloat16)
        for g in EIGHT:
            to, then = jnp.where(core == 0, b, g), jnp.where(core == 0, g, b)
            built[to, then, span] = half
            built[to, then, span + 1] = singles[4 * g : 4 * g + 4]
        on_core(near[b].wait, cross[b].wait)
        on_core(near_out[b].start, cross_out[b].start)
    for b in range(blocks):
        on_core(near_out[b].wait, cross_out[b].wait)


def pack(slot_block, terms, given, *states):
    blocks, chips, span, rows, width = terms.shape
    out = jax.ShapeDtypeStruct((blocks, chips, span + 2, rows, width), terms.dtype)
    held = [pltpu.VMEM(x.shape, x.dtype) for x in (out, given, *states[:3])]
    return local_call(
        pack_kernel,
        "pack_messages",
        out,
        [SCALARS] + [FAR] * 6,
        held + [pltpu.SemaphoreType.DMA((blocks + 4,)), pltpu.SemaphoreType.DMA((blocks,))],
        vmem=60,
        out=FAR,
    )(slot_block, terms, given, *states)


def total_of(received, *at):
    return jnp.sum(received[(slice(None), *at)].astype(jnp.float32), axis=0)


def relay_kernel(received, out):
    span = received.shape[2] - 2
    for then in EIGHT:
        for unit in range(span):
            out[then, unit] = total_of(received, then, unit).astype(jnp.bfloat16)
        for source in EIGHT:
            at = span + 2 * source
            out[then, at] = received[source, then, span]
            out[then, at + 1] = received[source, then, span + 1]


def relay(received):
    span = received.shape[2] - 2
    shape = (GROUP, span + 2 * GROUP) + received.shape[3:]
    out = jax.ShapeDtypeStruct(shape, received.dtype)
    return local_call(relay_kernel, "relay", out, [WHOLE])(received)


def sum_kernel(received, copies, state):
    core = lax.axis_index("fsdp")
    span = received.shape[1] - 2 * GROUP
    total = jnp.concatenate([total_of(received, unit) for unit in range(span)], axis=0)
    total = total.astype(jnp.bfloat16)
    for peer in range(copies.shape[0]):
        copies[peer] = total
    for later in EIGHT:
        for early in EIGHT:
            one, two = PLACE[early, later], PLACE[later, early]
            to = jnp.where(core == 0, one, two)
            at = span + 2 * early
            state[to, 0] = received[later, at]
            state[to, 1] = received[later, at + 1]


def sum_terms(received):
    rows, width = received.shape[2:]
    span = received.shape[1] - 2 * GROUP
    outs = [
        jax.ShapeDtypeStruct((GROUP, span * rows, width), received.dtype),
        jax.ShapeDtypeStruct((GROUP * GROUP, 2, rows, width), received.dtype),
    ]
    return local_call(sum_kernel, "sum_terms", outs, [WHOLE])(received)


def shards(
    grad_parts,
    slot_block,
    gram_left,
    gram_right,
    left_basis_t,
    right_basis,
    moment_first,
    moment_second,
):
    blocks = grad_parts.shape[1]
    q_total = grad_parts.shape[2]
    half_span = grad_parts.shape[3]
    width = grad_parts.shape[4]
    core = lax.axis_index("fsdp")

    states = (left_basis_t, right_basis, moment_first, moment_second)
    terms = grad_parts[0].reshape(blocks, GROUP, q_total // GROUP, half_span, width)
    message = pack(slot_block, terms, swap_cores(give_half(*states)), *states)
    received = exchange(relay(exchange(message, FIRST)), SECOND)
    raw, half = sum_terms(received)
    raw = exchange(raw, BLOCK).reshape(-1, width)

    given = swap_cores(half)
    low = jnp.where(core == 0, half, given)
    high = jnp.where(core == 0, given, half)
    right = jnp.concatenate([low[:, 0], high[:, 0]], axis=1).reshape(width, width)
    left_t = low[:, 1, 0]
    first = low[:, 1, 1].astype(jnp.float32) + low[:, 1, 2].astype(jnp.float32)
    second = high[:, 1, 1].astype(jnp.float32) + high[:, 1, 2].astype(jnp.float32)

    home = chain(raw, swap_cores(raw), right, left_t, first, second)
    home = exchange(home.reshape(blocks * GROUP, 8, width), ALL)

    outs = finish(
        slot_block,
        home.reshape(blocks, GROUP * 8, width),
        (gram_left, gram_right, moment_first, moment_second),
    )
    return (*outs[:4], outs[4][:, None])


def solution(mesh):
    state = P("fsdp", "dp", None)
    return jax.shard_map(
        shards,
        mesh=mesh,
        in_specs=(P("dp", None, None, "fsdp", None), P()) + (state,) * 6,
        out_specs=(state,) * 4 + (P(None, "dp", "fsdp", None),),
        check_vma=False,
    )
```

time: 924 us -> 91.3 us (0.10)
  waiting for transfers between devices: 860 us -> 11.6 us
  blocking collectives: 7.58 us -> 62.4 us
  matrix products: 18.7 us -> 0 us
  local copies, waits for them, and re-layouts: 14.6 us -> 1.24 us
  between operations: 13.9 us -> 0.79 us
  Pallas kernels: 0 us -> 11 us
    reduce_scatter x2 -> x0, waiting for transfers between devices: 719 us -> none  [the longest x1 360 us: shards(): lax.psum_scatter(jnp.einsum('cri,crj->icj', left_basis_t, back_right, pre...]
    all_gather x2 -> x0, waiting for transfers between devices: 140 us -> none  [the longest x1 75.1 us: shards(): full_grad = lax.all_gather(local_grad, 'dp', axis=1, tiled=True)]
    all_to_all x2 -> x3, blocking collectives: 7.58 us -> 62.4 us  [exchange(): return lax.all_to_all(x, AXES, 0, 0, axis_index_groups=groups, tiled=True)]
    dot_general x4 -> x0, matrix products: 18.7 us -> none  [the longest x1 7.83 us: shards(): jnp.einsum('cri,crj->icj', left_basis_t, back_right, preferred_element_ty...]
    pallas_call x0 -> x6, Pallas kernels: none -> 11 us  [the longest x1 3.86 us: pack(): local_call(pack_kernel, 'pack_messages', out, [SCALARS] + [FAR] * 6, held...]
    transpose x3 -> x0, local copies, waits for them, and re-layouts: 10.6 us -> none  [the longest x1 10.5 us: shards(): jnp.einsum('cri,crj->icj', left_basis_t, back_right, preferred_element_ty...]
  transfers between devices with their start and end apart: 4 -> 4, of which waited for: 4 -> 3; matrix products, arithmetic and copies ran while one was open for 1% -> 1% of each run, Pallas kernels for 0% -> 0%
where the time goes in v1:
time: 91.3 us; the launch traced here: 90.8 us
  blocking collectives  62.4 us (68%)
  waiting for transfers between devices  11.6 us (13%)
  Pallas kernels  11 us (12%)
  starting transfers between devices  3.59 us (4%)
  local copies, waits for them, and re-layouts  1.24 us (1%)
    all_to_all x3, blocking collectives, exchange(): return lax.all_to_all(x, AXES, 0, 0, axis_index_groups=groups, tiled=True)  62.4 us
    all_to_all x1, waiting for transfers between devices, exchange(): return lax.all_to_all(x, AXES, 0, 0, axis_index_groups=groups, tiled=True)  9.03 us
    pallas_call x1, Pallas kernels, pack(): local_call(pack_kernel, 'pack_messages', out, [SCALARS] + [FAR] * 6, held...  3.86 us
    all_to_all x1, starting transfers between devices, exchange(): return lax.all_to_all(x, AXES, 0, 0, axis_index_groups=groups, tiled=True)  3.42 us
    ppermute x3, waiting for transfers between devices, swap_cores(): return lax.ppermute(x, 'fsdp', [(0, 1), (1, 0)])  2.56 us
    pallas_call x1, Pallas kernels, chain(): local_call(chain_kernel, 'block_chain', out, [WHOLE] * 6)(raw, *others)  2.15 us
  transfers between devices with their start and end apart: 4, of which 3 were waited for; matrix products, arithmetic and copies ran while one was open for 1% of the time, Pallas kernels for 0%

profile of v1, /device:TPU:0, one launch (start us, length us, event | category | flops | bytes accessed | tf_op | source)
XLA Modules:
  0.0 90.8 jit_solution(5672446884186354831)
XLA Ops:
  0.6 1.7 %state_half.1 = bf16[8,32,512]{2,1,0:T(8,128)(2,1)} custom-call(bf16[8,8,512]{2,1,0:T(8,128)(2,1)} %left_t.3, bf16[8,8,512]{2,1,0:T(8,128)(2,1)} %right.3, f32[8,8,512]{2,1,0:T(8,128)} %first.5, f32[8,8,512]{2,1,0:T(8,128)} %second.5), custom_call_target="tpu_custom_call" | custom-call | tf_op jit(solution)/shard_map/state_half/pallas_call | solution.py:192
  2.3 0.1 collective-permute-start
  2.4 1.7 %collective-permute-done.given = bf16[8,32,512]{2,1,0:T(8,128)(2,1)S(1)} collective-permute-done((bf16[8,32,512]{2,1,0:T(8,128)(2,1)}, bf16[8,32,512]{2,1,0:T(8,128)(2,1)S(1)}, u32[]{:S(2)}, u32[]{:S(2)}) %collective-permute-start) | collective-permute-done | bytes 262176 | tf_op jit(solution)/shard_map/ppermute | solution.py:48
  4.2 0.0 copy-start.5
  4.2 0.7 copy-done.5
  4.9 3.9 %pack_messages.1 = bf16[8,8,10,4,512]{4,3,2,1,0:T(4,128)(2,1)} custom-call(s32[2,8]{1,0:T(2,128)} %slot_block.3, bf16[8,8,8,4,512]{4,3,2,1,0:T(4,128)(2,1)} %bitcast.25, bf16[8,32,512]{2,1,0:T(8,128)(2,1)} %copy-done.5, bf16[8,8,512]{2,1,0:T(8,128)(2,1)} %left_t.3, bf16[8,8,512]{2,1,0:T(8,128)(2,1)} %right.3, f32[8,8,512]{2,1,0:T(8,128)} %first.5, ...), custom_call_target="tpu_custom_call" | custom-call | tf_op jit(solution)/shard_map/pack_messages/pallas_call | solution.py:261
  8.7 30.8 %all_to_all.20.received = bf16[8,8,10,4,512]{4,3,2,1,0:T(4,128)(2,1)S(1)} all-to-all(bf16[8,8,10,4,512]{4,3,2,1,0:T(4,128)(2,1)} %pack_messages.1), channel_id=1, replica_groups={{0,1,12,13,48,49,60,61},{3,2,15,14,51,50,63,62},{4,5,8,9,52,53,56,57},{..., dimensions={0} | all-to-all | bytes 5242880 | tf_op jit(solution)/shard_map/all_to_all | solution.py:44
  39.6 0.8 relay.1
  40.4 14.2 %all_to_all.21.received = bf16[8,24,4,512]{3,2,1,0:T(4,128)(2,1)S(1)} all-to-all(bf16[8,24,4,512]{3,2,1,0:T(4,128)(2,1)S(1)} %relay.1), channel_id=1, replica_groups={{0,3,4,7,16,19,20,23},{1,2,5,6,17,18,21,22},{12,15,8,11,28,31,24,27},{1..., dimensions={0} | all-to-all | bytes 1572864 | tf_op jit(solution)/shard_map/all_to_all | solution.py:44
  54.5 0.8 sum_terms.1
  55.4 0.2 copy.18
  55.5 0.1 collective-permute-start.2
  55.6 3.4 %all-to-all-start.2 = ((bf16[8,32,512]{2,1,0:T(8,128)(2,1)}), bf16[8,32,512]{2,1,0:T(8,128)(2,1)S(1)}, u32[]{:S(2)}, u32[]{:S(2)}) async-start(bf16[8,32,512]{2,1,0:T(8,128)(2,1)} %get-tuple-element.12), calls=%async_computation.2 | async-start | bytes 524288 | tf_op jit(solution)/shard_map/all_to_all | solution.py:44
  59.1 9.0 %all-to-all-done.2 = bf16[8,32,512]{2,1,0:T(8,128)(2,1)S(1)} async-done(((bf16[8,32,512]{2,1,0:T(8,128)(2,1)}), bf16[8,32,512]{2,1,0:T(8,128)(2,1)S(1)}, u32[]{:S(2)}, u32[]{:S(2)}) %all-to-all-start.2) | async-done | bytes 262176 | tf_op jit(solution)/shard_map/all_to_all | solution.py:44
  68.1 0.0 collective-permute-start.1
  68.1 0.0 collective-permute-done.2
  68.1 0.2 broadcast_select_fusion.1
  68.3 0.0 copy-start
  68.3 0.0 copy-start.1
  68.4 0.0 copy-start.2
  68.4 0.0 copy-start.3
  68.4 0.0 copy-start.4
  68.5 0.3 copy.25
  68.8 0.8 collective-permute-done.1.swapped
  69.6 2.1 %block_chain.1 = bf16[512,512]{1,0:T(8,128)(2,1)S(1)} custom-call(bf16[256,512]{1,0:T(8,128)(2,1)S(1)} %bitcast.24, bf16[256,512]{1,0:T(8,128)(2,1)S(1)} %collective-permute-done.1.swapped, bf16[512,512]{1,0:T(8,128)(2,1)S(1)} %bitcast.21, bf16[64,512]{1,0:T(8,128)(2,1)S(1)} %slice_bitcast_fusion.2.left_t, f32[64,512]{1,0:T(8,128)S(1)} %get-tuple-element.34.first, ...), custom_call_target="tpu_custom_call" | custom-call | tf_op jit(solution)/shard_map/block_chain/pallas_call | solution.py:124
  71.8 17.4 %all_to_all.22 = bf16[64,8,512]{2,1,0:T(8,128)(2,1)S(1)} all-to-all(bf16[64,8,512]{2,1,0:T(8,128)(2,1)S(1)} %bitcast.22), channel_id=1, replica_groups={{0,3,4,7,16,19,20,23,1,2,5,6,17,18,21,22,12,15,8,11,28,31,24,27,13,14,9..., dimensions={0} | all-to-all | bytes 1048576 | tf_op jit(solution)/shard_map/all_to_all | solution.py:44
  89.2 0.0 copy-done
  89.2 0.0 copy-done.1
  89.2 0.0 copy-done.2
  89.2 0.0 copy-done.3
  89.2 0.0 copy-done.4
  89.2 1.6 %new_state.1 = (f32[8,8,512]{2,1,0:T(8,128)}, f32[8,8,512]{2,1,0:T(8,128)}, f32[8,8,512]{2,1,0:T(8,128)}, f32[8,8,512]{2,1,0:T(8,128)}, bf16[8,4,512]{2,1,0:T(4,128)(2,1)}) custom-call(s32[2,8]{1,0:T(2,128)S(1)} %copy-done.4, bf16[8,64,512]{2,1,0:T(8,128)(2,1)S(1)} %bitcast.20, f32[8,8,512]{2,1,0:T(8,128)S(1)} %copy-done.2, f32[8,8,512]{2,1,0:T(8,128)S(1)} %copy-done.3, ...), custom_call_target="tpu_custom_call" | custom-call | tf_op jit(solution)/shard_map/new_state/pallas_call | solution.py:155
  (4 shorter events, 0.1 us)
Async XLA Ops:
  2.3 1.8 %collective-permute-start = (bf16[8,32,512]{2,1,0:T(8,128)(2,1)}, bf16[8,32,512]{2,1,0:T(8,128)(2,1)S(1)}, u32[]{:S(2)}, u32[]{:S(2)}) collective-permute-start(bf16[8,32,512]{2,1,0:T(8,128)(2,1)} %state_half.1), channel_id=1, source_target_pairs={{0,64},{64,0},{1,65},{65,1},{2,66},{66,2},{3,67},{67,3},{4,68},{68... | collective-permute-start | bytes 786440 | tf_op jit(solution)/shard_map/ppermute | solution.py:48
  4.2 0.7 copy-start.5
  55.5 12.6 %collective-permute-start.2 = (bf16[64,2,4,512]{3,0,2,1:T(8,128)(2,1)S(1)}, bf16[64,2,4,512]{3,0,2,1:T(8,128)(2,1)S(1)}, u32[]{:S(2)}, u32[]{:S(2)}) collective-permute-start(bf16[64,2,4,512]{3,0,2,1:T(8,128)(2,1)S(1)} %copy.18), channel_id=1, source_target_pairs={{0,64},{64,0},{1,65},{65,1},{2,66},{66,2},{3,67},{67,3},{4,68},{68... | collective-permute-start | bytes 1572872 | tf_op jit(solution)/shard_map/ppermute | solution.py:48
  55.6 12.5 %all-to-all-start.2 = ((bf16[8,32,512]{2,1,0:T(8,128)(2,1)}), bf16[8,32,512]{2,1,0:T(8,128)(2,1)S(1)}, u32[]{:S(2)}, u32[]{:S(2)}) async-start(bf16[8,32,512]{2,1,0:T(8,128)(2,1)} %get-tuple-element.12), calls=%async_computation.2 | async-start | bytes 524288 | tf_op jit(solution)/shard_map/all_to_all | solution.py:44
  68.1 1.5 %collective-permute-start.1 = (bf16[256,512]{1,0:T(8,128)(2,1)S(1)}, bf16[256,512]{1,0:T(8,128)(2,1)S(1)}, u32[]{:S(2)}, u32[]{:S(2)}) collective-permute-start(bf16[256,512]{1,0:T(8,128)(2,1)S(1)} %bitcast.23), channel_id=1, source_target_pairs={{0,64},{64,0},{1,65},{65,1},{2,66},{66,2},{3,67},{67,3},{4,68},{68... | collective-permute-start | bytes 786440 | tf_op jit(solution)/shard_map/ppermute | solution.py:48
  68.3 20.9 %copy-start = (f32[8,8,512]{2,1,0:T(8,128)S(1)}, f32[8,8,512]{2,1,0:T(8,128)}, u32[]{:S(2)}) copy-start(f32[8,8,512]{2,1,0:T(8,128)} %first.5) | copy-start | bytes 393220
  68.3 20.8 %copy-start.1 = (f32[8,8,512]{2,1,0:T(8,128)S(1)}, f32[8,8,512]{2,1,0:T(8,128)}, u32[]{:S(2)}) copy-start(f32[8,8,512]{2,1,0:T(8,128)} %second.5) | copy-start | bytes 393220
  68.4 20.8 %copy-start.2 = (f32[8,8,512]{2,1,0:T(8,128)S(1)}, f32[8,8,512]{2,1,0:T(8,128)}, u32[]{:S(2)}) copy-start(f32[8,8,512]{2,1,0:T(8,128)} %gram_l.1) | copy-start | bytes 393220
  68.4 20.8 %copy-start.3 = (f32[8,8,512]{2,1,0:T(8,128)S(1)}, f32[8,8,512]{2,1,0:T(8,128)}, u32[]{:S(2)}) copy-start(f32[8,8,512]{2,1,0:T(8,128)} %gram_r.1) | copy-start | bytes 393220
  68.4 20.8 %copy-start.4 = (s32[2,8]{1,0:T(2,128)S(1)}, s32[2,8]{1,0:T(2,128)}, u32[]{:S(2)}) copy-start(s32[2,8]{1,0:T(2,128)} %slot_block.3) | copy-start | bytes 196

commit v2 on v1

--- a/solution.py
+++ b/solution.py
@@ -65,15 +65,20 @@
 FAR = pl.BlockSpec(memory_space=pltpu.HBM)
 
 
-def local_call(kernel, name, out_shape, in_specs, scratch=(), vmem=40, out=WHOLE):
+def in_hbm(x):
+    return pltpu.with_memory_space_constraint(x, pltpu.HBM)
+
+
+def local_call(kernel, name, out_shape, in_specs, scratch=(), **options):
     return pl.pallas_call(
         kernel,
         out_shape=out_shape,
         in_specs=in_specs,
-        out_specs=jax.tree.map(lambda _: out, out_shape),
+        out_specs=jax.tree.map(lambda _: WHOLE, out_shape),
         scratch_shapes=list(scratch),
-        compiler_params=pltpu.CompilerParams(vmem_limit_bytes=vmem * 2**20),
+        compiler_params=pltpu.CompilerParams(vmem_limit_bytes=40 * 2**20),
         name=name,
+        **options,
     )
 
 
@@ -195,40 +200,48 @@
         jax.ShapeDtypeStruct((blocks, 4 * rows, width), jnp.bfloat16),
         [FAR] * 4,
         [pltpu.VMEM(x.shape, x.dtype) for x in states[:3]] + [pltpu.SemaphoreType.DMA((3,))],
-        vmem=60,
     )(*states)
 
 
-def pack_kernel(slot_block, terms, given, left_t, right, first, second, out, *scratch):
-    built, brought, left_here, right_here, moment, done, sent = scratch
-    core = lax.axis_index("fsdp")
-    blocks, span = terms.shape[0], terms.shape[2]
-    units = pl.ds(0, span)
+def load_kernel(terms, out, done):
+    blocks, units = terms.shape[0], pl.ds(0, terms.shape[2])
+    near = [
+        pltpu.make_async_copy(terms.at[b], out.at[b, :, units], done.at[b]) for b in range(blocks)
+    ]
+    cross = [
+        pltpu.make_async_copy(terms.at[b], out.at[:, b, units], done.at[b]) for b in range(blocks)
+    ]
+    for b in range(blocks):
+        on_core(near[b].start, cross[b].start)
+    for b in range(blocks):
+        on_core(near[b].wait, cross[b].wait)
+
+
+def load(terms):
+    blocks, chips, span, rows, width = terms.shape
+    return local_call(
+        load_kernel,
+        "load_terms",
+        jax.ShapeDtypeStruct((blocks, chips, span + 2, rows, width), terms.dtype),
+        [FAR],
+        [pltpu.SemaphoreType.DMA((blocks,))],
+        cost_estimate=pl.CostEstimate(flops=0, bytes_accessed=2 * terms.nbytes, transcendentals=0),
+    )(terms)
+
+
+def pack_kernel(slot_block, loaded, given, left_t, right, first, second, out, *scratch):
+    left_here, right_here, moment, done = scratch
+    core = lax.axis_index("fsdp")
+    blocks, span = out.shape[0], out.shape[2] - 2
     fetch = [
-        pltpu.make_async_copy(given, brought, done.at[blocks]),
-        pltpu.make_async_copy(left_t, left_here, done.at[blocks + 1]),
-        pltpu.make_async_copy(right, right_here, done.at[blocks + 2]),
-    ]
-    first_copy = pltpu.make_async_copy(first, moment, done.at[blocks + 3])
-    second_copy = pltpu.make_async_copy(second, moment, done.at[blocks + 3])
+        pltpu.make_async_copy(left_t, left_here, done.at[0]),
+        pltpu.make_async_copy(right, right_here, done.at[1]),
+    ]
+    first_copy = pltpu.make_async_copy(first, moment, done.at[2])
+    second_copy = pltpu.make_async_copy(second, moment, done.at[2])
     for copy in fetch:
         copy.start()
     on_core(first_copy.start, second_copy.start)
-    near = [
-        pltpu.make_async_copy(terms.at[b], built.at[b, :, units], done.at[b])
-        for b in range(blocks)
-    ]
-    cross = [
-        pltpu.make_async_copy(terms.at[b], built.at[:, b, units], done.at[b])
-        for b in range(blocks)
-    ]
-    near_out = [pltpu.make_async_copy(built.at[b], out.at[b], sent.at[b]) for b in range(blocks)]
-    cross_out = [
-        pltpu.make_async_copy(built.at[:, b], out.at[:, b], sent.at[b]) for b in range(blocks)
-    ]
-    for b in range(blocks):
-        on_core(near[b].start, cross[b].start)
-
     mine = slot_block[core, 0] >= 0
     n, col = iota((32, 32), 0), iota((32, 32), 1)
     turn = one_hot(col == (((n & 3) + 1) & 3) * 8 + (n >> 2))
@@ -241,32 +254,24 @@
             for slot in range(blocks):
                 at += jnp.where(slot_block[owner, slot] == b, slot, 0)
         rows = half_rows(left_here[at], right_here[at], moment[at])
-        rows = jnp.where(mine, rows, brought[at].astype(jnp.float32))
+        rows = jnp.where(mine, rows, given[at].astype(jnp.float32))
         half = jnp.where(core == 0, rows[:4], rows[4:8]).astype(jnp.bfloat16)
         singles = dot(turn, rows.astype(jnp.bfloat16)).astype(jnp.bfloat16)
         for g in EIGHT:
             to, then = jnp.where(core == 0, b, g), jnp.where(core == 0, g, b)
-            built[to, then, span] = half
-            built[to, then, span + 1] = singles[4 * g : 4 * g + 4]
-        on_core(near[b].wait, cross[b].wait)
-        on_core(near_out[b].start, cross_out[b].start)
-    for b in range(blocks):
-        on_core(near_out[b].wait, cross_out[b].wait)
-
-
-def pack(slot_block, terms, given, *states):
-    blocks, chips, span, rows, width = terms.shape
-    out = jax.ShapeDtypeStruct((blocks, chips, span + 2, rows, width), terms.dtype)
-    held = [pltpu.VMEM(x.shape, x.dtype) for x in (out, given, *states[:3])]
+            out[to, then, span] = half
+            out[to, then, span + 1] = singles[4 * g : 4 * g + 4]
+
+
+def pack(slot_block, loaded, given, *states):
     return local_call(
         pack_kernel,
-        "pack_messages",
-        out,
-        [SCALARS] + [FAR] * 6,
-        held + [pltpu.SemaphoreType.DMA((blocks + 4,)), pltpu.SemaphoreType.DMA((blocks,))],
-        vmem=60,
-        out=FAR,
-    )(slot_block, terms, given, *states)
+        "pack_states",
+        jax.ShapeDtypeStruct(loaded.shape, loaded.dtype),
+        [SCALARS, WHOLE, WHOLE] + [FAR] * 4,
+        [pltpu.VMEM(x.shape, x.dtype) for x in states[:3]] + [pltpu.SemaphoreType.DMA((3,))],
+        input_output_aliases={1: 0},
+    )(slot_block, loaded, given, *states)
 
 
 def total_of(received, *at):
@@ -334,8 +339,10 @@
     core = lax.axis_index("fsdp")
 
     states = (left_basis_t, right_basis, moment_first, moment_second)
+    states = tuple(in_hbm(part) for part in states)
     terms = grad_parts[0].reshape(blocks, GROUP, q_total // GROUP, half_span, width)
-    message = pack(slot_block, terms, swap_cores(give_half(*states)), *states)
+    terms = in_hbm(terms)
+    message = pack(in_hbm(slot_block), load(terms), swap_cores(give_half(*states)), *states)
     received = exchange(relay(exchange(message, FIRST)), SECOND)
     raw, half = sum_terms(received)
     raw = exchange(raw, BLOCK).reshape(-1, width)

time: 91.3 us -> 87.6 us (0.959)
  waiting for transfers between devices: 11.6 us -> 9.86 us
  Pallas kernels: 11 us -> 9.96 us
    ppermute x3, waiting for transfers between devices: 2.56 us -> 0.83 us  [swap_cores(): return lax.ppermute(x, 'fsdp', [(0, 1), (1, 0)])]
    pallas_call x1 -> x2, Pallas kernels: 3.86 us -> 3.55 us  [the longest x1 1.97 us: pack(): local_call(pack_kernel, 'pack_states', jax.ShapeDtypeStruct(loaded.shape,...]
  transfers between devices with their start and end apart: 4 -> 4, of which waited for: 3 -> 2; matrix products, arithmetic and copies ran while one was open for 1% -> 1% of each run, Pallas kernels for 0% -> 2%
where the time goes in v2:
time: 87.6 us; the launch traced here: 87.2 us
  blocking collectives  62.2 us (71%)
  Pallas kernels  9.96 us (11%)
  waiting for transfers between devices  9.86 us (11%)
  starting transfers between devices  3.6 us (4%)
    all_to_all x3, blocking collectives, exchange(): return lax.all_to_all(x, AXES, 0, 0, axis_index_groups=groups, tiled=True)  62.2 us
    all_to_all x1, waiting for transfers between devices, exchange(): return lax.all_to_all(x, AXES, 0, 0, axis_index_groups=groups, tiled=True)  9.03 us
    all_to_all x1, starting transfers between devices, exchange(): return lax.all_to_all(x, AXES, 0, 0, axis_index_groups=groups, tiled=True)  3.42 us
    pallas_call x1, Pallas kernels, chain(): local_call(chain_kernel, 'block_chain', out, [WHOLE] * 6)(raw, *others)  2.14 us
    pallas_call x1, Pallas kernels, pack(): local_call(pack_kernel, 'pack_states', jax.ShapeDtypeStruct(loaded.shape,...  1.97 us
  transfers between devices with their start and end apart: 4, of which 2 were waited for; matrix products, arithmetic and copies ran while one was open for 1% of the time, Pallas kernels for 2%

profile of v2, /device:TPU:0, one launch (start us, length us, event | category | flops | bytes accessed | tf_op | source)
XLA Modules:
  0.0 87.2 jit_solution(14393173935598598039)
XLA Ops:
  0.6 1.0 %state_half.1 = bf16[8,32,512]{2,1,0:T(8,128)(2,1)S(1)} custom-call(bf16[8,8,512]{2,1,0:T(8,128)(2,1)} %left_t.3, bf16[8,8,512]{2,1,0:T(8,128)(2,1)} %right.3, f32[8,8,512]{2,1,0:T(8,128)} %first.5, f32[8,8,512]{2,1,0:T(8,128)} %second.5), custom_call_target="tpu_custom_call" | custom-call | tf_op jit(solution)/shard_map/state_half/pallas_call | solution.py:197
  1.6 0.1 collective-permute-start
  1.7 1.6 %load_terms.1.loaded = bf16[8,8,10,4,512]{4,3,2,1,0:T(4,128)(2,1)S(1)} custom-call(bf16[8,8,8,4,512]{4,3,2,1,0:T(4,128)(2,1)} %bitcast.25), custom_call_target="tpu_custom_call" | custom-call | bytes 4194304 | tf_op jit(solution)/shard_map/load_terms/pallas_call | solution.py:222
  3.3 0.0 collective-permute-done.given
  3.3 2.0 %pack_states.1 = bf16[8,8,10,4,512]{4,3,2,1,0:T(4,128)(2,1)S(1)} custom-call(s32[2,8]{1,0:T(2,128)} %slot_block.3, bf16[8,8,10,4,512]{4,3,2,1,0:T(4,128)(2,1)S(1)} %load_terms.1.loaded, bf16[8,32,512]{2,1,0:T(8,128)(2,1)S(1)} %collective-permute-done.given, bf16[8,8,512]{2,1,0:T(8,128)(2,1)} %left_t.3, ...), custom_call_target="tpu_custom_call", output_to_operand_aliasing={{}: (1, {})} | custom-call | tf_op jit(solution)/shard_map/pack_states/pallas_call | solution.py:267
  5.3 30.6 %all_to_all.20.received = bf16[8,8,10,4,512]{4,3,2,1,0:T(4,128)(2,1)S(1)} all-to-all(bf16[8,8,10,4,512]{4,3,2,1,0:T(4,128)(2,1)S(1)} %pack_states.1), channel_id=1, replica_groups={{0,1,12,13,48,49,60,61},{3,2,15,14,51,50,63,62},{4,5,8,9,52,53,56,57},{..., dimensions={0} | all-to-all | bytes 5242880 | tf_op jit(solution)/shard_map/all_to_all | solution.py:44
  35.9 0.8 relay.1
  36.7 14.2 %all_to_all.21.received = bf16[8,24,4,512]{3,2,1,0:T(4,128)(2,1)S(1)} all-to-all(bf16[8,24,4,512]{3,2,1,0:T(4,128)(2,1)S(1)} %relay.1), channel_id=1, replica_groups={{0,3,4,7,16,19,20,23},{1,2,5,6,17,18,21,22},{12,15,8,11,28,31,24,27},{1..., dimensions={0} | all-to-all | bytes 1572864 | tf_op jit(solution)/shard_map/all_to_all | solution.py:44
  50.9 0.8 sum_terms.1
  51.7 0.2 copy.19
  51.9 0.1 collective-permute-start.2
  52.0 3.4 %all-to-all-start.2 = ((bf16[8,32,512]{2,1,0:T(8,128)(2,1)}), bf16[8,32,512]{2,1,0:T(8,128)(2,1)S(1)}, u32[]{:S(2)}, u32[]{:S(2)}) async-start(bf16[8,32,512]{2,1,0:T(8,128)(2,1)} %get-tuple-element.12), calls=%async_computation.2 | async-start | bytes 524288 | tf_op jit(solution)/shard_map/all_to_all | solution.py:44
  55.4 9.0 %all-to-all-done.2 = bf16[8,32,512]{2,1,0:T(8,128)(2,1)S(1)} async-done(((bf16[8,32,512]{2,1,0:T(8,128)(2,1)}), bf16[8,32,512]{2,1,0:T(8,128)(2,1)S(1)}, u32[]{:S(2)}, u32[]{:S(2)}) %all-to-all-start.2) | async-done | bytes 262176 | tf_op jit(solution)/shard_map/all_to_all | solution.py:44
  64.4 0.0 collective-permute-start.1
  64.4 0.0 collective-permute-done.2
  64.4 0.2 broadcast_select_fusion.1
  64.7 0.0 copy-start
  64.7 0.0 copy-start.1
  64.7 0.0 copy-start.2
  64.7 0.0 copy-start.3
  64.7 0.0 copy-start.4
  64.8 0.3 copy.26
  65.1 0.8 collective-permute-done.1.swapped
  66.0 2.1 %block_chain.1 = bf16[512,512]{1,0:T(8,128)(2,1)S(1)} custom-call(bf16[256,512]{1,0:T(8,128)(2,1)S(1)} %bitcast.24, bf16[256,512]{1,0:T(8,128)(2,1)S(1)} %collective-permute-done.1.swapped, bf16[512,512]{1,0:T(8,128)(2,1)S(1)} %bitcast.21, bf16[64,512]{1,0:T(8,128)(2,1)S(1)} %slice_bitcast_fusion.2.left_t, f32[64,512]{1,0:T(8,128)S(1)} %get-tuple-element.34.first, ...), custom_call_target="tpu_custom_call" | custom-call | tf_op jit(solution)/shard_map/block_chain/pallas_call | solution.py:129
  68.1 17.4 %all_to_all.22 = bf16[64,8,512]{2,1,0:T(8,128)(2,1)S(1)} all-to-all(bf16[64,8,512]{2,1,0:T(8,128)(2,1)S(1)} %bitcast.22), channel_id=1, replica_groups={{0,3,4,7,16,19,20,23,1,2,5,6,17,18,21,22,12,15,8,11,28,31,24,27,13,14,9..., dimensions={0} | all-to-all | bytes 1048576 | tf_op jit(solution)/shard_map/all_to_all | solution.py:44
  85.5 0.0 copy-done
  85.5 0.0 copy-done.1
  85.5 0.0 copy-done.2
  85.5 0.0 copy-done.3
  85.6 0.0 copy-done.4
  85.6 1.6 %new_state.1 = (f32[8,8,512]{2,1,0:T(8,128)}, f32[8,8,512]{2,1,0:T(8,128)}, f32[8,8,512]{2,1,0:T(8,128)}, f32[8,8,512]{2,1,0:T(8,128)}, bf16[8,4,512]{2,1,0:T(4,128)(2,1)}) custom-call(s32[2,8]{1,0:T(2,128)S(1)} %copy-done.4, bf16[8,64,512]{2,1,0:T(8,128)(2,1)S(1)} %bitcast.20, f32[8,8,512]{2,1,0:T(8,128)S(1)} %copy-done.2, f32[8,8,512]{2,1,0:T(8,128)S(1)} %copy-done.3, ...), custom_call_target="tpu_custom_call" | custom-call | tf_op jit(solution)/shard_map/new_state/pallas_call | solution.py:160
  (4 shorter events, 0.1 us)
Async XLA Ops:
  1.6 1.7 %collective-permute-start = (bf16[8,32,512]{2,1,0:T(8,128)(2,1)S(1)}, bf16[8,32,512]{2,1,0:T(8,128)(2,1)S(1)}, u32[]{:S(2)}, u32[]{:S(2)}) collective-permute-start(bf16[8,32,512]{2,1,0:T(8,128)(2,1)S(1)} %state_half.1), channel_id=1, source_target_pairs={{0,64},{64,0},{1,65},{65,1},{2,66},{66,2},{3,67},{67,3},{4,68},{68... | collective-permute-start | bytes 786440 | tf_op jit(solution)/shard_map/ppermute | solution.py:48
  51.9 12.6 %collective-permute-start.2 = (bf16[64,2,4,512]{3,0,2,1:T(8,128)(2,1)S(1)}, bf16[64,2,4,512]{3,0,2,1:T(8,128)(2,1)S(1)}, u32[]{:S(2)}, u32[]{:S(2)}) collective-permute-start(bf16[64,2,4,512]{3,0,2,1:T(8,128)(2,1)S(1)} %copy.19), channel_id=1, source_target_pairs={{0,64},{64,0},{1,65},{65,1},{2,66},{66,2},{3,67},{67,3},{4,68},{68... | collective-permute-start | bytes 1572872 | tf_op jit(solution)/shard_map/ppermute | solution.py:48
  52.0 12.5 %all-to-all-start.2 = ((bf16[8,32,512]{2,1,0:T(8,128)(2,1)}), bf16[8,32,512]{2,1,0:T(8,128)(2,1)S(1)}, u32[]{:S(2)}, u32[]{:S(2)}) async-start(bf16[8,32,512]{2,1,0:T(8,128)(2,1)} %get-tuple-element.12), calls=%async_computation.2 | async-start | bytes 524288 | tf_op jit(solution)/shard_map/all_to_all | solution.py:44
  64.4 1.5 %collective-permute-start.1 = (bf16[256,512]{1,0:T(8,128)(2,1)S(1)}, bf16[256,512]{1,0:T(8,128)(2,1)S(1)}, u32[]{:S(2)}, u32[]{:S(2)}) collective-permute-start(bf16[256,512]{1,0:T(8,128)(2,1)S(1)} %bitcast.23), channel_id=1, source_target_pairs={{0,64},{64,0},{1,65},{65,1},{2,66},{66,2},{3,67},{67,3},{4,68},{68... | collective-permute-start | bytes 786440 | tf_op jit(solution)/shard_map/ppermute | solution.py:48
  64.7 20.8 %copy-start = (f32[8,8,512]{2,1,0:T(8,128)S(1)}, f32[8,8,512]{2,1,0:T(8,128)}, u32[]{:S(2)}) copy-start(f32[8,8,512]{2,1,0:T(8,128)} %first.5) | copy-start | bytes 393220
  64.7 20.8 %copy-start.1 = (f32[8,8,512]{2,1,0:T(8,128)S(1)}, f32[8,8,512]{2,1,0:T(8,128)}, u32[]{:S(2)}) copy-start(f32[8,8,512]{2,1,0:T(8,128)} %second.5) | copy-start | bytes 393220
  64.7 20.8 %copy-start.2 = (f32[8,8,512]{2,1,0:T(8,128)S(1)}, f32[8,8,512]{2,1,0:T(8,128)}, u32[]{:S(2)}) copy-start(f32[8,8,512]{2,1,0:T(8,128)} %gram_l.1) | copy-start | bytes 393220
  64.7 20.8 %copy-start.3 = (f32[8,8,512]{2,1,0:T(8,128)S(1)}, f32[8,8,512]{2,1,0:T(8,128)}, u32[]{:S(2)}) copy-start(f32[8,8,512]{2,1,0:T(8,128)} %gram_r.1) | copy-start | bytes 393220
  64.7 20.8 %copy-start.4 = (s32[2,8]{1,0:T(2,128)S(1)}, s32[2,8]{1,0:T(2,128)}, u32[]{:S(2)}) copy-start(s32[2,8]{1,0:T(2,128)} %slot_block.3) | copy-start | bytes 196

commit v3 on v2

--- a/solution.py
+++ b/solution.py
@@ -19,8 +19,8 @@
     for axis in range(3):
         place = (dp >> (2 * axis)) & 3
         wrap, inner = place >> 1, (place ^ (place >> 1)) & 1
-        b += (inner if axis == 0 else wrap) << axis
-        g += (wrap if axis == 0 else inner) << axis
+        b += (inner if axis == 2 else wrap) << axis
+        g += (wrap if axis == 2 else inner) << axis
     return b, g
 
 
@@ -69,12 +69,12 @@
     return pltpu.with_memory_space_constraint(x, pltpu.HBM)
 
 
-def local_call(kernel, name, out_shape, in_specs, scratch=(), **options):
+def local_call(kernel, name, out_shape, in_specs, scratch=(), out=WHOLE, **options):
     return pl.pallas_call(
         kernel,
         out_shape=out_shape,
         in_specs=in_specs,
-        out_specs=jax.tree.map(lambda _: WHOLE, out_shape),
+        out_specs=jax.tree.map(lambda _: out, out_shape),
         scratch_shapes=list(scratch),
         compiler_params=pltpu.CompilerParams(vmem_limit_bytes=40 * 2**20),
         name=name,
@@ -129,37 +129,57 @@
     return local_call(chain_kernel, "block_chain", out, [WHOLE] * 6)(raw, *others)
 
 
-def finish_kernel(slot_block, home, gram_l, gram_r, first, second, *outs):
-    gram_l_new, gram_r_new, first_new, second_new, direction = outs
-    core = lax.axis_index("fsdp")
+def finish_kernel(slot_block, home, gram_l, gram_r, first, second, *refs):
+    outs, built, sent = refs[:5], refs[5:10], refs[10]
+    core = lax.axis_index("fsdp")
+    blocks = home.shape[0]
     n, col = iota((32, 64), 0), iota((32, 64), 1)
     kind, chip, row = n >> 3, col >> 3, col & 7
     other = row - 4 * (1 - core)
     product = (chip == (n & 7)) & ((other == kind) | ((kind == 2) & (other == 3)))
     hit = ((kind == 3) & (row - 4 * core == (n & 7))) | ((kind < 3) & product)
     take = one_hot(hit)
-    for b in range(home.shape[0]):
-        direction[b] = dot(take[24:], home[b])[:4].astype(jnp.bfloat16)
     share = jnp.where(slot_block[core, 0] >= 0, 1.0, 0.0)
-    for slot in range(home.shape[0]):
+    copies = []
+    for slot in range(blocks):
         block = jnp.maximum(slot_block[core, slot], 0)
         rows = dot(take, home[block]) * share
         rotated = rows[16:24]
-        gram_l_new[slot] = shampoo_beta * gram_l[slot] + (1.0 - shampoo_beta) * rows[:8]
-        gram_r_new[slot] = shampoo_beta * gram_r[slot] + (1.0 - shampoo_beta) * rows[8:16]
-        first_new[slot] = adam_first * first[slot] + (1.0 - adam_first) * rotated
-        second_new[slot] = (
+        built[0][slot] = shampoo_beta * gram_l[slot] + (1.0 - shampoo_beta) * rows[:8]
+        built[1][slot] = shampoo_beta * gram_r[slot] + (1.0 - shampoo_beta) * rows[8:16]
+        built[2][slot] = adam_first * first[slot] + (1.0 - adam_first) * rotated
+        built[3][slot] = (
             adam_second * second[slot] + (1.0 - adam_second) * rotated * rotated
         )
+        if slot % 4 == 3:
+            part = pl.ds(slot - 3, 4)
+            for i in range(4):
+                copies.append(
+                    pltpu.make_async_copy(
+                        built[i].at[part], outs[i].at[part], sent.at[i, slot // 4]
+                    )
+                )
+                copies[-1].start()
+    for b in range(blocks):
+        built[4][b] = dot(take[24:], home[b])[:4].astype(jnp.bfloat16)
+    copies.append(pltpu.make_async_copy(built[4], outs[4], sent.at[4, 0]))
+    copies[-1].start()
+    for copy in copies:
+        copy.wait()
 
 
 def finish(slot_block, home, states):
     blocks, width = home.shape[0], home.shape[2]
     outs = [jax.ShapeDtypeStruct(x.shape, x.dtype) for x in states]
     outs.append(jax.ShapeDtypeStruct((blocks, 4, width), jnp.bfloat16))
-    return local_call(finish_kernel, "new_state", outs, [SCALARS] + [WHOLE] * 5)(
-        slot_block, home, *states
-    )
+    return local_call(
+        finish_kernel,
+        "new_state",
+        outs,
+        [SCALARS] + [WHOLE] * 5,
+        [pltpu.VMEM(x.shape, x.dtype) for x in outs] + [pltpu.SemaphoreType.DMA((5, 2))],
+        out=FAR,
+    )(slot_block, home, *states)
 
 
 def on_core(zero, one):
@@ -174,32 +194,34 @@
     return jnp.concatenate(rows, axis=0)
 
 
-def give_kernel(left_t, right, first, second, out, left_here, right_here, moment, done):
+def halves_kernel(left_t, right, first, second, keep, give, *scratch):
+    held, done = scratch[:4], scratch[4]
     copies = [
-        pltpu.make_async_copy(left_t, left_here, done.at[0]),
-        pltpu.make_async_copy(right, right_here, done.at[1]),
+        pltpu.make_async_copy(source, to, done.at[i])
+        for i, (source, to) in enumerate(zip((left_t, right, first, second), held))
     ]
-    first_copy = pltpu.make_async_copy(first, moment, done.at[2])
-    second_copy = pltpu.make_async_copy(second, moment, done.at[2])
-    on_core(second_copy.start, first_copy.start)
     for copy in copies:
         copy.start()
     for copy in copies:
         copy.wait()
-    on_core(second_copy.wait, first_copy.wait)
-    for slot in range(out.shape[0]):
-        rows = half_rows(left_here[slot], right_here[slot], moment[slot])
-        out[slot] = rows.astype(jnp.bfloat16)
-
-
-def give_half(*states):
+    core = lax.axis_index("fsdp")
+    for slot in range(keep.shape[0]):
+        left_rows, right_rows, one, two = (part[slot] for part in held)
+        for out, moment in (
+            (keep, jnp.where(core == 0, one, two)),
+            (give, jnp.where(core == 0, two, one)),
+        ):
+            out[slot] = half_rows(left_rows, right_rows, moment).astype(jnp.bfloat16)
+
+
+def halves(*states):
     blocks, rows, width = states[0].shape
     return local_call(
-        give_kernel,
-        "state_half",
-        jax.ShapeDtypeStruct((blocks, 4 * rows, width), jnp.bfloat16),
+        halves_kernel,
+        "state_halves",
+        [jax.ShapeDtypeStruct((blocks, 4 * rows, width), jnp.bfloat16)] * 2,
         [FAR] * 4,
-        [pltpu.VMEM(x.shape, x.dtype) for x in states[:3]] + [pltpu.SemaphoreType.DMA((3,))],
+        [pltpu.VMEM(x.shape, x.dtype) for x in states] + [pltpu.SemaphoreType.DMA((4,))],
     )(*states)
 
 
@@ -229,49 +251,35 @@
     )(terms)
 
 
-def pack_kernel(slot_block, loaded, given, left_t, right, first, second, out, *scratch):
-    left_here, right_here, moment, done = scratch
+def pack_kernel(slot_block, loaded, keep, given, out):
     core = lax.axis_index("fsdp")
     blocks, span = out.shape[0], out.shape[2] - 2
-    fetch = [
-        pltpu.make_async_copy(left_t, left_here, done.at[0]),
-        pltpu.make_async_copy(right, right_here, done.at[1]),
-    ]
-    first_copy = pltpu.make_async_copy(first, moment, done.at[2])
-    second_copy = pltpu.make_async_copy(second, moment, done.at[2])
-    for copy in fetch:
-        copy.start()
-    on_core(first_copy.start, second_copy.start)
     mine = slot_block[core, 0] >= 0
     n, col = iota((32, 32), 0), iota((32, 32), 1)
     turn = one_hot(col == (((n & 3) + 1) & 3) * 8 + (n >> 2))
-    for copy in fetch:
-        copy.wait()
-    on_core(first_copy.wait, second_copy.wait)
     for b in range(blocks):
         at = 0
         for owner in range(slot_block.shape[0]):
             for slot in range(blocks):
                 at += jnp.where(slot_block[owner, slot] == b, slot, 0)
-        rows = half_rows(left_here[at], right_here[at], moment[at])
-        rows = jnp.where(mine, rows, given[at].astype(jnp.float32))
-        half = jnp.where(core == 0, rows[:4], rows[4:8]).astype(jnp.bfloat16)
-        singles = dot(turn, rows.astype(jnp.bfloat16)).astype(jnp.bfloat16)
+        rows = jnp.where(mine, keep[at], given[at])
+        half = rows[:8].astype(jnp.float32)
+        half = jnp.where(core == 0, half[:4], half[4:]).astype(jnp.bfloat16)
+        singles = dot(turn, rows).astype(jnp.bfloat16)
         for g in EIGHT:
             to, then = jnp.where(core == 0, b, g), jnp.where(core == 0, g, b)
             out[to, then, span] = half
             out[to, then, span + 1] = singles[4 * g : 4 * g + 4]
 
 
-def pack(slot_block, loaded, given, *states):
+def pack(slot_block, loaded, keep, given):
     return local_call(
         pack_kernel,
         "pack_states",
         jax.ShapeDtypeStruct(loaded.shape, loaded.dtype),
-        [SCALARS, WHOLE, WHOLE] + [FAR] * 4,
-        [pltpu.VMEM(x.shape, x.dtype) for x in states[:3]] + [pltpu.SemaphoreType.DMA((3,))],
+        [SCALARS] + [WHOLE] * 3,
         input_output_aliases={1: 0},
-    )(slot_block, loaded, given, *states)
+    )(slot_block, loaded, keep, given)
 
 
 def total_of(received, *at):
@@ -342,7 +350,8 @@
     states = tuple(in_hbm(part) for part in states)
     terms = grad_parts[0].reshape(blocks, GROUP, q_total // GROUP, half_span, width)
     terms = in_hbm(terms)
-    message = pack(in_hbm(slot_block), load(terms), swap_cores(give_half(*states)), *states)
+    keep, give = halves(*states)
+    message = pack(in_hbm(slot_block), load(terms), keep, swap_cores(give))
     received = exchange(relay(exchange(message, FIRST)), SECOND)
     raw, half = sum_terms(received)
     raw = exchange(raw, BLOCK).reshape(-1, width)

time: 87.6 us -> 86.1 us (0.983)
  Pallas kernels: 9.96 us -> 9.08 us
    pallas_call x1, Pallas kernels: 1.97 us -> 0.97 us  [pack(): local_call(pack_kernel, 'pack_states', jax.ShapeDtypeStruct(loaded.shape,...]
where the time goes in v3:
time: 86.1 us; the launch traced here: 85.7 us
  blocking collectives  61.6 us (72%)
  waiting for transfers between devices  9.86 us (11%)
  Pallas kernels  9.08 us (11%)
  starting transfers between devices  3.6 us (4%)
    all_to_all x3, blocking collectives, exchange(): return lax.all_to_all(x, AXES, 0, 0, axis_index_groups=groups, tiled=True)  61.6 us
    all_to_all x1, waiting for transfers between devices, exchange(): return lax.all_to_all(x, AXES, 0, 0, axis_index_groups=groups, tiled=True)  9.03 us
    all_to_all x1, starting transfers between devices, exchange(): return lax.all_to_all(x, AXES, 0, 0, axis_index_groups=groups, tiled=True)  3.42 us
    pallas_call x1, Pallas kernels, chain(): local_call(chain_kernel, 'block_chain', out, [WHOLE] * 6)(raw, *others)  2.14 us
  transfers between devices with their start and end apart: 4, of which 2 were waited for; matrix products, arithmetic and copies ran while one was open for 1% of the time, Pallas kernels for 2%

profile of v3, /device:TPU:0, one launch (start us, length us, event | category | flops | bytes accessed | tf_op | source)
XLA Modules:
  0.0 85.7 jit_solution(17925421635438113853)
XLA Ops:
  0.6 1.1 %state_halves.1 = (bf16[8,32,512]{2,1,0:T(8,128)(2,1)S(1)}, bf16[8,32,512]{2,1,0:T(8,128)(2,1)S(1)}) custom-call(bf16[8,8,512]{2,1,0:T(8,128)(2,1)} %left_t.1, bf16[8,8,512]{2,1,0:T(8,128)(2,1)} %right.1, f32[8,8,512]{2,1,0:T(8,128)} %first.3, f32[8,8,512]{2,1,0:T(8,128)} %second.3), custom_call_target="tpu_custom_call" | custom-call | tf_op jit(solution)/shard_map/state_halves/pallas_call | solution.py:219
  1.8 0.1 collective-permute-start
  1.9 1.6 %load_terms.1.loaded = bf16[8,8,10,4,512]{4,3,2,1,0:T(4,128)(2,1)S(1)} custom-call(bf16[8,8,8,4,512]{4,3,2,1,0:T(4,128)(2,1)} %bitcast.25), custom_call_target="tpu_custom_call" | custom-call | bytes 4194304 | tf_op jit(solution)/shard_map/load_terms/pallas_call | solution.py:244
  3.5 0.0 collective-permute-done.given
  3.5 1.0 %pack_states.1 = bf16[8,8,10,4,512]{4,3,2,1,0:T(4,128)(2,1)S(1)} custom-call(s32[2,8]{1,0:T(2,128)} %slot_block.3, bf16[8,8,10,4,512]{4,3,2,1,0:T(4,128)(2,1)S(1)} %load_terms.1.loaded, bf16[8,32,512]{2,1,0:T(8,128)(2,1)S(1)} %get-tuple-element.14.keep, bf16[8,32,512]{2,1,0:T(8,128)(2,1)S(1)} %collective-permute-done.given), custom_call_target="tpu_custom_call", output_to_operand_aliasing={{}: (1, {})} | custom-call | tf_op jit(solution)/shard_map/pack_states/pallas_call | solution.py:276
  4.4 29.8 %all_to_all.20.received = bf16[8,8,10,4,512]{4,3,2,1,0:T(4,128)(2,1)S(1)} all-to-all(bf16[8,8,10,4,512]{4,3,2,1,0:T(4,128)(2,1)S(1)} %pack_states.1), channel_id=1, replica_groups={{0,3,12,15,16,19,28,31},{1,2,13,14,17,18,29,30},{4,7,8,11,20,23,24,27},..., dimensions={0} | all-to-all | bytes 5242880 | tf_op jit(solution)/shard_map/all_to_all | solution.py:44
  34.2 0.8 relay.1
  35.0 14.7 %all_to_all.21.received = bf16[8,24,4,512]{3,2,1,0:T(4,128)(2,1)S(1)} all-to-all(bf16[8,24,4,512]{3,2,1,0:T(4,128)(2,1)S(1)} %relay.1), channel_id=1, replica_groups={{0,1,4,5,48,49,52,53},{3,2,7,6,51,50,55,54},{12,13,8,9,60,61,56,57},{15..., dimensions={0} | all-to-all | bytes 1572864 | tf_op jit(solution)/shard_map/all_to_all | solution.py:44
  49.8 0.8 sum_terms.1
  50.6 0.2 copy.19
  50.7 0.1 collective-permute-start.2
  50.8 3.4 %all-to-all-start.2 = ((bf16[8,32,512]{2,1,0:T(8,128)(2,1)}), bf16[8,32,512]{2,1,0:T(8,128)(2,1)S(1)}, u32[]{:S(2)}, u32[]{:S(2)}) async-start(bf16[8,32,512]{2,1,0:T(8,128)(2,1)} %get-tuple-element.16), calls=%async_computation.2 | async-start | bytes 524288 | tf_op jit(solution)/shard_map/all_to_all | solution.py:44
  54.3 9.0 %all-to-all-done.2 = bf16[8,32,512]{2,1,0:T(8,128)(2,1)S(1)} async-done(((bf16[8,32,512]{2,1,0:T(8,128)(2,1)}), bf16[8,32,512]{2,1,0:T(8,128)(2,1)S(1)}, u32[]{:S(2)}, u32[]{:S(2)}) %all-to-all-start.2) | async-done | bytes 262176 | tf_op jit(solution)/shard_map/all_to_all | solution.py:44
  63.3 0.0 collective-permute-start.1
  63.3 0.0 collective-permute-done.2
  63.3 0.2 broadcast_select_fusion.1
  63.6 0.0 copy-start
  63.6 0.0 copy-start.1
  63.6 0.0 copy-start.2
  63.6 0.0 copy-start.3
  63.6 0.0 copy-start.4
  63.7 0.3 copy.26
  64.0 0.8 collective-permute-done.1.swapped
  64.8 2.1 %block_chain.1 = bf16[512,512]{1,0:T(8,128)(2,1)S(1)} custom-call(bf16[256,512]{1,0:T(8,128)(2,1)S(1)} %bitcast.24, bf16[256,512]{1,0:T(8,128)(2,1)S(1)} %collective-permute-done.1.swapped, bf16[512,512]{1,0:T(8,128)(2,1)S(1)} %bitcast.21, bf16[64,512]{1,0:T(8,128)(2,1)S(1)} %slice_bitcast_fusion.2.left_t, f32[64,512]{1,0:T(8,128)S(1)} %get-tuple-element.38.first, ...), custom_call_target="tpu_custom_call" | custom-call | tf_op jit(solution)/shard_map/block_chain/pallas_call | solution.py:129
  67.0 17.1 %all_to_all.22 = bf16[64,8,512]{2,1,0:T(8,128)(2,1)S(1)} all-to-all(bf16[64,8,512]{2,1,0:T(8,128)(2,1)S(1)} %bitcast.22), channel_id=1, replica_groups={{0,1,4,5,48,49,52,53,3,2,7,6,51,50,55,54,12,13,8,9,60,61,56,57,15,14,11..., dimensions={0} | all-to-all | bytes 1048576 | tf_op jit(solution)/shard_map/all_to_all | solution.py:44
  84.1 0.0 copy-done
  84.1 0.0 copy-done.1
  84.1 0.0 copy-done.2
  84.1 0.0 copy-done.3
  84.1 0.0 copy-done.4
  84.1 1.6 %new_state.1 = (f32[8,8,512]{2,1,0:T(8,128)}, f32[8,8,512]{2,1,0:T(8,128)}, f32[8,8,512]{2,1,0:T(8,128)}, f32[8,8,512]{2,1,0:T(8,128)}, bf16[8,4,512]{2,1,0:T(4,128)(2,1)}) custom-call(s32[2,8]{1,0:T(2,128)S(1)} %copy-done.4, bf16[8,64,512]{2,1,0:T(8,128)(2,1)S(1)} %bitcast.20, f32[8,8,512]{2,1,0:T(8,128)S(1)} %copy-done.2, f32[8,8,512]{2,1,0:T(8,128)S(1)} %copy-done.3, ...), custom_call_target="tpu_custom_call" | custom-call | tf_op jit(solution)/shard_map/new_state/pallas_call | solution.py:175
  (4 shorter events, 0.1 us)
Async XLA Ops:
  1.8 1.7 %collective-permute-start = (bf16[8,32,512]{2,1,0:T(8,128)(2,1)S(1)}, bf16[8,32,512]{2,1,0:T(8,128)(2,1)S(1)}, u32[]{:S(2)}, u32[]{:S(2)}) collective-permute-start(bf16[8,32,512]{2,1,0:T(8,128)(2,1)S(1)} %get-tuple-element.15), channel_id=1, source_target_pairs={{0,64},{64,0},{1,65},{65,1},{2,66},{66,2},{3,67},{67,3},{4,68},{68... | collective-permute-start | bytes 786440 | tf_op jit(solution)/shard_map/ppermute | solution.py:48
  50.7 12.6 %collective-permute-start.2 = (bf16[64,2,4,512]{3,0,2,1:T(8,128)(2,1)S(1)}, bf16[64,2,4,512]{3,0,2,1:T(8,128)(2,1)S(1)}, u32[]{:S(2)}, u32[]{:S(2)}) collective-permute-start(bf16[64,2,4,512]{3,0,2,1:T(8,128)(2,1)S(1)} %copy.19), channel_id=1, source_target_pairs={{0,64},{64,0},{1,65},{65,1},{2,66},{66,2},{3,67},{67,3},{4,68},{68... | collective-permute-start | bytes 1572872 | tf_op jit(solution)/shard_map/ppermute | solution.py:48
  50.8 12.5 %all-to-all-start.2 = ((bf16[8,32,512]{2,1,0:T(8,128)(2,1)}), bf16[8,32,512]{2,1,0:T(8,128)(2,1)S(1)}, u32[]{:S(2)}, u32[]{:S(2)}) async-start(bf16[8,32,512]{2,1,0:T(8,128)(2,1)} %get-tuple-element.16), calls=%async_computation.2 | async-start | bytes 524288 | tf_op jit(solution)/shard_map/all_to_all | solution.py:44
  63.3 1.5 %collective-permute-start.1 = (bf16[256,512]{1,0:T(8,128)(2,1)S(1)}, bf16[256,512]{1,0:T(8,128)(2,1)S(1)}, u32[]{:S(2)}, u32[]{:S(2)}) collective-permute-start(bf16[256,512]{1,0:T(8,128)(2,1)S(1)} %bitcast.23), channel_id=1, source_target_pairs={{0,64},{64,0},{1,65},{65,1},{2,66},{66,2},{3,67},{67,3},{4,68},{68... | collective-permute-start | bytes 786440 | tf_op jit(solution)/shard_map/ppermute | solution.py:48
  63.6 20.5 %copy-start = (f32[8,8,512]{2,1,0:T(8,128)S(1)}, f32[8,8,512]{2,1,0:T(8,128)}, u32[]{:S(2)}) copy-start(f32[8,8,512]{2,1,0:T(8,128)} %first.3) | copy-start | bytes 393220
  63.6 20.5 %copy-start.1 = (f32[8,8,512]{2,1,0:T(8,128)S(1)}, f32[8,8,512]{2,1,0:T(8,128)}, u32[]{:S(2)}) copy-start(f32[8,8,512]{2,1,0:T(8,128)} %second.3) | copy-start | bytes 393220
  63.6 20.5 %copy-start.2 = (f32[8,8,512]{2,1,0:T(8,128)S(1)}, f32[8,8,512]{2,1,0:T(8,128)}, u32[]{:S(2)}) copy-start(f32[8,8,512]{2,1,0:T(8,128)} %gram_l.1) | copy-start | bytes 393220
  63.6 20.5 %copy-start.3 = (f32[8,8,512]{2,1,0:T(8,128)S(1)}, f32[8,8,512]{2,1,0:T(8,128)}, u32[]{:S(2)}) copy-start(f32[8,8,512]{2,1,0:T(8,128)} %gram_r.1) | copy-start | bytes 393220
  63.6 20.5 %copy-start.4 = (s32[2,8]{1,0:T(2,128)S(1)}, s32[2,8]{1,0:T(2,128)}, u32[]{:S(2)}) copy-start(s32[2,8]{1,0:T(2,128)} %slot_block.3) | copy-start | bytes 196

commit v4 on v3

--- a/solution.py
+++ b/solution.py
@@ -188,12 +188,6 @@
     pl.when(core != 0)(one)
 
 
-def half_rows(left_t, right, moment):
-    upper = moment.astype(jnp.bfloat16).astype(jnp.float32)
-    rows = [right.astype(jnp.float32), left_t.astype(jnp.float32), upper, moment - upper]
-    return jnp.concatenate(rows, axis=0)
-
-
 def halves_kernel(left_t, right, first, second, keep, give, *scratch):
     held, done = scratch[:4], scratch[4]
     copies = [
@@ -206,12 +200,12 @@
         copy.wait()
     core = lax.axis_index("fsdp")
     for slot in range(keep.shape[0]):
-        left_rows, right_rows, one, two = (part[slot] for part in held)
-        for out, moment in (
-            (keep, jnp.where(core == 0, one, two)),
-            (give, jnp.where(core == 0, two, one)),
-        ):
-            out[slot] = half_rows(left_rows, right_rows, moment).astype(jnp.bfloat16)
+        left_rows, right_rows, one, two = (part[slot].astype(jnp.float32) for part in held)
+        upper = one.astype(jnp.bfloat16).astype(jnp.float32)
+        whole = jnp.concatenate([right_rows] * 4, axis=0)
+        singles = jnp.concatenate([left_rows, upper, one - upper, two], axis=0)
+        keep[slot] = jnp.where(core == 0, whole, singles).astype(jnp.bfloat16)
+        give[slot] = jnp.where(core == 0, singles, whole).astype(jnp.bfloat16)
 
 
 def halves(*states):
@@ -225,13 +219,15 @@
     )(*states)
 
 
-def load_kernel(terms, out, done):
-    blocks, units = terms.shape[0], pl.ds(0, terms.shape[2])
+def load_kernel(terms, by_block, out, done):
+    blocks, chips, span = terms.shape[:3]
     near = [
-        pltpu.make_async_copy(terms.at[b], out.at[b, :, units], done.at[b]) for b in range(blocks)
+        pltpu.make_async_copy(by_block.at[b], out.at[b, pl.ds(0, chips * span)], done.at[b])
+        for b in range(blocks)
     ]
     cross = [
-        pltpu.make_async_copy(terms.at[b], out.at[:, b, units], done.at[b]) for b in range(blocks)
+        pltpu.make_async_copy(terms.at[b], out.at[:, pl.ds(b * span, span)], done.at[b])
+        for b in range(blocks)
     ]
     for b in range(blocks):
         on_core(near[b].start, cross[b].start)
@@ -244,32 +240,38 @@
     return local_call(
         load_kernel,
         "load_terms",
-        jax.ShapeDtypeStruct((blocks, chips, span + 2, rows, width), terms.dtype),
-        [FAR],
+        jax.ShapeDtypeStruct((blocks, chips * span + GROUP, rows, width), terms.dtype),
+        [FAR] * 2,
         [pltpu.SemaphoreType.DMA((blocks,))],
         cost_estimate=pl.CostEstimate(flops=0, bytes_accessed=2 * terms.nbytes, transcendentals=0),
-    )(terms)
+    )(in_hbm(terms), in_hbm(terms.reshape(blocks, chips * span, rows, width)))
 
 
 def pack_kernel(slot_block, loaded, keep, given, out):
     core = lax.axis_index("fsdp")
-    blocks, span = out.shape[0], out.shape[2] - 2
+    blocks = out.shape[0]
+    units = out.shape[1] - GROUP
     mine = slot_block[core, 0] >= 0
     n, col = iota((32, 32), 0), iota((32, 32), 1)
-    turn = one_hot(col == (((n & 3) + 1) & 3) * 8 + (n >> 2))
+    turn = one_hot(col == (n & 3) * 8 + (n >> 2))
     for b in range(blocks):
         at = 0
         for owner in range(slot_block.shape[0]):
             for slot in range(blocks):
                 at += jnp.where(slot_block[owner, slot] == b, slot, 0)
         rows = jnp.where(mine, keep[at], given[at])
-        half = rows[:8].astype(jnp.float32)
-        half = jnp.where(core == 0, half[:4], half[4:]).astype(jnp.bfloat16)
-        singles = dot(turn, rows).astype(jnp.bfloat16)
-        for g in EIGHT:
-            to, then = jnp.where(core == 0, b, g), jnp.where(core == 0, g, b)
-            out[to, then, span] = half
-            out[to, then, span + 1] = singles[4 * g : 4 * g + 4]
+
+        def whole(b=b, rows=rows):
+            right = rows[:8].astype(jnp.float32)
+            out[b, units] = right[:4].astype(jnp.bfloat16)
+            out[b, units + 1] = right[4:].astype(jnp.bfloat16)
+
+        def singles(b=b, rows=rows):
+            turned = dot(turn, rows).astype(jnp.bfloat16)
+            for g in EIGHT:
+                out[g, units + b] = turned[4 * g : 4 * g + 4]
+
+        on_core(whole, singles)
 
 
 def pack(slot_block, loaded, keep, given):
@@ -287,37 +289,54 @@
 
 
 def relay_kernel(received, out):
-    span = received.shape[2] - 2
+    units = received.shape[1] - GROUP
+    span = units // GROUP
     for then in EIGHT:
         for unit in range(span):
-            out[then, unit] = total_of(received, then, unit).astype(jnp.bfloat16)
+            total = total_of(received, then * span + unit)
+            out[then, unit] = total.astype(jnp.bfloat16)
+
+    def whole():
         for source in EIGHT:
-            at = span + 2 * source
-            out[then, at] = received[source, then, span]
-            out[then, at + 1] = received[source, then, span + 1]
+            for i in range(2):
+                rows = received[source, units + i]
+                for then in EIGHT:
+                    out[then, span + 2 * source + i] = rows
+
+    def singles():
+        for source in EIGHT:
+            for then in EIGHT:
+                out[then, span + source] = received[source, units + then]
+
+    on_core(whole, singles)
 
 
 def relay(received):
-    span = received.shape[2] - 2
-    shape = (GROUP, span + 2 * GROUP) + received.shape[3:]
+    span = received.shape[1] // GROUP - 1
+    shape = (GROUP, span + 2 * GROUP) + received.shape[2:]
     out = jax.ShapeDtypeStruct(shape, received.dtype)
     return local_call(relay_kernel, "relay", out, [WHOLE])(received)
 
 
 def sum_kernel(received, copies, state):
-    core = lax.axis_index("fsdp")
     span = received.shape[1] - 2 * GROUP
     total = jnp.concatenate([total_of(received, unit) for unit in range(span)], axis=0)
     total = total.astype(jnp.bfloat16)
     for peer in range(copies.shape[0]):
         copies[peer] = total
-    for later in EIGHT:
-        for early in EIGHT:
-            one, two = PLACE[early, later], PLACE[later, early]
-            to = jnp.where(core == 0, one, two)
-            at = span + 2 * early
-            state[to, 0] = received[later, at]
-            state[to, 1] = received[later, at + 1]
+
+    def whole():
+        for later in EIGHT:
+            for early in EIGHT:
+                for i in range(2):
+                    state[PLACE[early, later], i] = received[later, span + 2 * early + i]
+
+    def singles():
+        for later in EIGHT:
+            for early in EIGHT:
+                state[PLACE[later, early], 0] = received[later, span + early]
+
+    on_core(whole, singles)
 
 
 def sum_terms(received):
@@ -349,7 +368,6 @@
     states = (left_basis_t, right_basis, moment_first, moment_second)
     states = tuple(in_hbm(part) for part in states)
     terms = grad_parts[0].reshape(blocks, GROUP, q_total // GROUP, half_span, width)
-    terms = in_hbm(terms)
     keep, give = halves(*states)
     message = pack(in_hbm(slot_block), load(terms), keep, swap_cores(give))
     received = exchange(relay(exchange(message, FIRST)), SECOND)
@@ -357,12 +375,11 @@
     raw = exchange(raw, BLOCK).reshape(-1, width)
 
     given = swap_cores(half)
-    low = jnp.where(core == 0, half, given)
-    high = jnp.where(core == 0, given, half)
-    right = jnp.concatenate([low[:, 0], high[:, 0]], axis=1).reshape(width, width)
-    left_t = low[:, 1, 0]
-    first = low[:, 1, 1].astype(jnp.float32) + low[:, 1, 2].astype(jnp.float32)
-    second = high[:, 1, 1].astype(jnp.float32) + high[:, 1, 2].astype(jnp.float32)
+    right = jnp.where(core == 0, half, given).reshape(width, width)
+    singles = jnp.where(core == 0, given, half)[:, 0]
+    left_t = singles[:, 0]
+    first = singles[:, 1].astype(jnp.float32) + singles[:, 2].astype(jnp.float32)
+    second = singles[:, 3].astype(jnp.float32)
 
     home = chain(raw, swap_cores(raw), right, left_t, first, second)
     home = exchange(home.reshape(blocks * GROUP, 8, width), ALL)

time: 86.1 us -> 84.8 us (0.985)
  blocking collectives: 61.6 us -> 60.2 us
    all_to_all x3, blocking collectives: 61.6 us -> 60.2 us  [exchange(): return lax.all_to_all(x, AXES, 0, 0, axis_index_groups=groups, tiled=True)]
where the time goes in v4:
time: 84.8 us; the launch traced here: 84.4 us
  blocking collectives  60.2 us (71%)
  waiting for transfers between devices  9.69 us (11%)
  Pallas kernels  9.12 us (11%)
  starting transfers between devices  3.6 us (4%)
    all_to_all x3, blocking collectives, exchange(): return lax.all_to_all(x, AXES, 0, 0, axis_index_groups=groups, tiled=True)  60.2 us
    all_to_all x1, waiting for transfers between devices, exchange(): return lax.all_to_all(x, AXES, 0, 0, axis_index_groups=groups, tiled=True)  9.03 us
    all_to_all x1, starting transfers between devices, exchange(): return lax.all_to_all(x, AXES, 0, 0, axis_index_groups=groups, tiled=True)  3.42 us
    pallas_call x1, Pallas kernels, chain(): local_call(chain_kernel, 'block_chain', out, [WHOLE] * 6)(raw, *others)  2.14 us
  transfers between devices with their start and end apart: 4, of which 2 were waited for; matrix products, arithmetic and copies ran while one was open for 1% of the time, Pallas kernels for 2%

profile of v4, /device:TPU:0, one launch (start us, length us, event | category | flops | bytes accessed | tf_op | source)
XLA Modules:
  0.0 84.4 jit_solution(18273970269318597255)
XLA Ops:
  0.6 1.2 %state_halves.1 = (bf16[8,32,512]{2,1,0:T(8,128)(2,1)S(1)}, bf16[8,32,512]{2,1,0:T(8,128)(2,1)S(1)}) custom-call(bf16[8,8,512]{2,1,0:T(8,128)(2,1)} %left_t.1, bf16[8,8,512]{2,1,0:T(8,128)(2,1)} %right.1, f32[8,8,512]{2,1,0:T(8,128)} %first.3, f32[8,8,512]{2,1,0:T(8,128)} %second.3), custom_call_target="tpu_custom_call" | custom-call | tf_op jit(solution)/shard_map/state_halves/pallas_call | solution.py:213
  1.8 0.1 collective-permute-start
  1.9 1.6 %load_terms.1.loaded = bf16[8,72,4,512]{3,2,1,0:T(4,128)(2,1)S(1)} custom-call(bf16[8,8,8,4,512]{4,3,2,1,0:T(4,128)(2,1)} %bitcast.23, bf16[8,64,4,512]{3,2,1,0:T(4,128)(2,1)} %bitcast.24), custom_call_target="tpu_custom_call" | custom-call | bytes 4194304 | tf_op jit(solution)/shard_map/load_terms/pallas_call | solution.py:240
  3.5 0.0 collective-permute-done.given
  3.5 0.9 %pack_states.1 = bf16[8,72,4,512]{3,2,1,0:T(4,128)(2,1)S(1)} custom-call(s32[2,8]{1,0:T(2,128)} %slot_block.3, bf16[8,72,4,512]{3,2,1,0:T(4,128)(2,1)S(1)} %load_terms.1.loaded, bf16[8,32,512]{2,1,0:T(8,128)(2,1)S(1)} %get-tuple-element.14.keep, bf16[8,32,512]{2,1,0:T(8,128)(2,1)S(1)} %collective-permute-done.given), custom_call_target="tpu_custom_call", output_to_operand_aliasing={{}: (1, {})} | custom-call | tf_op jit(solution)/shard_map/pack_states/pallas_call | solution.py:278
  4.4 28.3 %all_to_all.20.received = bf16[8,72,4,512]{3,2,1,0:T(4,128)(2,1)S(1)} all-to-all(bf16[8,72,4,512]{3,2,1,0:T(4,128)(2,1)S(1)} %pack_states.1), channel_id=1, replica_groups={{0,3,12,15,16,19,28,31},{1,2,13,14,17,18,29,30},{4,7,8,11,20,23,24,27},..., dimensions={0} | all-to-all | bytes 4718592 | tf_op jit(solution)/shard_map/all_to_all | solution.py:44
  32.8 0.9 %relay.1 = bf16[8,24,4,512]{3,2,1,0:T(4,128)(2,1)S(1)} custom-call(bf16[8,72,4,512]{3,2,1,0:T(4,128)(2,1)S(1)} %all_to_all.20.received), custom_call_target="tpu_custom_call" | custom-call | tf_op jit(solution)/shard_map/relay/pallas_call | solution.py:318
  33.6 14.7 %all_to_all.21.received = bf16[8,24,4,512]{3,2,1,0:T(4,128)(2,1)S(1)} all-to-all(bf16[8,24,4,512]{3,2,1,0:T(4,128)(2,1)S(1)} %relay.1), channel_id=1, replica_groups={{0,1,4,5,48,49,52,53},{3,2,7,6,51,50,55,54},{12,13,8,9,60,61,56,57},{15..., dimensions={0} | all-to-all | bytes 1572864 | tf_op jit(solution)/shard_map/all_to_all | solution.py:44
  48.4 0.8 sum_terms.1
  49.2 0.2 copy.19
  49.4 0.1 collective-permute-start.2
  49.5 3.4 %all-to-all-start.2 = ((bf16[8,32,512]{2,1,0:T(8,128)(2,1)}), bf16[8,32,512]{2,1,0:T(8,128)(2,1)S(1)}, u32[]{:S(2)}, u32[]{:S(2)}) async-start(bf16[8,32,512]{2,1,0:T(8,128)(2,1)} %get-tuple-element.16), calls=%async_computation.2 | async-start | bytes 524288 | tf_op jit(solution)/shard_map/all_to_all | solution.py:44
  52.9 9.0 %all-to-all-done.2 = bf16[8,32,512]{2,1,0:T(8,128)(2,1)S(1)} async-done(((bf16[8,32,512]{2,1,0:T(8,128)(2,1)}), bf16[8,32,512]{2,1,0:T(8,128)(2,1)S(1)}, u32[]{:S(2)}, u32[]{:S(2)}) %all-to-all-start.2) | async-done | bytes 262176 | tf_op jit(solution)/shard_map/all_to_all | solution.py:44
  61.9 0.0 collective-permute-start.1
  61.9 0.0 collective-permute-done.2
  62.0 0.2 broadcast_select_fusion
  62.2 0.4 copy.20
  62.6 0.0 copy-start
  62.6 0.0 copy-start.1
  62.6 0.0 copy-start.2
  62.6 0.0 copy-start.3
  62.7 0.0 copy-start.4
  62.7 0.1 reshape.28.right
  62.8 0.7 collective-permute-done.1.swapped
  63.5 2.1 %block_chain.1 = bf16[512,512]{1,0:T(8,128)(2,1)S(1)} custom-call(bf16[256,512]{1,0:T(8,128)(2,1)S(1)} %bitcast.22, bf16[256,512]{1,0:T(8,128)(2,1)S(1)} %collective-permute-done.1.swapped, bf16[512,512]{1,0:T(8,128)(2,1)S(1)} %reshape.28.right, bf16[64,512]{1,0:T(8,128)(2,1)S(1)} %get-tuple-element.34.left_t, f32[64,512]{1,0:T(8,128)S(1)} %add_bitcast_fusion.first, ...), custom_call_target="tpu_custom_call" | custom-call | tf_op jit(solution)/shard_map/block_chain/pallas_call | solution.py:129
  65.6 17.1 %all_to_all.22 = bf16[64,8,512]{2,1,0:T(8,128)(2,1)S(1)} all-to-all(bf16[64,8,512]{2,1,0:T(8,128)(2,1)S(1)} %bitcast.20), channel_id=1, replica_groups={{0,1,4,5,48,49,52,53,3,2,7,6,51,50,55,54,12,13,8,9,60,61,56,57,15,14,11..., dimensions={0} | all-to-all | bytes 1048576 | tf_op jit(solution)/shard_map/all_to_all | solution.py:44
  82.7 0.0 copy-done
  82.7 0.0 copy-done.1
  82.7 0.0 copy-done.2
  82.7 0.0 copy-done.3
  82.7 0.0 copy-done.4
  82.7 1.6 %new_state.1 = (f32[8,8,512]{2,1,0:T(8,128)}, f32[8,8,512]{2,1,0:T(8,128)}, f32[8,8,512]{2,1,0:T(8,128)}, f32[8,8,512]{2,1,0:T(8,128)}, bf16[8,4,512]{2,1,0:T(4,128)(2,1)}) custom-call(s32[2,8]{1,0:T(2,128)S(1)} %copy-done.4, bf16[8,64,512]{2,1,0:T(8,128)(2,1)S(1)} %bitcast.19, f32[8,8,512]{2,1,0:T(8,128)S(1)} %copy-done.2, f32[8,8,512]{2,1,0:T(8,128)S(1)} %copy-done.3, ...), custom_call_target="tpu_custom_call" | custom-call | tf_op jit(solution)/shard_map/new_state/pallas_call | solution.py:175
  (3 shorter events, 0.1 us)
Async XLA Ops:
  1.8 1.7 %collective-permute-start = (bf16[8,32,512]{2,1,0:T(8,128)(2,1)S(1)}, bf16[8,32,512]{2,1,0:T(8,128)(2,1)S(1)}, u32[]{:S(2)}, u32[]{:S(2)}) collective-permute-start(bf16[8,32,512]{2,1,0:T(8,128)(2,1)S(1)} %get-tuple-element.15), channel_id=1, source_target_pairs={{0,64},{64,0},{1,65},{65,1},{2,66},{66,2},{3,67},{67,3},{4,68},{68... | collective-permute-start | bytes 786440 | tf_op jit(solution)/shard_map/ppermute | solution.py:48
  49.4 12.6 %collective-permute-start.2 = (bf16[64,2,4,512]{3,0,2,1:T(8,128)(2,1)S(1)}, bf16[64,2,4,512]{3,0,2,1:T(8,128)(2,1)S(1)}, u32[]{:S(2)}, u32[]{:S(2)}) collective-permute-start(bf16[64,2,4,512]{3,0,2,1:T(8,128)(2,1)S(1)} %copy.19), channel_id=1, source_target_pairs={{0,64},{64,0},{1,65},{65,1},{2,66},{66,2},{3,67},{67,3},{4,68},{68... | collective-permute-start | bytes 1572872 | tf_op jit(solution)/shard_map/ppermute | solution.py:48
  49.5 12.5 %all-to-all-start.2 = ((bf16[8,32,512]{2,1,0:T(8,128)(2,1)}), bf16[8,32,512]{2,1,0:T(8,128)(2,1)S(1)}, u32[]{:S(2)}, u32[]{:S(2)}) async-start(bf16[8,32,512]{2,1,0:T(8,128)(2,1)} %get-tuple-element.16), calls=%async_computation.2 | async-start | bytes 524288 | tf_op jit(solution)/shard_map/all_to_all | solution.py:44
  61.9 1.5 %collective-permute-start.1 = (bf16[256,512]{1,0:T(8,128)(2,1)S(1)}, bf16[256,512]{1,0:T(8,128)(2,1)S(1)}, u32[]{:S(2)}, u32[]{:S(2)}) collective-permute-start(bf16[256,512]{1,0:T(8,128)(2,1)S(1)} %bitcast.21), channel_id=1, source_target_pairs={{0,64},{64,0},{1,65},{65,1},{2,66},{66,2},{3,67},{67,3},{4,68},{68... | collective-permute-start | bytes 786440 | tf_op jit(solution)/shard_map/ppermute | solution.py:48
  62.6 20.1 %copy-start = (f32[8,8,512]{2,1,0:T(8,128)S(1)}, f32[8,8,512]{2,1,0:T(8,128)}, u32[]{:S(2)}) copy-start(f32[8,8,512]{2,1,0:T(8,128)} %first.3) | copy-start | bytes 393220
  62.6 20.1 %copy-start.1 = (f32[8,8,512]{2,1,0:T(8,128)S(1)}, f32[8,8,512]{2,1,0:T(8,128)}, u32[]{:S(2)}) copy-start(f32[8,8,512]{2,1,0:T(8,128)} %second.3) | copy-start | bytes 393220
  62.6 20.1 %copy-start.2 = (f32[8,8,512]{2,1,0:T(8,128)S(1)}, f32[8,8,512]{2,1,0:T(8,128)}, u32[]{:S(2)}) copy-start(f32[8,8,512]{2,1,0:T(8,128)} %gram_l.1) | copy-start | bytes 393220
  62.6 20.1 %copy-start.3 = (f32[8,8,512]{2,1,0:T(8,128)S(1)}, f32[8,8,512]{2,1,0:T(8,128)}, u32[]{:S(2)}) copy-start(f32[8,8,512]{2,1,0:T(8,128)} %gram_r.1) | copy-start | bytes 393220
  62.7 20.1 %copy-start.4 = (s32[2,8]{1,0:T(2,128)S(1)}, s32[2,8]{1,0:T(2,128)}, u32[]{:S(2)}) copy-start(s32[2,8]{1,0:T(2,128)} %slot_block.3) | copy-start | bytes 196

commit v5 on v4

--- a/solution.py
+++ b/solution.py
@@ -19,8 +19,8 @@
     for axis in range(3):
         place = (dp >> (2 * axis)) & 3
         wrap, inner = place >> 1, (place ^ (place >> 1)) & 1
-        b += (inner if axis == 2 else wrap) << axis
-        g += (wrap if axis == 2 else inner) << axis
+        b += (wrap if axis == 2 else inner) << axis
+        g += (inner if axis == 2 else wrap) << axis
     return b, g
 
 
@@ -142,8 +142,10 @@
     share = jnp.where(slot_block[core, 0] >= 0, 1.0, 0.0)
     copies = []
     for slot in range(blocks):
-        block = jnp.maximum(slot_block[core, slot], 0)
-        rows = dot(take, home[block]) * share
+        block = jnp.maximum(slot_block[0, slot], slot_block[1, slot])
+        rows = dot(take, home[block])
+        built[4][block] = rows[24:28].astype(jnp.bfloat16)
+        rows = rows[:24] * share
         rotated = rows[16:24]
         built[0][slot] = shampoo_beta * gram_l[slot] + (1.0 - shampoo_beta) * rows[:8]
         built[1][slot] = shampoo_beta * gram_r[slot] + (1.0 - shampoo_beta) * rows[8:16]
@@ -160,8 +162,6 @@
                     )
                 )
                 copies[-1].start()
-    for b in range(blocks):
-        built[4][b] = dot(take[24:], home[b])[:4].astype(jnp.bfloat16)
     copies.append(pltpu.make_async_copy(built[4], outs[4], sent.at[4, 0]))
     copies[-1].start()
     for copy in copies:
@@ -221,18 +221,19 @@
 
 def load_kernel(terms, by_block, out, done):
     blocks, chips, span = terms.shape[:3]
-    near = [
-        pltpu.make_async_copy(by_block.at[b], out.at[b, pl.ds(0, chips * span)], done.at[b])
-        for b in range(blocks)
-    ]
-    cross = [
-        pltpu.make_async_copy(terms.at[b], out.at[:, pl.ds(b * span, span)], done.at[b])
-        for b in range(blocks)
-    ]
+    part = chips // 2
+    near, cross = [], []
     for b in range(blocks):
-        on_core(near[b].start, cross[b].start)
-    for b in range(blocks):
-        on_core(near[b].wait, cross[b].wait)
+        for i in range(2):
+            units, some = pl.ds(i * part * span, part * span), pl.ds(i * part, part)
+            near.append((by_block.at[b, units], out.at[b, units]))
+            cross.append((terms.at[b, some], out.at[some, pl.ds(b * span, span)]))
+    near = [pltpu.make_async_copy(*ends, done.at[i]) for i, ends in enumerate(near)]
+    cross = [pltpu.make_async_copy(*ends, done.at[i]) for i, ends in enumerate(cross)]
+    for one, two in zip(near, cross):
+        on_core(one.start, two.start)
+    for one, two in zip(near, cross):
+        on_core(one.wait, two.wait)
 
 
 def load(terms):
@@ -242,7 +243,7 @@
         "load_terms",
         jax.ShapeDtypeStruct((blocks, chips * span + GROUP, rows, width), terms.dtype),
         [FAR] * 2,
-        [pltpu.SemaphoreType.DMA((blocks,))],
+        [pltpu.SemaphoreType.DMA((2 * blocks,))],
         cost_estimate=pl.CostEstimate(flops=0, bytes_accessed=2 * terms.nbytes, transcendentals=0),
     )(in_hbm(terms), in_hbm(terms.reshape(blocks, chips * span, rows, width)))
 
@@ -328,13 +329,17 @@
     def whole():
         for later in EIGHT:
             for early in EIGHT:
-                for i in range(2):
-                    state[PLACE[early, later], i] = received[later, span + 2 * early + i]
+                at = span + 2 * early
+                pair = [received[later, at + i].astype(jnp.float32) for i in range(2)]
+                rows = jnp.concatenate(pair, axis=0)
+                state[PLACE[early, later]] = rows.astype(jnp.bfloat16)
 
     def singles():
         for later in EIGHT:
             for early in EIGHT:
-                state[PLACE[later, early], 0] = received[later, span + early]
+                rows = received[later, span + early].astype(jnp.float32)
+                rows = jnp.concatenate([rows, rows], axis=0)
+                state[PLACE[later, early]] = rows.astype(jnp.bfloat16)
 
     on_core(whole, singles)
 
@@ -344,7 +349,7 @@
     span = received.shape[1] - 2 * GROUP
     outs = [
         jax.ShapeDtypeStruct((GROUP, span * rows, width), received.dtype),
-        jax.ShapeDtypeStruct((GROUP * GROUP, 2, rows, width), received.dtype),
+        jax.ShapeDtypeStruct((GROUP * GROUP, 2 * rows, width), received.dtype),
     ]
     return local_call(sum_kernel, "sum_terms", outs, [WHOLE])(received)
 
@@ -376,7 +381,7 @@
 
     given = swap_cores(half)
     right = jnp.where(core == 0, half, given).reshape(width, width)
-    singles = jnp.where(core == 0, given, half)[:, 0]
+    singles = jnp.where(core == 0, given, half)
     left_t = singles[:, 0]
     first = singles[:, 1].astype(jnp.float32) + singles[:, 2].astype(jnp.float32)
     second = singles[:, 3].astype(jnp.float32)

time: 84.8 us -> 87 us (1.026)
  waiting for transfers between devices: 9.69 us -> 11.2 us
    all_to_all x1, waiting for transfers between devices: 9.03 us -> 10.2 us  [exchange(): return lax.all_to_all(x, AXES, 0, 0, axis_index_groups=groups, tiled=True)]
where the time goes in v5:
time: 87 us; the launch traced here: 86.6 us
  blocking collectives  61 us (70%)
  waiting for transfers between devices  11.2 us (13%)
  Pallas kernels  9.37 us (11%)
  starting transfers between devices  3.6 us (4%)
    all_to_all x3, blocking collectives, exchange(): return lax.all_to_all(x, AXES, 0, 0, axis_index_groups=groups, tiled=True)  61 us
    all_to_all x1, waiting for transfers between devices, exchange(): return lax.all_to_all(x, AXES, 0, 0, axis_index_groups=groups, tiled=True)  10.2 us
    all_to_all x1, starting transfers between devices, exchange(): return lax.all_to_all(x, AXES, 0, 0, axis_index_groups=groups, tiled=True)  3.42 us
    pallas_call x1, Pallas kernels, chain(): local_call(chain_kernel, 'block_chain', out, [WHOLE] * 6)(raw, *others)  2.14 us
    pallas_call x1, Pallas kernels, load(): local_call(load_kernel, 'load_terms', jax.ShapeDtypeStruct((blocks, chips...  1.75 us
  transfers between devices with their start and end apart: 4, of which 2 were waited for; matrix products, arithmetic and copies ran while one was open for 1% of the time, Pallas kernels for 2%

profile of v5, /device:TPU:0, one launch (start us, length us, event | category | flops | bytes accessed | tf_op | source)
XLA Modules:
  0.0 86.6 jit_solution(9720715844464196764)
XLA Ops:
  0.6 1.2 %state_halves.1 = (bf16[8,32,512]{2,1,0:T(8,128)(2,1)S(1)}, bf16[8,32,512]{2,1,0:T(8,128)(2,1)S(1)}) custom-call(bf16[8,8,512]{2,1,0:T(8,128)(2,1)} %left_t.1, bf16[8,8,512]{2,1,0:T(8,128)(2,1)} %right.1, f32[8,8,512]{2,1,0:T(8,128)} %first.3, f32[8,8,512]{2,1,0:T(8,128)} %second.3), custom_call_target="tpu_custom_call" | custom-call | tf_op jit(solution)/shard_map/state_halves/pallas_call | solution.py:213
  1.8 0.1 collective-permute-start
  1.9 1.8 %load_terms.1.loaded = bf16[8,72,4,512]{3,2,1,0:T(4,128)(2,1)S(1)} custom-call(bf16[8,8,8,4,512]{4,3,2,1,0:T(4,128)(2,1)} %bitcast.25, bf16[8,64,4,512]{3,2,1,0:T(4,128)(2,1)} %bitcast.26), custom_call_target="tpu_custom_call" | custom-call | bytes 4194304 | tf_op jit(solution)/shard_map/load_terms/pallas_call | solution.py:241
  3.6 0.0 collective-permute-done.given
  3.7 0.9 %pack_states.1 = bf16[8,72,4,512]{3,2,1,0:T(4,128)(2,1)S(1)} custom-call(s32[2,8]{1,0:T(2,128)} %slot_block.3, bf16[8,72,4,512]{3,2,1,0:T(4,128)(2,1)S(1)} %load_terms.1.loaded, bf16[8,32,512]{2,1,0:T(8,128)(2,1)S(1)} %get-tuple-element.14.keep, bf16[8,32,512]{2,1,0:T(8,128)(2,1)S(1)} %collective-permute-done.given), custom_call_target="tpu_custom_call", output_to_operand_aliasing={{}: (1, {})} | custom-call | tf_op jit(solution)/shard_map/pack_states/pallas_call | solution.py:279
  4.6 26.6 %all_to_all.20.received = bf16[8,72,4,512]{3,2,1,0:T(4,128)(2,1)S(1)} all-to-all(bf16[8,72,4,512]{3,2,1,0:T(4,128)(2,1)S(1)} %pack_states.1), channel_id=1, replica_groups={{0,1,4,5,48,49,52,53},{3,2,7,6,51,50,55,54},{12,13,8,9,60,61,56,57},{15..., dimensions={0} | all-to-all | bytes 4718592 | tf_op jit(solution)/shard_map/all_to_all | solution.py:44
  31.2 0.9 relay.1
  32.0 17.0 %all_to_all.21.received = bf16[8,24,4,512]{3,2,1,0:T(4,128)(2,1)S(1)} all-to-all(bf16[8,24,4,512]{3,2,1,0:T(4,128)(2,1)S(1)} %relay.1), channel_id=1, replica_groups={{0,3,12,15,16,19,28,31},{1,2,13,14,17,18,29,30},{4,7,8,11,20,23,24,27},..., dimensions={0} | all-to-all | bytes 1572864 | tf_op jit(solution)/shard_map/all_to_all | solution.py:44
  49.0 0.9 %sum_terms.1 = (bf16[8,32,512]{2,1,0:T(8,128)(2,1)}, bf16[64,8,512]{2,1,0:T(8,128)(2,1)S(1)}) custom-call(bf16[8,24,4,512]{3,2,1,0:T(4,128)(2,1)S(1)} %all_to_all.21.received), custom_call_target="tpu_custom_call" | custom-call | tf_op jit(solution)/shard_map/sum_terms/pallas_call | solution.py:354
  49.9 0.2 copy.19
  50.1 0.1 collective-permute-start.2
  50.2 3.4 %all-to-all-start.2 = ((bf16[8,32,512]{2,1,0:T(8,128)(2,1)}), bf16[8,32,512]{2,1,0:T(8,128)(2,1)S(1)}, u32[]{:S(2)}, u32[]{:S(2)}) async-start(bf16[8,32,512]{2,1,0:T(8,128)(2,1)} %get-tuple-element.16), calls=%async_computation.2 | async-start | bytes 524288 | tf_op jit(solution)/shard_map/all_to_all | solution.py:44
  53.6 10.2 %all-to-all-done.2 = bf16[8,32,512]{2,1,0:T(8,128)(2,1)S(1)} async-done(((bf16[8,32,512]{2,1,0:T(8,128)(2,1)}), bf16[8,32,512]{2,1,0:T(8,128)(2,1)S(1)}, u32[]{:S(2)}, u32[]{:S(2)}) %all-to-all-start.2) | async-done | bytes 262176 | tf_op jit(solution)/shard_map/all_to_all | solution.py:44
  63.9 0.0 collective-permute-start.1
  63.9 0.0 collective-permute-done.2
  63.9 0.2 broadcast_select_fusion
  64.1 0.0 copy-start
  64.1 0.0 copy-start.1
  64.1 0.0 copy-start.2
  64.1 0.0 copy-start.3
  64.1 0.0 copy-start.4
  64.1 0.3 copy.26
  64.5 0.9 %collective-permute-done.1.swapped = bf16[256,512]{1,0:T(8,128)(2,1)S(1)} collective-permute-done((bf16[256,512]{1,0:T(8,128)(2,1)S(1)}, bf16[256,512]{1,0:T(8,128)(2,1)S(1)}, u32[]{:S(2)}, u32[]{:S(2)}) %collective-permute-start.1) | collective-permute-done | bytes 262176 | tf_op jit(solution)/shard_map/ppermute | solution.py:48
  65.4 2.1 %block_chain.1 = bf16[512,512]{1,0:T(8,128)(2,1)S(1)} custom-call(bf16[256,512]{1,0:T(8,128)(2,1)S(1)} %bitcast.24, bf16[256,512]{1,0:T(8,128)(2,1)S(1)} %collective-permute-done.1.swapped, bf16[512,512]{1,0:T(8,128)(2,1)S(1)} %bitcast.21, bf16[64,512]{1,0:T(8,128)(2,1)S(1)} %get-tuple-element.36.left_t, f32[64,512]{1,0:T(8,128)S(1)} %add_bitcast_fusion.first, ...), custom_call_target="tpu_custom_call" | custom-call | tf_op jit(solution)/shard_map/block_chain/pallas_call | solution.py:129
  67.5 17.5 %all_to_all.22 = bf16[64,8,512]{2,1,0:T(8,128)(2,1)S(1)} all-to-all(bf16[64,8,512]{2,1,0:T(8,128)(2,1)S(1)} %bitcast.22), channel_id=1, replica_groups={{0,3,12,15,16,19,28,31,1,2,13,14,17,18,29,30,4,7,8,11,20,23,24,27,5,6,9..., dimensions={0} | all-to-all | bytes 1048576 | tf_op jit(solution)/shard_map/all_to_all | solution.py:44
  85.0 0.0 copy-done
  85.0 0.0 copy-done.1
  85.0 0.0 copy-done.2
  85.0 0.0 copy-done.3
  85.0 0.0 copy-done.4
  85.0 1.6 %new_state.1 = (f32[8,8,512]{2,1,0:T(8,128)}, f32[8,8,512]{2,1,0:T(8,128)}, f32[8,8,512]{2,1,0:T(8,128)}, f32[8,8,512]{2,1,0:T(8,128)}, bf16[8,4,512]{2,1,0:T(4,128)(2,1)}) custom-call(s32[2,8]{1,0:T(2,128)S(1)} %copy-done.4, bf16[8,64,512]{2,1,0:T(8,128)(2,1)S(1)} %bitcast.20, f32[8,8,512]{2,1,0:T(8,128)S(1)} %copy-done.2, f32[8,8,512]{2,1,0:T(8,128)S(1)} %copy-done.3, ...), custom_call_target="tpu_custom_call" | custom-call | tf_op jit(solution)/shard_map/new_state/pallas_call | solution.py:175
  (2 shorter events, 0.0 us)
Async XLA Ops:
  1.8 1.9 %collective-permute-start = (bf16[8,32,512]{2,1,0:T(8,128)(2,1)S(1)}, bf16[8,32,512]{2,1,0:T(8,128)(2,1)S(1)}, u32[]{:S(2)}, u32[]{:S(2)}) collective-permute-start(bf16[8,32,512]{2,1,0:T(8,128)(2,1)S(1)} %get-tuple-element.15), channel_id=1, source_target_pairs={{0,64},{64,0},{1,65},{65,1},{2,66},{66,2},{3,67},{67,3},{4,68},{68... | collective-permute-start | bytes 786440 | tf_op jit(solution)/shard_map/ppermute | solution.py:48
  50.1 13.8 %collective-permute-start.2 = (bf16[64,8,512]{2,0,1:T(8,128)(2,1)S(1)}, bf16[64,8,512]{2,0,1:T(8,128)(2,1)S(1)}, u32[]{:S(2)}, u32[]{:S(2)}) collective-permute-start(bf16[64,8,512]{2,0,1:T(8,128)(2,1)S(1)} %copy.19), channel_id=1, source_target_pairs={{0,64},{64,0},{1,65},{65,1},{2,66},{66,2},{3,67},{67,3},{4,68},{68... | collective-permute-start | bytes 1572872 | tf_op jit(solution)/shard_map/ppermute | solution.py:48
  50.2 13.7 %all-to-all-start.2 = ((bf16[8,32,512]{2,1,0:T(8,128)(2,1)}), bf16[8,32,512]{2,1,0:T(8,128)(2,1)S(1)}, u32[]{:S(2)}, u32[]{:S(2)}) async-start(bf16[8,32,512]{2,1,0:T(8,128)(2,1)} %get-tuple-element.16), calls=%async_computation.2 | async-start | bytes 524288 | tf_op jit(solution)/shard_map/all_to_all | solution.py:44
  63.9 1.5 %collective-permute-start.1 = (bf16[256,512]{1,0:T(8,128)(2,1)S(1)}, bf16[256,512]{1,0:T(8,128)(2,1)S(1)}, u32[]{:S(2)}, u32[]{:S(2)}) collective-permute-start(bf16[256,512]{1,0:T(8,128)(2,1)S(1)} %bitcast.23), channel_id=1, source_target_pairs={{0,64},{64,0},{1,65},{65,1},{2,66},{66,2},{3,67},{67,3},{4,68},{68... | collective-permute-start | bytes 786440 | tf_op jit(solution)/shard_map/ppermute | solution.py:48
  64.1 21.0 %copy-start = (f32[8,8,512]{2,1,0:T(8,128)S(1)}, f32[8,8,512]{2,1,0:T(8,128)}, u32[]{:S(2)}) copy-start(f32[8,8,512]{2,1,0:T(8,128)} %first.3) | copy-start | bytes 393220
  64.1 20.9 %copy-start.1 = (f32[8,8,512]{2,1,0:T(8,128)S(1)}, f32[8,8,512]{2,1,0:T(8,128)}, u32[]{:S(2)}) copy-start(f32[8,8,512]{2,1,0:T(8,128)} %second.3) | copy-start | bytes 393220
  64.1 20.9 %copy-start.2 = (f32[8,8,512]{2,1,0:T(8,128)S(1)}, f32[8,8,512]{2,1,0:T(8,128)}, u32[]{:S(2)}) copy-start(f32[8,8,512]{2,1,0:T(8,128)} %gram_l.1) | copy-start | bytes 393220
  64.1 20.9 %copy-start.3 = (f32[8,8,512]{2,1,0:T(8,128)S(1)}, f32[8,8,512]{2,1,0:T(8,128)}, u32[]{:S(2)}) copy-start(f32[8,8,512]{2,1,0:T(8,128)} %gram_r.1) | copy-start | bytes 393220
  64.1 20.9 %copy-start.4 = (s32[2,8]{1,0:T(2,128)S(1)}, s32[2,8]{1,0:T(2,128)}, u32[]{:S(2)}) copy-start(s32[2,8]{1,0:T(2,128)} %slot_block.3) | copy-start | bytes 196

commit v6 on v4

--- a/solution.py
+++ b/solution.py
@@ -132,21 +132,26 @@
 def finish_kernel(slot_block, home, gram_l, gram_r, first, second, *refs):
     outs, built, sent = refs[:5], refs[5:10], refs[10]
     core = lax.axis_index("fsdp")
-    blocks = home.shape[0]
-    n, col = iota((32, 64), 0), iota((32, 64), 1)
-    kind, chip, row = n >> 3, col >> 3, col & 7
-    other = row - 4 * (1 - core)
-    product = (chip == (n & 7)) & ((other == kind) | ((kind == 2) & (other == 3)))
-    hit = ((kind == 3) & (row - 4 * core == (n & 7))) | ((kind < 3) & product)
-    take = one_hot(hit)
+    blocks, width = gram_l.shape[0], home.shape[1]
+    n, col = iota((24, width), 0), iota((24, width), 1)
+    other = (col & 7) - 4 * (1 - core)
+    kind = n >> 3
+    wanted = (other == kind) | ((kind == 2) & (other == 3))
+    picks = []
+    for slot in range(blocks):
+        block = jnp.maximum(slot_block[core, slot], 0)
+        picks.append(one_hot(wanted & ((col >> 3) == block * 8 + (n & 7))))
     share = jnp.where(slot_block[core, 0] >= 0, 1.0, 0.0)
+    rows = dot(jnp.concatenate(picks, axis=0), home[...]) * share
+    n, col = iota((4 * blocks, width), 0), iota((4 * blocks, width), 1)
+    sums = one_hot(((col >> 6) == (n >> 2)) & ((col & 7) - 4 * core == (n & 3)))
+    sums = dot(sums, home[...])
     copies = []
     for slot in range(blocks):
-        block = jnp.maximum(slot_block[core, slot], 0)
-        rows = dot(take, home[block]) * share
-        rotated = rows[16:24]
-        built[0][slot] = shampoo_beta * gram_l[slot] + (1.0 - shampoo_beta) * rows[:8]
-        built[1][slot] = shampoo_beta * gram_r[slot] + (1.0 - shampoo_beta) * rows[8:16]
+        mine = rows[24 * slot : 24 * slot + 24]
+        rotated = mine[16:24]
+        built[0][slot] = shampoo_beta * gram_l[slot] + (1.0 - shampoo_beta) * mine[:8]
+        built[1][slot] = shampoo_beta * gram_r[slot] + (1.0 - shampoo_beta) * mine[8:16]
         built[2][slot] = adam_first * first[slot] + (1.0 - adam_first) * rotated
         built[3][slot] = (
             adam_second * second[slot] + (1.0 - adam_second) * rotated * rotated
@@ -161,7 +166,7 @@
                 )
                 copies[-1].start()
     for b in range(blocks):
-        built[4][b] = dot(take[24:], home[b])[:4].astype(jnp.bfloat16)
+        built[4][b] = sums[4 * b : 4 * b + 4].astype(jnp.bfloat16)
     copies.append(pltpu.make_async_copy(built[4], outs[4], sent.at[4, 0]))
     copies[-1].start()
     for copy in copies:
@@ -169,7 +174,7 @@
 
 
 def finish(slot_block, home, states):
-    blocks, width = home.shape[0], home.shape[2]
+    blocks, width = states[0].shape[0], home.shape[1]
     outs = [jax.ShapeDtypeStruct(x.shape, x.dtype) for x in states]
     outs.append(jax.ShapeDtypeStruct((blocks, 4, width), jnp.bfloat16))
     return local_call(
@@ -386,7 +391,7 @@
 
     outs = finish(
         slot_block,
-        home.reshape(blocks, GROUP * 8, width),
+        home.reshape(width, width),
         (gram_left, gram_right, moment_first, moment_second),
     )
     return (*outs[:4], outs[4][:, None])

time: 84.8 us -> 84.8 us (level)
  no operation moved by 1% of the time
where the time goes in v6:
time: 84.8 us; the launch traced here: 84.4 us
  blocking collectives  60.2 us (71%)
  waiting for transfers between devices  9.69 us (11%)
  Pallas kernels  9.18 us (11%)
  starting transfers between devices  3.6 us (4%)
    all_to_all x3, blocking collectives, exchange(): return lax.all_to_all(x, AXES, 0, 0, axis_index_groups=groups, tiled=True)  60.2 us
    all_to_all x1, waiting for transfers between devices, exchange(): return lax.all_to_all(x, AXES, 0, 0, axis_index_groups=groups, tiled=True)  9.03 us
    all_to_all x1, starting transfers between devices, exchange(): return lax.all_to_all(x, AXES, 0, 0, axis_index_groups=groups, tiled=True)  3.42 us
    pallas_call x1, Pallas kernels, chain(): local_call(chain_kernel, 'block_chain', out, [WHOLE] * 6)(raw, *others)  2.14 us
  transfers between devices with their start and end apart: 4, of which 2 were waited for; matrix products, arithmetic and copies ran while one was open for 1% of the time, Pallas kernels for 2%

profile of v6, /device:TPU:0, one launch (start us, length us, event | category | flops | bytes accessed | tf_op | source)
XLA Modules:
  0.0 84.4 jit_solution(6898091486241355348)
XLA Ops:
  0.6 1.2 %state_halves.1 = (bf16[8,32,512]{2,1,0:T(8,128)(2,1)S(1)}, bf16[8,32,512]{2,1,0:T(8,128)(2,1)S(1)}) custom-call(bf16[8,8,512]{2,1,0:T(8,128)(2,1)} %left_t.1, bf16[8,8,512]{2,1,0:T(8,128)(2,1)} %right.1, f32[8,8,512]{2,1,0:T(8,128)} %first.3, f32[8,8,512]{2,1,0:T(8,128)} %second.3), custom_call_target="tpu_custom_call" | custom-call | tf_op jit(solution)/shard_map/state_halves/pallas_call | solution.py:218
  1.8 0.1 collective-permute-start
  1.9 1.6 %load_terms.1.loaded = bf16[8,72,4,512]{3,2,1,0:T(4,128)(2,1)S(1)} custom-call(bf16[8,8,8,4,512]{4,3,2,1,0:T(4,128)(2,1)} %bitcast.23, bf16[8,64,4,512]{3,2,1,0:T(4,128)(2,1)} %bitcast.24), custom_call_target="tpu_custom_call" | custom-call | bytes 4194304 | tf_op jit(solution)/shard_map/load_terms/pallas_call | solution.py:245
  3.5 0.0 collective-permute-done.given
  3.5 0.9 %pack_states.1 = bf16[8,72,4,512]{3,2,1,0:T(4,128)(2,1)S(1)} custom-call(s32[2,8]{1,0:T(2,128)} %slot_block.3, bf16[8,72,4,512]{3,2,1,0:T(4,128)(2,1)S(1)} %load_terms.1.loaded, bf16[8,32,512]{2,1,0:T(8,128)(2,1)S(1)} %get-tuple-element.14.keep, bf16[8,32,512]{2,1,0:T(8,128)(2,1)S(1)} %collective-permute-done.given), custom_call_target="tpu_custom_call", output_to_operand_aliasing={{}: (1, {})} | custom-call | tf_op jit(solution)/shard_map/pack_states/pallas_call | solution.py:283
  4.4 28.3 %all_to_all.20.received = bf16[8,72,4,512]{3,2,1,0:T(4,128)(2,1)S(1)} all-to-all(bf16[8,72,4,512]{3,2,1,0:T(4,128)(2,1)S(1)} %pack_states.1), channel_id=1, replica_groups={{0,3,12,15,16,19,28,31},{1,2,13,14,17,18,29,30},{4,7,8,11,20,23,24,27},..., dimensions={0} | all-to-all | bytes 4718592 | tf_op jit(solution)/shard_map/all_to_all | solution.py:44
  32.8 0.9 %relay.1 = bf16[8,24,4,512]{3,2,1,0:T(4,128)(2,1)S(1)} custom-call(bf16[8,72,4,512]{3,2,1,0:T(4,128)(2,1)S(1)} %all_to_all.20.received), custom_call_target="tpu_custom_call" | custom-call | tf_op jit(solution)/shard_map/relay/pallas_call | solution.py:323
  33.6 14.7 %all_to_all.21.received = bf16[8,24,4,512]{3,2,1,0:T(4,128)(2,1)S(1)} all-to-all(bf16[8,24,4,512]{3,2,1,0:T(4,128)(2,1)S(1)} %relay.1), channel_id=1, replica_groups={{0,1,4,5,48,49,52,53},{3,2,7,6,51,50,55,54},{12,13,8,9,60,61,56,57},{15..., dimensions={0} | all-to-all | bytes 1572864 | tf_op jit(solution)/shard_map/all_to_all | solution.py:44
  48.4 0.8 sum_terms.1
  49.2 0.2 copy.19
  49.4 0.1 collective-permute-start.2
  49.5 3.4 %all-to-all-start.2 = ((bf16[8,32,512]{2,1,0:T(8,128)(2,1)}), bf16[8,32,512]{2,1,0:T(8,128)(2,1)S(1)}, u32[]{:S(2)}, u32[]{:S(2)}) async-start(bf16[8,32,512]{2,1,0:T(8,128)(2,1)} %get-tuple-element.16), calls=%async_computation.2 | async-start | bytes 524288 | tf_op jit(solution)/shard_map/all_to_all | solution.py:44
  52.9 9.0 %all-to-all-done.2 = bf16[8,32,512]{2,1,0:T(8,128)(2,1)S(1)} async-done(((bf16[8,32,512]{2,1,0:T(8,128)(2,1)}), bf16[8,32,512]{2,1,0:T(8,128)(2,1)S(1)}, u32[]{:S(2)}, u32[]{:S(2)}) %all-to-all-start.2) | async-done | bytes 262176 | tf_op jit(solution)/shard_map/all_to_all | solution.py:44
  61.9 0.0 collective-permute-start.1
  61.9 0.0 collective-permute-done.2
  62.0 0.2 broadcast_select_fusion
  62.2 0.4 copy.20
  62.6 0.0 copy-start
  62.6 0.0 copy-start.1
  62.6 0.0 copy-start.2
  62.6 0.0 copy-start.3
  62.7 0.0 copy-start.4
  62.7 0.1 reshape.28.right
  62.8 0.7 collective-permute-done.1.swapped
  63.5 2.1 %block_chain.1 = bf16[512,512]{1,0:T(8,128)(2,1)S(1)} custom-call(bf16[256,512]{1,0:T(8,128)(2,1)S(1)} %bitcast.22, bf16[256,512]{1,0:T(8,128)(2,1)S(1)} %collective-permute-done.1.swapped, bf16[512,512]{1,0:T(8,128)(2,1)S(1)} %reshape.28.right, bf16[64,512]{1,0:T(8,128)(2,1)S(1)} %get-tuple-element.34.left_t, f32[64,512]{1,0:T(8,128)S(1)} %add_bitcast_fusion.first, ...), custom_call_target="tpu_custom_call" | custom-call | tf_op jit(solution)/shard_map/block_chain/pallas_call | solution.py:129
  65.6 17.1 %all_to_all.22 = bf16[64,8,512]{2,1,0:T(8,128)(2,1)S(1)} all-to-all(bf16[64,8,512]{2,1,0:T(8,128)(2,1)S(1)} %bitcast.20), channel_id=1, replica_groups={{0,1,4,5,48,49,52,53,3,2,7,6,51,50,55,54,12,13,8,9,60,61,56,57,15,14,11..., dimensions={0} | all-to-all | bytes 1048576 | tf_op jit(solution)/shard_map/all_to_all | solution.py:44
  82.7 0.0 copy-done
  82.7 0.0 copy-done.1
  82.7 0.0 copy-done.2
  82.7 0.0 copy-done.3
  82.7 0.0 copy-done.4
  82.7 1.7 %new_state.1 = (f32[8,8,512]{2,1,0:T(8,128)}, f32[8,8,512]{2,1,0:T(8,128)}, f32[8,8,512]{2,1,0:T(8,128)}, f32[8,8,512]{2,1,0:T(8,128)}, bf16[8,4,512]{2,1,0:T(4,128)(2,1)}) custom-call(s32[2,8]{1,0:T(2,128)S(1)} %copy-done.4, bf16[512,512]{1,0:T(8,128)(2,1)S(1)} %bitcast.19, f32[8,8,512]{2,1,0:T(8,128)S(1)} %copy-done.2, f32[8,8,512]{2,1,0:T(8,128)S(1)} %copy-done.3, ...), custom_call_target="tpu_custom_call" | custom-call | tf_op jit(solution)/shard_map/new_state/pallas_call | solution.py:180
  (3 shorter events, 0.1 us)
Async XLA Ops:
  1.8 1.7 %collective-permute-start = (bf16[8,32,512]{2,1,0:T(8,128)(2,1)S(1)}, bf16[8,32,512]{2,1,0:T(8,128)(2,1)S(1)}, u32[]{:S(2)}, u32[]{:S(2)}) collective-permute-start(bf16[8,32,512]{2,1,0:T(8,128)(2,1)S(1)} %get-tuple-element.15), channel_id=1, source_target_pairs={{0,64},{64,0},{1,65},{65,1},{2,66},{66,2},{3,67},{67,3},{4,68},{68... | collective-permute-start | bytes 786440 | tf_op jit(solution)/shard_map/ppermute | solution.py:48
  49.4 12.6 %collective-permute-start.2 = (bf16[64,2,4,512]{3,0,2,1:T(8,128)(2,1)S(1)}, bf16[64,2,4,512]{3,0,2,1:T(8,128)(2,1)S(1)}, u32[]{:S(2)}, u32[]{:S(2)}) collective-permute-start(bf16[64,2,4,512]{3,0,2,1:T(8,128)(2,1)S(1)} %copy.19), channel_id=1, source_target_pairs={{0,64},{64,0},{1,65},{65,1},{2,66},{66,2},{3,67},{67,3},{4,68},{68... | collective-permute-start | bytes 1572872 | tf_op jit(solution)/shard_map/ppermute | solution.py:48
  49.5 12.5 %all-to-all-start.2 = ((bf16[8,32,512]{2,1,0:T(8,128)(2,1)}), bf16[8,32,512]{2,1,0:T(8,128)(2,1)S(1)}, u32[]{:S(2)}, u32[]{:S(2)}) async-start(bf16[8,32,512]{2,1,0:T(8,128)(2,1)} %get-tuple-element.16), calls=%async_computation.2 | async-start | bytes 524288 | tf_op jit(solution)/shard_map/all_to_all | solution.py:44
  61.9 1.5 %collective-permute-start.1 = (bf16[256,512]{1,0:T(8,128)(2,1)S(1)}, bf16[256,512]{1,0:T(8,128)(2,1)S(1)}, u32[]{:S(2)}, u32[]{:S(2)}) collective-permute-start(bf16[256,512]{1,0:T(8,128)(2,1)S(1)} %bitcast.21), channel_id=1, source_target_pairs={{0,64},{64,0},{1,65},{65,1},{2,66},{66,2},{3,67},{67,3},{4,68},{68... | collective-permute-start | bytes 786440 | tf_op jit(solution)/shard_map/ppermute | solution.py:48
  62.6 20.1 %copy-start = (f32[8,8,512]{2,1,0:T(8,128)S(1)}, f32[8,8,512]{2,1,0:T(8,128)}, u32[]{:S(2)}) copy-start(f32[8,8,512]{2,1,0:T(8,128)} %first.3) | copy-start | bytes 393220
  62.6 20.1 %copy-start.1 = (f32[8,8,512]{2,1,0:T(8,128)S(1)}, f32[8,8,512]{2,1,0:T(8,128)}, u32[]{:S(2)}) copy-start(f32[8,8,512]{2,1,0:T(8,128)} %second.3) | copy-start | bytes 393220
  62.6 20.1 %copy-start.2 = (f32[8,8,512]{2,1,0:T(8,128)S(1)}, f32[8,8,512]{2,1,0:T(8,128)}, u32[]{:S(2)}) copy-start(f32[8,8,512]{2,1,0:T(8,128)} %gram_l.1) | copy-start | bytes 393220
  62.6 20.1 %copy-start.3 = (f32[8,8,512]{2,1,0:T(8,128)S(1)}, f32[8,8,512]{2,1,0:T(8,128)}, u32[]{:S(2)}) copy-start(f32[8,8,512]{2,1,0:T(8,128)} %gram_r.1) | copy-start | bytes 393220
  62.7 20.1 %copy-start.4 = (s32[2,8]{1,0:T(2,128)S(1)}, s32[2,8]{1,0:T(2,128)}, u32[]{:S(2)}) copy-start(s32[2,8]{1,0:T(2,128)} %slot_block.3) | copy-start | bytes 196

commit v7 on v4

--- a/solution.py
+++ b/solution.py
@@ -18,9 +18,8 @@
     b = g = 0
     for axis in range(3):
         place = (dp >> (2 * axis)) & 3
-        wrap, inner = place >> 1, (place ^ (place >> 1)) & 1
-        b += (inner if axis == 2 else wrap) << axis
-        g += (wrap if axis == 2 else inner) << axis
+        b += (place >> 1) << axis
+        g += ((place ^ (place >> 1)) & 1) << axis
     return b, g
 
 

time: 84.8 us -> 84.7 us (level)
  waiting for transfers between devices: 9.69 us -> 8.48 us
  blocking collectives: 60.2 us -> 61.4 us
    all_to_all x1, waiting for transfers between devices: 9.03 us -> 7.82 us  [exchange(): return lax.all_to_all(x, AXES, 0, 0, axis_index_groups=groups, tiled=True)]
    all_to_all x3, blocking collectives: 60.2 us -> 61.4 us  [exchange(): return lax.all_to_all(x, AXES, 0, 0, axis_index_groups=groups, tiled=True)]
where the time goes in v7:
time: 84.7 us; the launch traced here: 84.4 us
  blocking collectives  61.4 us (72%)
  Pallas kernels  9.12 us (11%)
  waiting for transfers between devices  8.48 us (10%)
  starting transfers between devices  3.6 us (4%)
    all_to_all x3, blocking collectives, exchange(): return lax.all_to_all(x, AXES, 0, 0, axis_index_groups=groups, tiled=True)  61.4 us
    all_to_all x1, waiting for transfers between devices, exchange(): return lax.all_to_all(x, AXES, 0, 0, axis_index_groups=groups, tiled=True)  7.82 us
    all_to_all x1, starting transfers between devices, exchange(): return lax.all_to_all(x, AXES, 0, 0, axis_index_groups=groups, tiled=True)  3.42 us
    pallas_call x1, Pallas kernels, chain(): local_call(chain_kernel, 'block_chain', out, [WHOLE] * 6)(raw, *others)  2.14 us
  transfers between devices with their start and end apart: 4, of which 2 were waited for; matrix products, arithmetic and copies ran while one was open for 1% of the time, Pallas kernels for 2%

profile of v7, /device:TPU:0, one launch (start us, length us, event | category | flops | bytes accessed | tf_op | source)
XLA Modules:
  0.0 84.4 jit_solution(4157493483446189644)
XLA Ops:
  0.6 1.2 %state_halves.1 = (bf16[8,32,512]{2,1,0:T(8,128)(2,1)S(1)}, bf16[8,32,512]{2,1,0:T(8,128)(2,1)S(1)}) custom-call(bf16[8,8,512]{2,1,0:T(8,128)(2,1)} %left_t.1, bf16[8,8,512]{2,1,0:T(8,128)(2,1)} %right.1, f32[8,8,512]{2,1,0:T(8,128)} %first.3, f32[8,8,512]{2,1,0:T(8,128)} %second.3), custom_call_target="tpu_custom_call" | custom-call | tf_op jit(solution)/shard_map/state_halves/pallas_call | solution.py:212
  1.8 0.1 collective-permute-start
  1.9 1.6 %load_terms.1.loaded = bf16[8,72,4,512]{3,2,1,0:T(4,128)(2,1)S(1)} custom-call(bf16[8,8,8,4,512]{4,3,2,1,0:T(4,128)(2,1)} %bitcast.23, bf16[8,64,4,512]{3,2,1,0:T(4,128)(2,1)} %bitcast.24), custom_call_target="tpu_custom_call" | custom-call | bytes 4194304 | tf_op jit(solution)/shard_map/load_terms/pallas_call | solution.py:239
  3.5 0.0 collective-permute-done.given
  3.5 0.9 %pack_states.1 = bf16[8,72,4,512]{3,2,1,0:T(4,128)(2,1)S(1)} custom-call(s32[2,8]{1,0:T(2,128)} %slot_block.3, bf16[8,72,4,512]{3,2,1,0:T(4,128)(2,1)S(1)} %load_terms.1.loaded, bf16[8,32,512]{2,1,0:T(8,128)(2,1)S(1)} %get-tuple-element.14.keep, bf16[8,32,512]{2,1,0:T(8,128)(2,1)S(1)} %collective-permute-done.given), custom_call_target="tpu_custom_call", output_to_operand_aliasing={{}: (1, {})} | custom-call | tf_op jit(solution)/shard_map/pack_states/pallas_call | solution.py:277
  4.4 31.7 %all_to_all.20.received = bf16[8,72,4,512]{3,2,1,0:T(4,128)(2,1)S(1)} all-to-all(bf16[8,72,4,512]{3,2,1,0:T(4,128)(2,1)S(1)} %pack_states.1), channel_id=1, replica_groups={{0,3,12,15,48,51,60,63},{1,2,13,14,49,50,61,62},{4,7,8,11,52,55,56,59},..., dimensions={0} | all-to-all | bytes 4718592 | tf_op jit(solution)/shard_map/all_to_all | solution.py:43
  36.1 0.9 %relay.1 = bf16[8,24,4,512]{3,2,1,0:T(4,128)(2,1)S(1)} custom-call(bf16[8,72,4,512]{3,2,1,0:T(4,128)(2,1)S(1)} %all_to_all.20.received), custom_call_target="tpu_custom_call" | custom-call | tf_op jit(solution)/shard_map/relay/pallas_call | solution.py:317
  37.0 12.2 %all_to_all.21.received = bf16[8,24,4,512]{3,2,1,0:T(4,128)(2,1)S(1)} all-to-all(bf16[8,24,4,512]{3,2,1,0:T(4,128)(2,1)S(1)} %relay.1), channel_id=1, replica_groups={{0,1,4,5,16,17,20,21},{3,2,7,6,19,18,23,22},{12,13,8,9,28,29,24,25},{15..., dimensions={0} | all-to-all | bytes 1572864 | tf_op jit(solution)/shard_map/all_to_all | solution.py:43
  49.2 0.8 sum_terms.1
  50.0 0.2 copy.19
  50.2 0.1 collective-permute-start.2
  50.3 3.4 %all-to-all-start.2 = ((bf16[8,32,512]{2,1,0:T(8,128)(2,1)}), bf16[8,32,512]{2,1,0:T(8,128)(2,1)S(1)}, u32[]{:S(2)}, u32[]{:S(2)}) async-start(bf16[8,32,512]{2,1,0:T(8,128)(2,1)} %get-tuple-element.16), calls=%async_computation.2 | async-start | bytes 524288 | tf_op jit(solution)/shard_map/all_to_all | solution.py:43
  53.7 7.8 %all-to-all-done.2 = bf16[8,32,512]{2,1,0:T(8,128)(2,1)S(1)} async-done(((bf16[8,32,512]{2,1,0:T(8,128)(2,1)}), bf16[8,32,512]{2,1,0:T(8,128)(2,1)S(1)}, u32[]{:S(2)}, u32[]{:S(2)}) %all-to-all-start.2) | async-done | bytes 262176 | tf_op jit(solution)/shard_map/all_to_all | solution.py:43
  61.5 0.0 collective-permute-start.1
  61.5 0.0 collective-permute-done.2
  61.6 0.2 broadcast_select_fusion
  61.8 0.4 copy.20
  62.2 0.0 copy-start
  62.2 0.0 copy-start.1
  62.2 0.0 copy-start.2
  62.2 0.0 copy-start.3
  62.2 0.0 copy-start.4
  62.2 0.1 reshape.28.right
  62.4 0.7 collective-permute-done.1.swapped
  63.1 2.1 %block_chain.1 = bf16[512,512]{1,0:T(8,128)(2,1)S(1)} custom-call(bf16[256,512]{1,0:T(8,128)(2,1)S(1)} %bitcast.22, bf16[256,512]{1,0:T(8,128)(2,1)S(1)} %collective-permute-done.1.swapped, bf16[512,512]{1,0:T(8,128)(2,1)S(1)} %reshape.28.right, bf16[64,512]{1,0:T(8,128)(2,1)S(1)} %get-tuple-element.34.left_t, f32[64,512]{1,0:T(8,128)S(1)} %add_bitcast_fusion.first, ...), custom_call_target="tpu_custom_call" | custom-call | tf_op jit(solution)/shard_map/block_chain/pallas_call | solution.py:128
  65.2 17.5 %all_to_all.22 = bf16[64,8,512]{2,1,0:T(8,128)(2,1)S(1)} all-to-all(bf16[64,8,512]{2,1,0:T(8,128)(2,1)S(1)} %bitcast.20), channel_id=1, replica_groups={{0,1,4,5,16,17,20,21,3,2,7,6,19,18,23,22,12,13,8,9,28,29,24,25,15,14,11..., dimensions={0} | all-to-all | bytes 1048576 | tf_op jit(solution)/shard_map/all_to_all | solution.py:43
  82.7 0.0 copy-done
  82.7 0.0 copy-done.1
  82.7 0.0 copy-done.2
  82.7 0.0 copy-done.3
  82.7 0.0 copy-done.4
  82.7 1.6 %new_state.1 = (f32[8,8,512]{2,1,0:T(8,128)}, f32[8,8,512]{2,1,0:T(8,128)}, f32[8,8,512]{2,1,0:T(8,128)}, f32[8,8,512]{2,1,0:T(8,128)}, bf16[8,4,512]{2,1,0:T(4,128)(2,1)}) custom-call(s32[2,8]{1,0:T(2,128)S(1)} %copy-done.4, bf16[8,64,512]{2,1,0:T(8,128)(2,1)S(1)} %bitcast.19, f32[8,8,512]{2,1,0:T(8,128)S(1)} %copy-done.2, f32[8,8,512]{2,1,0:T(8,128)S(1)} %copy-done.3, ...), custom_call_target="tpu_custom_call" | custom-call | tf_op jit(solution)/shard_map/new_state/pallas_call | solution.py:174
  (3 shorter events, 0.1 us)
Async XLA Ops:
  1.8 1.7 %collective-permute-start = (bf16[8,32,512]{2,1,0:T(8,128)(2,1)S(1)}, bf16[8,32,512]{2,1,0:T(8,128)(2,1)S(1)}, u32[]{:S(2)}, u32[]{:S(2)}) collective-permute-start(bf16[8,32,512]{2,1,0:T(8,128)(2,1)S(1)} %get-tuple-element.15), channel_id=1, source_target_pairs={{0,64},{64,0},{1,65},{65,1},{2,66},{66,2},{3,67},{67,3},{4,68},{68... | collective-permute-start | bytes 786440 | tf_op jit(solution)/shard_map/ppermute | solution.py:47
  50.2 11.4 %collective-permute-start.2 = (bf16[64,2,4,512]{3,0,2,1:T(8,128)(2,1)S(1)}, bf16[64,2,4,512]{3,0,2,1:T(8,128)(2,1)S(1)}, u32[]{:S(2)}, u32[]{:S(2)}) collective-permute-start(bf16[64,2,4,512]{3,0,2,1:T(8,128)(2,1)S(1)} %copy.19), channel_id=1, source_target_pairs={{0,64},{64,0},{1,65},{65,1},{2,66},{66,2},{3,67},{67,3},{4,68},{68... | collective-permute-start | bytes 1572872 | tf_op jit(solution)/shard_map/ppermute | solution.py:47
  50.3 11.3 %all-to-all-start.2 = ((bf16[8,32,512]{2,1,0:T(8,128)(2,1)}), bf16[8,32,512]{2,1,0:T(8,128)(2,1)S(1)}, u32[]{:S(2)}, u32[]{:S(2)}) async-start(bf16[8,32,512]{2,1,0:T(8,128)(2,1)} %get-tuple-element.16), calls=%async_computation.2 | async-start | bytes 524288 | tf_op jit(solution)/shard_map/all_to_all | solution.py:43
  61.5 1.5 %collective-permute-start.1 = (bf16[256,512]{1,0:T(8,128)(2,1)S(1)}, bf16[256,512]{1,0:T(8,128)(2,1)S(1)}, u32[]{:S(2)}, u32[]{:S(2)}) collective-permute-start(bf16[256,512]{1,0:T(8,128)(2,1)S(1)} %bitcast.21), channel_id=1, source_target_pairs={{0,64},{64,0},{1,65},{65,1},{2,66},{66,2},{3,67},{67,3},{4,68},{68... | collective-permute-start | bytes 786440 | tf_op jit(solution)/shard_map/ppermute | solution.py:47
  62.2 20.5 %copy-start = (f32[8,8,512]{2,1,0:T(8,128)S(1)}, f32[8,8,512]{2,1,0:T(8,128)}, u32[]{:S(2)}) copy-start(f32[8,8,512]{2,1,0:T(8,128)} %first.3) | copy-start | bytes 393220
  62.2 20.5 %copy-start.1 = (f32[8,8,512]{2,1,0:T(8,128)S(1)}, f32[8,8,512]{2,1,0:T(8,128)}, u32[]{:S(2)}) copy-start(f32[8,8,512]{2,1,0:T(8,128)} %second.3) | copy-start | bytes 393220
  62.2 20.5 %copy-start.2 = (f32[8,8,512]{2,1,0:T(8,128)S(1)}, f32[8,8,512]{2,1,0:T(8,128)}, u32[]{:S(2)}) copy-start(f32[8,8,512]{2,1,0:T(8,128)} %gram_l.1) | copy-start | bytes 393220
  62.2 20.5 %copy-start.3 = (f32[8,8,512]{2,1,0:T(8,128)S(1)}, f32[8,8,512]{2,1,0:T(8,128)}, u32[]{:S(2)}) copy-start(f32[8,8,512]{2,1,0:T(8,128)} %gram_r.1) | copy-start | bytes 393220
  62.2 20.5 %copy-start.4 = (s32[2,8]{1,0:T(2,128)S(1)}, s32[2,8]{1,0:T(2,128)}, u32[]{:S(2)}) copy-start(s32[2,8]{1,0:T(2,128)} %slot_block.3) | copy-start | bytes 196

commit v8 on v4

--- a/solution.py
+++ b/solution.py
@@ -188,63 +188,91 @@
     pl.when(core != 0)(one)
 
 
-def halves_kernel(left_t, right, first, second, keep, give, *scratch):
-    held, done = scratch[:4], scratch[4]
+EARLY = 3
+
+
+def term_copies(terms, by_block, out, done, which):
+    chips, span = terms.shape[1:3]
+    near = [
+        pltpu.make_async_copy(by_block.at[b], out.at[b, pl.ds(0, chips * span)], done.at[b])
+        for b in which
+    ]
+    cross = [
+        pltpu.make_async_copy(terms.at[b], out.at[:, pl.ds(b * span, span)], done.at[b])
+        for b in which
+    ]
+    return list(zip(near, cross))
+
+
+def fill_half(out, held, whole):
+    left_t, right, first, second = held
+    for slot in range(out.shape[0]):
+        rows = [part[slot].astype(jnp.float32) for part in (left_t, right, first, second)]
+        upper = rows[2].astype(jnp.bfloat16).astype(jnp.float32)
+        singles = jnp.concatenate([rows[0], upper, rows[2] - upper, rows[3]], axis=0)
+        right_rows = jnp.concatenate([rows[1]] * 4, axis=0)
+        out[slot] = jnp.where(whole, right_rows, singles).astype(jnp.bfloat16)
+
+
+def fetch(states, held, done):
     copies = [
         pltpu.make_async_copy(source, to, done.at[i])
-        for i, (source, to) in enumerate(zip((left_t, right, first, second), held))
+        for i, (source, to) in enumerate(zip(states, held))
     ]
     for copy in copies:
         copy.start()
+    return copies
+
+
+def start_kernel(terms, by_block, *refs):
+    states, out, give, held, done, landed = refs[:4], refs[4], refs[5], refs[6:10], refs[10], refs[11]
+    copies = fetch(states, held, landed)
+    early = term_copies(terms, by_block, out, done, range(EARLY))
+    for near, cross in early:
+        on_core(near.start, cross.start)
     for copy in copies:
         copy.wait()
-    core = lax.axis_index("fsdp")
-    for slot in range(keep.shape[0]):
-        left_rows, right_rows, one, two = (part[slot].astype(jnp.float32) for part in held)
-        upper = one.astype(jnp.bfloat16).astype(jnp.float32)
-        whole = jnp.concatenate([right_rows] * 4, axis=0)
-        singles = jnp.concatenate([left_rows, upper, one - upper, two], axis=0)
-        keep[slot] = jnp.where(core == 0, whole, singles).astype(jnp.bfloat16)
-        give[slot] = jnp.where(core == 0, singles, whole).astype(jnp.bfloat16)
-
-
-def halves(*states):
-    blocks, rows, width = states[0].shape
-    return local_call(
-        halves_kernel,
-        "state_halves",
-        [jax.ShapeDtypeStruct((blocks, 4 * rows, width), jnp.bfloat16)] * 2,
-        [FAR] * 4,
-        [pltpu.VMEM(x.shape, x.dtype) for x in states] + [pltpu.SemaphoreType.DMA((4,))],
-    )(*states)
-
-
-def load_kernel(terms, by_block, out, done):
-    blocks, chips, span = terms.shape[:3]
-    near = [
-        pltpu.make_async_copy(by_block.at[b], out.at[b, pl.ds(0, chips * span)], done.at[b])
-        for b in range(blocks)
+    fill_half(give, held, lax.axis_index("fsdp") == 1)
+    for near, cross in early:
+        on_core(near.wait, cross.wait)
+
+
+def load_kernel(loaded, terms, by_block, *refs):
+    states, out, keep, held, done, landed = refs[:4], refs[4], refs[5], refs[6:10], refs[10], refs[11]
+    copies = fetch(states, held, landed)
+    late = term_copies(terms, by_block, out, done, range(EARLY, terms.shape[0]))
+    for near, cross in late:
+        on_core(near.start, cross.start)
+    for copy in copies:
+        copy.wait()
+    fill_half(keep, held, lax.axis_index("fsdp") == 0)
+    for near, cross in late:
+        on_core(near.wait, cross.wait)
+
+
+def prepare(terms, states):
+    blocks, chips, span, rows, width = terms.shape
+    sources = [in_hbm(terms), in_hbm(terms.reshape(blocks, chips * span, rows, width))]
+    sources += map(in_hbm, states)
+    shape = (blocks, chips * span + GROUP, rows, width)
+    outs = [
+        jax.ShapeDtypeStruct(shape, terms.dtype),
+        jax.ShapeDtypeStruct((blocks, 4 * states[0].shape[1], width), jnp.bfloat16),
     ]
-    cross = [
-        pltpu.make_async_copy(terms.at[b], out.at[:, pl.ds(b * span, span)], done.at[b])
-        for b in range(blocks)
-    ]
-    for b in range(blocks):
-        on_core(near[b].start, cross[b].start)
-    for b in range(blocks):
-        on_core(near[b].wait, cross[b].wait)
-
-
-def load(terms):
-    blocks, chips, span, rows, width = terms.shape
-    return local_call(
+    scratch = [pltpu.VMEM(x.shape, x.dtype) for x in states]
+    scratch += [pltpu.SemaphoreType.DMA((blocks,)), pltpu.SemaphoreType.DMA((4,))]
+    loaded, give = local_call(start_kernel, "start_terms", outs, [FAR] * 6, scratch)(*sources)
+    given = swap_cores(give)
+    loaded, keep = local_call(
         load_kernel,
         "load_terms",
-        jax.ShapeDtypeStruct((blocks, chips * span + GROUP, rows, width), terms.dtype),
-        [FAR] * 2,
-        [pltpu.SemaphoreType.DMA((blocks,))],
+        outs,
+        [WHOLE] + [FAR] * 6,
+        scratch,
+        input_output_aliases={0: 0},
         cost_estimate=pl.CostEstimate(flops=0, bytes_accessed=2 * terms.nbytes, transcendentals=0),
-    )(in_hbm(terms), in_hbm(terms.reshape(blocks, chips * span, rows, width)))
+    )(loaded, *sources)
+    return loaded, keep, given
 
 
 def pack_kernel(slot_block, loaded, keep, given, out):
@@ -366,10 +394,8 @@
     core = lax.axis_index("fsdp")
 
     states = (left_basis_t, right_basis, moment_first, moment_second)
-    states = tuple(in_hbm(part) for part in states)
     terms = grad_parts[0].reshape(blocks, GROUP, q_total // GROUP, half_span, width)
-    keep, give = halves(*states)
-    message = pack(in_hbm(slot_block), load(terms), keep, swap_cores(give))
+    message = pack(in_hbm(slot_block), *prepare(terms, states))
     received = exchange(relay(exchange(message, FIRST)), SECOND)
     raw, half = sum_terms(received)
     raw = exchange(raw, BLOCK).reshape(-1, width)

time: 84.8 us -> 85 us (level)
  no operation moved by 1% of the time
where the time goes in v8:
time: 85 us; the launch traced here: 84.6 us
  blocking collectives  60.2 us (71%)
  waiting for transfers between devices  9.69 us (11%)
  Pallas kernels  9.4 us (11%)
  starting transfers between devices  3.6 us (4%)
    all_to_all x3, blocking collectives, exchange(): return lax.all_to_all(x, AXES, 0, 0, axis_index_groups=groups, tiled=True)  60.2 us
    all_to_all x1, waiting for transfers between devices, exchange(): return lax.all_to_all(x, AXES, 0, 0, axis_index_groups=groups, tiled=True)  9.03 us
    all_to_all x1, starting transfers between devices, exchange(): return lax.all_to_all(x, AXES, 0, 0, axis_index_groups=groups, tiled=True)  3.42 us
    pallas_call x1, Pallas kernels, chain(): local_call(chain_kernel, 'block_chain', out, [WHOLE] * 6)(raw, *others)  2.15 us
  transfers between devices with their start and end apart: 4, of which 2 were waited for; matrix products, arithmetic and copies ran while one was open for 1% of the time, Pallas kernels for 2%

profile of v8, /device:TPU:0, one launch (start us, length us, event | category | flops | bytes accessed | tf_op | source)
XLA Modules:
  0.0 84.6 jit_solution(6714622168502296988)
XLA Ops:
  0.6 1.5 %start_terms.1 = (bf16[8,72,4,512]{3,2,1,0:T(4,128)(2,1)S(1)}, bf16[8,32,512]{2,1,0:T(8,128)(2,1)S(1)}) custom-call(bf16[8,8,8,4,512]{4,3,2,1,0:T(4,128)(2,1)} %bitcast.23, bf16[8,64,4,512]{3,2,1,0:T(4,128)(2,1)} %bitcast.24, bf16[8,8,512]{2,1,0:T(8,128)(2,1)} %refs_0_.3, bf16[8,8,512]{2,1,0:T(8,128)(2,1)} %refs_1_.3, f32[8,8,512]{2,1,0:T(8,128)} %first.1, ...), custom_call_target="tpu_custom_call" | custom-call | tf_op jit(solution)/shard_map/start_terms/pallas_call | solution.py:264
  2.1 0.1 collective-permute-start
  2.2 1.6 %load_terms.1 = (bf16[8,72,4,512]{3,2,1,0:T(4,128)(2,1)S(1)}, bf16[8,32,512]{2,1,0:T(8,128)(2,1)S(1)}) custom-call(bf16[8,72,4,512]{3,2,1,0:T(4,128)(2,1)S(1)} %get-tuple-element.16.loaded, bf16[8,8,8,4,512]{4,3,2,1,0:T(4,128)(2,1)} %bitcast.25, bf16[8,64,4,512]{3,2,1,0:T(4,128)(2,1)} %bitcast.26, ...), custom_call_target="tpu_custom_call", output_to_operand_aliasing={{0}: (0, {})} | custom-call | bytes 4194304 | tf_op jit(solution)/shard_map/load_terms/pallas_call | solution.py:266
  3.7 0.0 collective-permute-done.given
  3.8 0.9 %pack_states.1 = bf16[8,72,4,512]{3,2,1,0:T(4,128)(2,1)S(1)} custom-call(s32[2,8]{1,0:T(2,128)} %slot_block.3, bf16[8,72,4,512]{3,2,1,0:T(4,128)(2,1)S(1)} %get-tuple-element.17.loaded, bf16[8,32,512]{2,1,0:T(8,128)(2,1)S(1)} %get-tuple-element.18.keep, bf16[8,32,512]{2,1,0:T(8,128)(2,1)S(1)} %collective-permute-done.given), custom_call_target="tpu_custom_call", output_to_operand_aliasing={{}: (1, {})} | custom-call | tf_op jit(solution)/shard_map/pack_states/pallas_call | solution.py:306
  4.7 28.3 %all_to_all.20.received = bf16[8,72,4,512]{3,2,1,0:T(4,128)(2,1)S(1)} all-to-all(bf16[8,72,4,512]{3,2,1,0:T(4,128)(2,1)S(1)} %pack_states.1), channel_id=1, replica_groups={{0,3,12,15,16,19,28,31},{1,2,13,14,17,18,29,30},{4,7,8,11,20,23,24,27},..., dimensions={0} | all-to-all | bytes 4718592 | tf_op jit(solution)/shard_map/all_to_all | solution.py:44
  33.0 0.9 %relay.1 = bf16[8,24,4,512]{3,2,1,0:T(4,128)(2,1)S(1)} custom-call(bf16[8,72,4,512]{3,2,1,0:T(4,128)(2,1)S(1)} %all_to_all.20.received), custom_call_target="tpu_custom_call" | custom-call | tf_op jit(solution)/shard_map/relay/pallas_call | solution.py:346
  33.9 14.7 %all_to_all.21.received = bf16[8,24,4,512]{3,2,1,0:T(4,128)(2,1)S(1)} all-to-all(bf16[8,24,4,512]{3,2,1,0:T(4,128)(2,1)S(1)} %relay.1), channel_id=1, replica_groups={{0,1,4,5,48,49,52,53},{3,2,7,6,51,50,55,54},{12,13,8,9,60,61,56,57},{15..., dimensions={0} | all-to-all | bytes 1572864 | tf_op jit(solution)/shard_map/all_to_all | solution.py:44
  48.7 0.8 sum_terms.1
  49.5 0.2 copy.20
  49.7 0.1 collective-permute-start.2
  49.8 3.4 %all-to-all-start.2 = ((bf16[8,32,512]{2,1,0:T(8,128)(2,1)}), bf16[8,32,512]{2,1,0:T(8,128)(2,1)S(1)}, u32[]{:S(2)}, u32[]{:S(2)}) async-start(bf16[8,32,512]{2,1,0:T(8,128)(2,1)} %get-tuple-element.20), calls=%async_computation.2 | async-start | bytes 524288 | tf_op jit(solution)/shard_map/all_to_all | solution.py:44
  53.2 9.0 %all-to-all-done.2 = bf16[8,32,512]{2,1,0:T(8,128)(2,1)S(1)} async-done(((bf16[8,32,512]{2,1,0:T(8,128)(2,1)}), bf16[8,32,512]{2,1,0:T(8,128)(2,1)S(1)}, u32[]{:S(2)}, u32[]{:S(2)}) %all-to-all-start.2) | async-done | bytes 262176 | tf_op jit(solution)/shard_map/all_to_all | solution.py:44
  62.2 0.0 collective-permute-start.1
  62.2 0.0 collective-permute-done.2
  62.3 0.2 broadcast_select_fusion
  62.5 0.4 copy.21
  62.9 0.0 copy-start
  62.9 0.0 copy-start.1
  62.9 0.0 copy-start.2
  62.9 0.0 copy-start.3
  62.9 0.0 copy-start.4
  62.9 0.1 reshape.28.right
  63.1 0.7 collective-permute-done.1.swapped
  63.8 2.1 %block_chain.1 = bf16[512,512]{1,0:T(8,128)(2,1)S(1)} custom-call(bf16[256,512]{1,0:T(8,128)(2,1)S(1)} %bitcast.22, bf16[256,512]{1,0:T(8,128)(2,1)S(1)} %collective-permute-done.1.swapped, bf16[512,512]{1,0:T(8,128)(2,1)S(1)} %reshape.28.right, bf16[64,512]{1,0:T(8,128)(2,1)S(1)} %get-tuple-element.38.left_t, f32[64,512]{1,0:T(8,128)S(1)} %add_bitcast_fusion.first, ...), custom_call_target="tpu_custom_call" | custom-call | tf_op jit(solution)/shard_map/block_chain/pallas_call | solution.py:129
  65.9 17.1 %all_to_all.22 = bf16[64,8,512]{2,1,0:T(8,128)(2,1)S(1)} all-to-all(bf16[64,8,512]{2,1,0:T(8,128)(2,1)S(1)} %bitcast.20), channel_id=1, replica_groups={{0,1,4,5,48,49,52,53,3,2,7,6,51,50,55,54,12,13,8,9,60,61,56,57,15,14,11..., dimensions={0} | all-to-all | bytes 1048576 | tf_op jit(solution)/shard_map/all_to_all | solution.py:44
  83.0 0.0 copy-done
  83.0 0.0 copy-done.1
  83.0 0.0 copy-done.2
  83.0 0.0 copy-done.3
  83.0 0.0 copy-done.4
  83.0 1.6 %new_state.1 = (f32[8,8,512]{2,1,0:T(8,128)}, f32[8,8,512]{2,1,0:T(8,128)}, f32[8,8,512]{2,1,0:T(8,128)}, f32[8,8,512]{2,1,0:T(8,128)}, bf16[8,4,512]{2,1,0:T(4,128)(2,1)}) custom-call(s32[2,8]{1,0:T(2,128)S(1)} %copy-done.4, bf16[8,64,512]{2,1,0:T(8,128)(2,1)S(1)} %bitcast.19, f32[8,8,512]{2,1,0:T(8,128)S(1)} %copy-done.2, f32[8,8,512]{2,1,0:T(8,128)S(1)} %copy-done.3, ...), custom_call_target="tpu_custom_call" | custom-call | tf_op jit(solution)/shard_map/new_state/pallas_call | solution.py:175
  (3 shorter events, 0.1 us)
Async XLA Ops:
  2.1 1.7 %collective-permute-start = (bf16[8,32,512]{2,1,0:T(8,128)(2,1)S(1)}, bf16[8,32,512]{2,1,0:T(8,128)(2,1)S(1)}, u32[]{:S(2)}, u32[]{:S(2)}) collective-permute-start(bf16[8,32,512]{2,1,0:T(8,128)(2,1)S(1)} %get-tuple-element.19), channel_id=1, source_target_pairs={{0,64},{64,0},{1,65},{65,1},{2,66},{66,2},{3,67},{67,3},{4,68},{68... | collective-permute-start | bytes 786440 | tf_op jit(solution)/shard_map/ppermute | solution.py:48
  49.7 12.6 %collective-permute-start.2 = (bf16[64,2,4,512]{3,0,2,1:T(8,128)(2,1)S(1)}, bf16[64,2,4,512]{3,0,2,1:T(8,128)(2,1)S(1)}, u32[]{:S(2)}, u32[]{:S(2)}) collective-permute-start(bf16[64,2,4,512]{3,0,2,1:T(8,128)(2,1)S(1)} %copy.20), channel_id=1, source_target_pairs={{0,64},{64,0},{1,65},{65,1},{2,66},{66,2},{3,67},{67,3},{4,68},{68... | collective-permute-start | bytes 1572872 | tf_op jit(solution)/shard_map/ppermute | solution.py:48
  49.8 12.5 %all-to-all-start.2 = ((bf16[8,32,512]{2,1,0:T(8,128)(2,1)}), bf16[8,32,512]{2,1,0:T(8,128)(2,1)S(1)}, u32[]{:S(2)}, u32[]{:S(2)}) async-start(bf16[8,32,512]{2,1,0:T(8,128)(2,1)} %get-tuple-element.20), calls=%async_computation.2 | async-start | bytes 524288 | tf_op jit(solution)/shard_map/all_to_all | solution.py:44
  62.2 1.5 %collective-permute-start.1 = (bf16[256,512]{1,0:T(8,128)(2,1)S(1)}, bf16[256,512]{1,0:T(8,128)(2,1)S(1)}, u32[]{:S(2)}, u32[]{:S(2)}) collective-permute-start(bf16[256,512]{1,0:T(8,128)(2,1)S(1)} %bitcast.21), channel_id=1, source_target_pairs={{0,64},{64,0},{1,65},{65,1},{2,66},{66,2},{3,67},{67,3},{4,68},{68... | collective-permute-start | bytes 786440 | tf_op jit(solution)/shard_map/ppermute | solution.py:48
  62.9 20.1 %copy-start = (f32[8,8,512]{2,1,0:T(8,128)S(1)}, f32[8,8,512]{2,1,0:T(8,128)}, u32[]{:S(2)}) copy-start(f32[8,8,512]{2,1,0:T(8,128)} %first.1) | copy-start | bytes 393220
  62.9 20.1 %copy-start.1 = (f32[8,8,512]{2,1,0:T(8,128)S(1)}, f32[8,8,512]{2,1,0:T(8,128)}, u32[]{:S(2)}) copy-start(f32[8,8,512]{2,1,0:T(8,128)} %second.1) | copy-start | bytes 393220
  62.9 20.1 %copy-start.2 = (f32[8,8,512]{2,1,0:T(8,128)S(1)}, f32[8,8,512]{2,1,0:T(8,128)}, u32[]{:S(2)}) copy-start(f32[8,8,512]{2,1,0:T(8,128)} %gram_l.1) | copy-start | bytes 393220
  62.9 20.1 %copy-start.3 = (f32[8,8,512]{2,1,0:T(8,128)S(1)}, f32[8,8,512]{2,1,0:T(8,128)}, u32[]{:S(2)}) copy-start(f32[8,8,512]{2,1,0:T(8,128)} %gram_r.1) | copy-start | bytes 393220
  62.9 20.1 %copy-start.4 = (s32[2,8]{1,0:T(2,128)S(1)}, s32[2,8]{1,0:T(2,128)}, u32[]{:S(2)}) copy-start(s32[2,8]{1,0:T(2,128)} %slot_block.3) | copy-start | bytes 196

commit v9 on v6

--- a/solution.py
+++ b/solution.py
@@ -37,7 +37,7 @@
 FIRST = OVER_B[0] + OVER_G[1]
 SECOND = OVER_G[0] + OVER_B[1]
 BLOCK = OVER_G[0] + OVER_G[1]
-ALL = [[device(c, b, g) for b in EIGHT for g in EIGHT] for c in range(2)]
+ALL = [[c * GROUP * GROUP + dp for dp in range(GROUP * GROUP)] for c in range(2)]
 
 
 def exchange(x, groups):
@@ -118,9 +118,7 @@
     n, col = iota((size, 4 * picks), 0), iota((size, 4 * picks), 1)
     spread = one_hot(col == ((n & 7) - 4 * (1 - core)) * picks + (n >> 3))
     kept = (iota((size, size), 0) & 4) == 4 * core
-    result = jnp.where(kept, update, dot(spread, rows))
-    order = [PLACE[b, g] * 8 for b in EIGHT for g in EIGHT]
-    out[...] = jnp.concatenate([result[at : at + 8] for at in order], axis=0).astype(bf16)
+    out[...] = jnp.where(kept, update, dot(spread, rows)).astype(bf16)
 
 
 def chain(raw, *others):
@@ -136,15 +134,17 @@
     n, col = iota((24, width), 0), iota((24, width), 1)
     other = (col & 7) - 4 * (1 - core)
     kind = n >> 3
-    wanted = (other == kind) | ((kind == 2) & (other == 3))
+    source, lane = number(col >> 3)
+    wanted = ((other == kind) | ((kind == 2) & (other == 3))) & (lane == (n & 7))
     picks = []
     for slot in range(blocks):
         block = jnp.maximum(slot_block[core, slot], 0)
-        picks.append(one_hot(wanted & ((col >> 3) == block * 8 + (n & 7))))
+        picks.append(one_hot(wanted & (source == block)))
     share = jnp.where(slot_block[core, 0] >= 0, 1.0, 0.0)
     rows = dot(jnp.concatenate(picks, axis=0), home[...]) * share
     n, col = iota((4 * blocks, width), 0), iota((4 * blocks, width), 1)
-    sums = one_hot(((col >> 6) == (n >> 2)) & ((col & 7) - 4 * core == (n & 3)))
+    source = number(col >> 3)[0]
+    sums = one_hot((source == (n >> 2)) & ((col & 7) - 4 * core == (n & 3)))
     sums = dot(sums, home[...])
     copies = []
     for slot in range(blocks):

time: 84.8 us -> 85.5 us (level)
  no operation moved by 1% of the time
where the time goes in v9:
time: 85.5 us; the launch traced here: 85.1 us
  blocking collectives  60.9 us (71%)
  waiting for transfers between devices  9.69 us (11%)
  Pallas kernels  9.18 us (11%)
  starting transfers between devices  3.6 us (4%)
    all_to_all x3, blocking collectives, exchange(): return lax.all_to_all(x, AXES, 0, 0, axis_index_groups=groups, tiled=True)  60.9 us
    all_to_all x1, waiting for transfers between devices, exchange(): return lax.all_to_all(x, AXES, 0, 0, axis_index_groups=groups, tiled=True)  9.03 us
    all_to_all x1, starting transfers between devices, exchange(): return lax.all_to_all(x, AXES, 0, 0, axis_index_groups=groups, tiled=True)  3.42 us
    pallas_call x1, Pallas kernels, chain(): local_call(chain_kernel, 'block_chain', out, [WHOLE] * 6)(raw, *others)  2.14 us
  transfers between devices with their start and end apart: 4, of which 2 were waited for; matrix products, arithmetic and copies ran while one was open for 1% of the time, Pallas kernels for 2%

profile of v9, /device:TPU:0, one launch (start us, length us, event | category | flops | bytes accessed | tf_op | source)
XLA Modules:
  0.0 85.1 jit_solution(17341051989900836292)
XLA Ops:
  0.6 1.2 %state_halves.1 = (bf16[8,32,512]{2,1,0:T(8,128)(2,1)S(1)}, bf16[8,32,512]{2,1,0:T(8,128)(2,1)S(1)}) custom-call(bf16[8,8,512]{2,1,0:T(8,128)(2,1)} %left_t.1, bf16[8,8,512]{2,1,0:T(8,128)(2,1)} %right.1, f32[8,8,512]{2,1,0:T(8,128)} %first.3, f32[8,8,512]{2,1,0:T(8,128)} %second.3), custom_call_target="tpu_custom_call" | custom-call | tf_op jit(solution)/shard_map/state_halves/pallas_call | solution.py:218
  1.8 0.1 collective-permute-start
  1.9 1.6 %load_terms.1.loaded = bf16[8,72,4,512]{3,2,1,0:T(4,128)(2,1)S(1)} custom-call(bf16[8,8,8,4,512]{4,3,2,1,0:T(4,128)(2,1)} %bitcast.23, bf16[8,64,4,512]{3,2,1,0:T(4,128)(2,1)} %bitcast.24), custom_call_target="tpu_custom_call" | custom-call | bytes 4194304 | tf_op jit(solution)/shard_map/load_terms/pallas_call | solution.py:245
  3.5 0.0 collective-permute-done.given
  3.5 0.9 %pack_states.1 = bf16[8,72,4,512]{3,2,1,0:T(4,128)(2,1)S(1)} custom-call(s32[2,8]{1,0:T(2,128)} %slot_block.3, bf16[8,72,4,512]{3,2,1,0:T(4,128)(2,1)S(1)} %load_terms.1.loaded, bf16[8,32,512]{2,1,0:T(8,128)(2,1)S(1)} %get-tuple-element.14.keep, bf16[8,32,512]{2,1,0:T(8,128)(2,1)S(1)} %collective-permute-done.given), custom_call_target="tpu_custom_call", output_to_operand_aliasing={{}: (1, {})} | custom-call | tf_op jit(solution)/shard_map/pack_states/pallas_call | solution.py:283
  4.4 28.3 %all_to_all.20.received = bf16[8,72,4,512]{3,2,1,0:T(4,128)(2,1)S(1)} all-to-all(bf16[8,72,4,512]{3,2,1,0:T(4,128)(2,1)S(1)} %pack_states.1), channel_id=1, replica_groups={{0,3,12,15,16,19,28,31},{1,2,13,14,17,18,29,30},{4,7,8,11,20,23,24,27},..., dimensions={0} | all-to-all | bytes 4718592 | tf_op jit(solution)/shard_map/all_to_all | solution.py:44
  32.8 0.9 %relay.1 = bf16[8,24,4,512]{3,2,1,0:T(4,128)(2,1)S(1)} custom-call(bf16[8,72,4,512]{3,2,1,0:T(4,128)(2,1)S(1)} %all_to_all.20.received), custom_call_target="tpu_custom_call" | custom-call | tf_op jit(solution)/shard_map/relay/pallas_call | solution.py:323
  33.6 14.7 %all_to_all.21.received = bf16[8,24,4,512]{3,2,1,0:T(4,128)(2,1)S(1)} all-to-all(bf16[8,24,4,512]{3,2,1,0:T(4,128)(2,1)S(1)} %relay.1), channel_id=1, replica_groups={{0,1,4,5,48,49,52,53},{3,2,7,6,51,50,55,54},{12,13,8,9,60,61,56,57},{15..., dimensions={0} | all-to-all | bytes 1572864 | tf_op jit(solution)/shard_map/all_to_all | solution.py:44
  48.4 0.8 sum_terms.1
  49.2 0.2 copy.19
  49.4 0.1 collective-permute-start.2
  49.5 3.4 %all-to-all-start.2 = ((bf16[8,32,512]{2,1,0:T(8,128)(2,1)}), bf16[8,32,512]{2,1,0:T(8,128)(2,1)S(1)}, u32[]{:S(2)}, u32[]{:S(2)}) async-start(bf16[8,32,512]{2,1,0:T(8,128)(2,1)} %get-tuple-element.16), calls=%async_computation.2 | async-start | bytes 524288 | tf_op jit(solution)/shard_map/all_to_all | solution.py:44
  52.9 9.0 %all-to-all-done.2 = bf16[8,32,512]{2,1,0:T(8,128)(2,1)S(1)} async-done(((bf16[8,32,512]{2,1,0:T(8,128)(2,1)}), bf16[8,32,512]{2,1,0:T(8,128)(2,1)S(1)}, u32[]{:S(2)}, u32[]{:S(2)}) %all-to-all-start.2) | async-done | bytes 262176 | tf_op jit(solution)/shard_map/all_to_all | solution.py:44
  61.9 0.0 collective-permute-start.1
  61.9 0.0 collective-permute-done.2
  62.0 0.2 broadcast_select_fusion
  62.2 0.4 copy.20
  62.6 0.0 copy-start
  62.6 0.0 copy-start.1
  62.6 0.0 copy-start.2
  62.6 0.0 copy-start.3
  62.7 0.0 copy-start.4
  62.7 0.1 reshape.28.right
  62.8 0.7 collective-permute-done.1.swapped
  63.5 2.1 %block_chain.1 = bf16[512,512]{1,0:T(8,128)(2,1)S(1)} custom-call(bf16[256,512]{1,0:T(8,128)(2,1)S(1)} %bitcast.22, bf16[256,512]{1,0:T(8,128)(2,1)S(1)} %collective-permute-done.1.swapped, bf16[512,512]{1,0:T(8,128)(2,1)S(1)} %reshape.28.right, bf16[64,512]{1,0:T(8,128)(2,1)S(1)} %get-tuple-element.34.left_t, f32[64,512]{1,0:T(8,128)S(1)} %add_bitcast_fusion.first, ...), custom_call_target="tpu_custom_call" | custom-call | tf_op jit(solution)/shard_map/block_chain/pallas_call | solution.py:127
  65.6 17.8 %all_to_all.22 = bf16[64,8,512]{2,1,0:T(8,128)(2,1)S(1)} all-to-all(bf16[64,8,512]{2,1,0:T(8,128)(2,1)S(1)} %bitcast.20), channel_id=1, replica_groups={{0,1,2,3,4,5,6,7,8,9,10,11,12,13,14,15,16,17,18,19,20,21,22,23,24,25,26..., dimensions={0} | all-to-all | bytes 1048576 | tf_op jit(solution)/shard_map/all_to_all | solution.py:44
  83.4 0.0 copy-done
  83.4 0.0 copy-done.1
  83.4 0.0 copy-done.2
  83.4 0.0 copy-done.3
  83.4 0.0 copy-done.4
  83.4 1.7 %new_state.1 = (f32[8,8,512]{2,1,0:T(8,128)}, f32[8,8,512]{2,1,0:T(8,128)}, f32[8,8,512]{2,1,0:T(8,128)}, f32[8,8,512]{2,1,0:T(8,128)}, bf16[8,4,512]{2,1,0:T(4,128)(2,1)}) custom-call(s32[2,8]{1,0:T(2,128)S(1)} %copy-done.4, bf16[512,512]{1,0:T(8,128)(2,1)S(1)} %bitcast.19, f32[8,8,512]{2,1,0:T(8,128)S(1)} %copy-done.2, f32[8,8,512]{2,1,0:T(8,128)S(1)} %copy-done.3, ...), custom_call_target="tpu_custom_call" | custom-call | tf_op jit(solution)/shard_map/new_state/pallas_call | solution.py:180
  (3 shorter events, 0.1 us)
Async XLA Ops:
  1.8 1.7 %collective-permute-start = (bf16[8,32,512]{2,1,0:T(8,128)(2,1)S(1)}, bf16[8,32,512]{2,1,0:T(8,128)(2,1)S(1)}, u32[]{:S(2)}, u32[]{:S(2)}) collective-permute-start(bf16[8,32,512]{2,1,0:T(8,128)(2,1)S(1)} %get-tuple-element.15), channel_id=1, source_target_pairs={{0,64},{64,0},{1,65},{65,1},{2,66},{66,2},{3,67},{67,3},{4,68},{68... | collective-permute-start | bytes 786440 | tf_op jit(solution)/shard_map/ppermute | solution.py:48
  49.4 12.6 %collective-permute-start.2 = (bf16[64,2,4,512]{3,0,2,1:T(8,128)(2,1)S(1)}, bf16[64,2,4,512]{3,0,2,1:T(8,128)(2,1)S(1)}, u32[]{:S(2)}, u32[]{:S(2)}) collective-permute-start(bf16[64,2,4,512]{3,0,2,1:T(8,128)(2,1)S(1)} %copy.19), channel_id=1, source_target_pairs={{0,64},{64,0},{1,65},{65,1},{2,66},{66,2},{3,67},{67,3},{4,68},{68... | collective-permute-start | bytes 1572872 | tf_op jit(solution)/shard_map/ppermute | solution.py:48
  49.5 12.5 %all-to-all-start.2 = ((bf16[8,32,512]{2,1,0:T(8,128)(2,1)}), bf16[8,32,512]{2,1,0:T(8,128)(2,1)S(1)}, u32[]{:S(2)}, u32[]{:S(2)}) async-start(bf16[8,32,512]{2,1,0:T(8,128)(2,1)} %get-tuple-element.16), calls=%async_computation.2 | async-start | bytes 524288 | tf_op jit(solution)/shard_map/all_to_all | solution.py:44
  61.9 1.5 %collective-permute-start.1 = (bf16[256,512]{1,0:T(8,128)(2,1)S(1)}, bf16[256,512]{1,0:T(8,128)(2,1)S(1)}, u32[]{:S(2)}, u32[]{:S(2)}) collective-permute-start(bf16[256,512]{1,0:T(8,128)(2,1)S(1)} %bitcast.21), channel_id=1, source_target_pairs={{0,64},{64,0},{1,65},{65,1},{2,66},{66,2},{3,67},{67,3},{4,68},{68... | collective-permute-start | bytes 786440 | tf_op jit(solution)/shard_map/ppermute | solution.py:48
  62.6 20.8 %copy-start = (f32[8,8,512]{2,1,0:T(8,128)S(1)}, f32[8,8,512]{2,1,0:T(8,128)}, u32[]{:S(2)}) copy-start(f32[8,8,512]{2,1,0:T(8,128)} %first.3) | copy-start | bytes 393220
  62.6 20.8 %copy-start.1 = (f32[8,8,512]{2,1,0:T(8,128)S(1)}, f32[8,8,512]{2,1,0:T(8,128)}, u32[]{:S(2)}) copy-start(f32[8,8,512]{2,1,0:T(8,128)} %second.3) | copy-start | bytes 393220
  62.6 20.8 %copy-start.2 = (f32[8,8,512]{2,1,0:T(8,128)S(1)}, f32[8,8,512]{2,1,0:T(8,128)}, u32[]{:S(2)}) copy-start(f32[8,8,512]{2,1,0:T(8,128)} %gram_l.1) | copy-start | bytes 393220
  62.6 20.8 %copy-start.3 = (f32[8,8,512]{2,1,0:T(8,128)S(1)}, f32[8,8,512]{2,1,0:T(8,128)}, u32[]{:S(2)}) copy-start(f32[8,8,512]{2,1,0:T(8,128)} %gram_r.1) | copy-start | bytes 393220
  62.7 20.8 %copy-start.4 = (s32[2,8]{1,0:T(2,128)S(1)}, s32[2,8]{1,0:T(2,128)}, u32[]{:S(2)}) copy-start(s32[2,8]{1,0:T(2,128)} %slot_block.3) | copy-start | bytes 196

commit v10 on v4

--- a/solution.py
+++ b/solution.py
@@ -252,26 +252,31 @@
     blocks = out.shape[0]
     units = out.shape[1] - GROUP
     mine = slot_block[core, 0] >= 0
-    n, col = iota((32, 32), 0), iota((32, 32), 1)
-    turn = one_hot(col == (n & 3) * 8 + (n >> 2))
+    state = []
     for b in range(blocks):
         at = 0
         for owner in range(slot_block.shape[0]):
             for slot in range(blocks):
                 at += jnp.where(slot_block[owner, slot] == b, slot, 0)
-        rows = jnp.where(mine, keep[at], given[at])
-
-        def whole(b=b, rows=rows):
-            right = rows[:8].astype(jnp.float32)
+        state.append(jnp.where(mine, keep[at], given[at]))
+
+    def whole():
+        for b in range(blocks):
+            right = state[b][:8].astype(jnp.float32)
             out[b, units] = right[:4].astype(jnp.bfloat16)
             out[b, units + 1] = right[4:].astype(jnp.bfloat16)
 
-        def singles(b=b, rows=rows):
-            turned = dot(turn, rows).astype(jnp.bfloat16)
+    def singles():
+        size = 32 * blocks
+        n, col = iota((size, size), 0), iota((size, size), 1)
+        turn = one_hot(col == (n & ~31) + (n & 3) * 8 + ((n >> 2) & 7))
+        turned = dot(turn, jnp.concatenate(state, axis=0)).astype(jnp.bfloat16)
+        for b in range(blocks):
             for g in EIGHT:
-                out[g, units + b] = turned[4 * g : 4 * g + 4]
-
-        on_core(whole, singles)
+                at = 32 * b + 4 * g
+                out[g, units + b] = turned[at : at + 4]
+
+    on_core(whole, singles)
 
 
 def pack(slot_block, loaded, keep, given):

time: 84.8 us -> 84.7 us (level)
  no operation moved by 1% of the time
where the time goes in v10:
time: 84.7 us; the launch traced here: 84.3 us
  blocking collectives  60.2 us (71%)
  waiting for transfers between devices  9.69 us (11%)
  Pallas kernels  9.03 us (11%)
  starting transfers between devices  3.6 us (4%)
    all_to_all x3, blocking collectives, exchange(): return lax.all_to_all(x, AXES, 0, 0, axis_index_groups=groups, tiled=True)  60.2 us
    all_to_all x1, waiting for transfers between devices, exchange(): return lax.all_to_all(x, AXES, 0, 0, axis_index_groups=groups, tiled=True)  9.03 us
    all_to_all x1, starting transfers between devices, exchange(): return lax.all_to_all(x, AXES, 0, 0, axis_index_groups=groups, tiled=True)  3.42 us
    pallas_call x1, Pallas kernels, chain(): local_call(chain_kernel, 'block_chain', out, [WHOLE] * 6)(raw, *others)  2.14 us
  transfers between devices with their start and end apart: 4, of which 2 were waited for; matrix products, arithmetic and copies ran while one was open for 1% of the time, Pallas kernels for 2%

profile of v10, /device:TPU:0, one launch (start us, length us, event | category | flops | bytes accessed | tf_op | source)
XLA Modules:
  0.0 84.3 jit_solution(1007049212556732734)
XLA Ops:
  0.6 1.2 %state_halves.1 = (bf16[8,32,512]{2,1,0:T(8,128)(2,1)S(1)}, bf16[8,32,512]{2,1,0:T(8,128)(2,1)S(1)}) custom-call(bf16[8,8,512]{2,1,0:T(8,128)(2,1)} %left_t.1, bf16[8,8,512]{2,1,0:T(8,128)(2,1)} %right.1, f32[8,8,512]{2,1,0:T(8,128)} %first.3, f32[8,8,512]{2,1,0:T(8,128)} %second.3), custom_call_target="tpu_custom_call" | custom-call | tf_op jit(solution)/shard_map/state_halves/pallas_call | solution.py:213
  1.8 0.1 collective-permute-start
  1.9 1.6 %load_terms.1.loaded = bf16[8,72,4,512]{3,2,1,0:T(4,128)(2,1)S(1)} custom-call(bf16[8,8,8,4,512]{4,3,2,1,0:T(4,128)(2,1)} %bitcast.23, bf16[8,64,4,512]{3,2,1,0:T(4,128)(2,1)} %bitcast.24), custom_call_target="tpu_custom_call" | custom-call | bytes 4194304 | tf_op jit(solution)/shard_map/load_terms/pallas_call | solution.py:240
  3.5 0.0 collective-permute-done.given
  3.5 0.8 %pack_states.1 = bf16[8,72,4,512]{3,2,1,0:T(4,128)(2,1)S(1)} custom-call(s32[2,8]{1,0:T(2,128)} %slot_block.3, bf16[8,72,4,512]{3,2,1,0:T(4,128)(2,1)S(1)} %load_terms.1.loaded, bf16[8,32,512]{2,1,0:T(8,128)(2,1)S(1)} %get-tuple-element.14.keep, bf16[8,32,512]{2,1,0:T(8,128)(2,1)S(1)} %collective-permute-done.given), custom_call_target="tpu_custom_call", output_to_operand_aliasing={{}: (1, {})} | custom-call | tf_op jit(solution)/shard_map/pack_states/pallas_call | solution.py:283
  4.3 28.3 %all_to_all.20.received = bf16[8,72,4,512]{3,2,1,0:T(4,128)(2,1)S(1)} all-to-all(bf16[8,72,4,512]{3,2,1,0:T(4,128)(2,1)S(1)} %pack_states.1), channel_id=1, replica_groups={{0,3,12,15,16,19,28,31},{1,2,13,14,17,18,29,30},{4,7,8,11,20,23,24,27},..., dimensions={0} | all-to-all | bytes 4718592 | tf_op jit(solution)/shard_map/all_to_all | solution.py:44
  32.7 0.9 %relay.1 = bf16[8,24,4,512]{3,2,1,0:T(4,128)(2,1)S(1)} custom-call(bf16[8,72,4,512]{3,2,1,0:T(4,128)(2,1)S(1)} %all_to_all.20.received), custom_call_target="tpu_custom_call" | custom-call | tf_op jit(solution)/shard_map/relay/pallas_call | solution.py:323
  33.6 14.7 %all_to_all.21.received = bf16[8,24,4,512]{3,2,1,0:T(4,128)(2,1)S(1)} all-to-all(bf16[8,24,4,512]{3,2,1,0:T(4,128)(2,1)S(1)} %relay.1), channel_id=1, replica_groups={{0,1,4,5,48,49,52,53},{3,2,7,6,51,50,55,54},{12,13,8,9,60,61,56,57},{15..., dimensions={0} | all-to-all | bytes 1572864 | tf_op jit(solution)/shard_map/all_to_all | solution.py:44
  48.3 0.8 sum_terms.1
  49.1 0.2 copy.19
  49.3 0.1 collective-permute-start.2
  49.4 3.4 %all-to-all-start.2 = ((bf16[8,32,512]{2,1,0:T(8,128)(2,1)}), bf16[8,32,512]{2,1,0:T(8,128)(2,1)S(1)}, u32[]{:S(2)}, u32[]{:S(2)}) async-start(bf16[8,32,512]{2,1,0:T(8,128)(2,1)} %get-tuple-element.16), calls=%async_computation.2 | async-start | bytes 524288 | tf_op jit(solution)/shard_map/all_to_all | solution.py:44
  52.8 9.0 %all-to-all-done.2 = bf16[8,32,512]{2,1,0:T(8,128)(2,1)S(1)} async-done(((bf16[8,32,512]{2,1,0:T(8,128)(2,1)}), bf16[8,32,512]{2,1,0:T(8,128)(2,1)S(1)}, u32[]{:S(2)}, u32[]{:S(2)}) %all-to-all-start.2) | async-done | bytes 262176 | tf_op jit(solution)/shard_map/all_to_all | solution.py:44
  61.9 0.0 collective-permute-start.1
  61.9 0.0 collective-permute-done.2
  61.9 0.2 broadcast_select_fusion
  62.1 0.4 copy.20
  62.5 0.0 copy-start
  62.5 0.0 copy-start.1
  62.5 0.0 copy-start.2
  62.6 0.0 copy-start.3
  62.6 0.0 copy-start.4
  62.6 0.1 reshape.28.right
  62.7 0.7 collective-permute-done.1.swapped
  63.4 2.1 %block_chain.1 = bf16[512,512]{1,0:T(8,128)(2,1)S(1)} custom-call(bf16[256,512]{1,0:T(8,128)(2,1)S(1)} %bitcast.22, bf16[256,512]{1,0:T(8,128)(2,1)S(1)} %collective-permute-done.1.swapped, bf16[512,512]{1,0:T(8,128)(2,1)S(1)} %reshape.28.right, bf16[64,512]{1,0:T(8,128)(2,1)S(1)} %get-tuple-element.34.left_t, f32[64,512]{1,0:T(8,128)S(1)} %add_bitcast_fusion.first, ...), custom_call_target="tpu_custom_call" | custom-call | tf_op jit(solution)/shard_map/block_chain/pallas_call | solution.py:129
  65.5 17.1 %all_to_all.22 = bf16[64,8,512]{2,1,0:T(8,128)(2,1)S(1)} all-to-all(bf16[64,8,512]{2,1,0:T(8,128)(2,1)S(1)} %bitcast.20), channel_id=1, replica_groups={{0,1,4,5,48,49,52,53,3,2,7,6,51,50,55,54,12,13,8,9,60,61,56,57,15,14,11..., dimensions={0} | all-to-all | bytes 1048576 | tf_op jit(solution)/shard_map/all_to_all | solution.py:44
  82.6 0.0 copy-done
  82.6 0.0 copy-done.1
  82.6 0.0 copy-done.2
  82.6 0.0 copy-done.3
  82.6 0.0 copy-done.4
  82.6 1.6 %new_state.1 = (f32[8,8,512]{2,1,0:T(8,128)}, f32[8,8,512]{2,1,0:T(8,128)}, f32[8,8,512]{2,1,0:T(8,128)}, f32[8,8,512]{2,1,0:T(8,128)}, bf16[8,4,512]{2,1,0:T(4,128)(2,1)}) custom-call(s32[2,8]{1,0:T(2,128)S(1)} %copy-done.4, bf16[8,64,512]{2,1,0:T(8,128)(2,1)S(1)} %bitcast.19, f32[8,8,512]{2,1,0:T(8,128)S(1)} %copy-done.2, f32[8,8,512]{2,1,0:T(8,128)S(1)} %copy-done.3, ...), custom_call_target="tpu_custom_call" | custom-call | tf_op jit(solution)/shard_map/new_state/pallas_call | solution.py:175
  (3 shorter events, 0.1 us)
Async XLA Ops:
  1.8 1.7 %collective-permute-start = (bf16[8,32,512]{2,1,0:T(8,128)(2,1)S(1)}, bf16[8,32,512]{2,1,0:T(8,128)(2,1)S(1)}, u32[]{:S(2)}, u32[]{:S(2)}) collective-permute-start(bf16[8,32,512]{2,1,0:T(8,128)(2,1)S(1)} %get-tuple-element.15), channel_id=1, source_target_pairs={{0,64},{64,0},{1,65},{65,1},{2,66},{66,2},{3,67},{67,3},{4,68},{68... | collective-permute-start | bytes 786440 | tf_op jit(solution)/shard_map/ppermute | solution.py:48
  49.3 12.6 %collective-permute-start.2 = (bf16[64,2,4,512]{3,0,2,1:T(8,128)(2,1)S(1)}, bf16[64,2,4,512]{3,0,2,1:T(8,128)(2,1)S(1)}, u32[]{:S(2)}, u32[]{:S(2)}) collective-permute-start(bf16[64,2,4,512]{3,0,2,1:T(8,128)(2,1)S(1)} %copy.19), channel_id=1, source_target_pairs={{0,64},{64,0},{1,65},{65,1},{2,66},{66,2},{3,67},{67,3},{4,68},{68... | collective-permute-start | bytes 1572872 | tf_op jit(solution)/shard_map/ppermute | solution.py:48
  49.4 12.5 %all-to-all-start.2 = ((bf16[8,32,512]{2,1,0:T(8,128)(2,1)}), bf16[8,32,512]{2,1,0:T(8,128)(2,1)S(1)}, u32[]{:S(2)}, u32[]{:S(2)}) async-start(bf16[8,32,512]{2,1,0:T(8,128)(2,1)} %get-tuple-element.16), calls=%async_computation.2 | async-start | bytes 524288 | tf_op jit(solution)/shard_map/all_to_all | solution.py:44
  61.9 1.5 %collective-permute-start.1 = (bf16[256,512]{1,0:T(8,128)(2,1)S(1)}, bf16[256,512]{1,0:T(8,128)(2,1)S(1)}, u32[]{:S(2)}, u32[]{:S(2)}) collective-permute-start(bf16[256,512]{1,0:T(8,128)(2,1)S(1)} %bitcast.21), channel_id=1, source_target_pairs={{0,64},{64,0},{1,65},{65,1},{2,66},{66,2},{3,67},{67,3},{4,68},{68... | collective-permute-start | bytes 786440 | tf_op jit(solution)/shard_map/ppermute | solution.py:48
  62.5 20.1 %copy-start = (f32[8,8,512]{2,1,0:T(8,128)S(1)}, f32[8,8,512]{2,1,0:T(8,128)}, u32[]{:S(2)}) copy-start(f32[8,8,512]{2,1,0:T(8,128)} %first.3) | copy-start | bytes 393220
  62.5 20.1 %copy-start.1 = (f32[8,8,512]{2,1,0:T(8,128)S(1)}, f32[8,8,512]{2,1,0:T(8,128)}, u32[]{:S(2)}) copy-start(f32[8,8,512]{2,1,0:T(8,128)} %second.3) | copy-start | bytes 393220
  62.5 20.1 %copy-start.2 = (f32[8,8,512]{2,1,0:T(8,128)S(1)}, f32[8,8,512]{2,1,0:T(8,128)}, u32[]{:S(2)}) copy-start(f32[8,8,512]{2,1,0:T(8,128)} %gram_l.1) | copy-start | bytes 393220
  62.6 20.1 %copy-start.3 = (f32[8,8,512]{2,1,0:T(8,128)S(1)}, f32[8,8,512]{2,1,0:T(8,128)}, u32[]{:S(2)}) copy-start(f32[8,8,512]{2,1,0:T(8,128)} %gram_r.1) | copy-start | bytes 393220
  62.6 20.1 %copy-start.4 = (s32[2,8]{1,0:T(2,128)S(1)}, s32[2,8]{1,0:T(2,128)}, u32[]{:S(2)}) copy-start(s32[2,8]{1,0:T(2,128)} %slot_block.3) | copy-start | bytes 196

commit v11 on v10

--- a/solution.py
+++ b/solution.py
@@ -18,9 +18,8 @@
     b = g = 0
     for axis in range(3):
         place = (dp >> (2 * axis)) & 3
-        wrap, inner = place >> 1, (place ^ (place >> 1)) & 1
-        b += (inner if axis == 2 else wrap) << axis
-        g += (wrap if axis == 2 else inner) << axis
+        b += (place >> 1) << axis
+        g += ((place ^ (place >> 1)) & 1) << axis
     return b, g
 
 

time: 84.7 us -> 84.6 us (level)
  waiting for transfers between devices: 9.69 us -> 8.48 us
  blocking collectives: 60.2 us -> 61.4 us
    all_to_all x1, waiting for transfers between devices: 9.03 us -> 7.82 us  [exchange(): return lax.all_to_all(x, AXES, 0, 0, axis_index_groups=groups, tiled=True)]
    all_to_all x3, blocking collectives: 60.2 us -> 61.4 us  [exchange(): return lax.all_to_all(x, AXES, 0, 0, axis_index_groups=groups, tiled=True)]
where the time goes in v11:
time: 84.6 us; the launch traced here: 84.3 us
  blocking collectives  61.4 us (73%)
  Pallas kernels  9.04 us (11%)
  waiting for transfers between devices  8.48 us (10%)
  starting transfers between devices  3.6 us (4%)
    all_to_all x3, blocking collectives, exchange(): return lax.all_to_all(x, AXES, 0, 0, axis_index_groups=groups, tiled=True)  61.4 us
    all_to_all x1, waiting for transfers between devices, exchange(): return lax.all_to_all(x, AXES, 0, 0, axis_index_groups=groups, tiled=True)  7.82 us
    all_to_all x1, starting transfers between devices, exchange(): return lax.all_to_all(x, AXES, 0, 0, axis_index_groups=groups, tiled=True)  3.42 us
    pallas_call x1, Pallas kernels, chain(): local_call(chain_kernel, 'block_chain', out, [WHOLE] * 6)(raw, *others)  2.15 us
  transfers between devices with their start and end apart: 4, of which 2 were waited for; matrix products, arithmetic and copies ran while one was open for 1% of the time, Pallas kernels for 2%

profile of v11, /device:TPU:0, one launch (start us, length us, event | category | flops | bytes accessed | tf_op | source)
XLA Modules:
  0.0 84.3 jit_solution(4948838164245796023)
XLA Ops:
  0.6 1.2 %state_halves.1 = (bf16[8,32,512]{2,1,0:T(8,128)(2,1)S(1)}, bf16[8,32,512]{2,1,0:T(8,128)(2,1)S(1)}) custom-call(bf16[8,8,512]{2,1,0:T(8,128)(2,1)} %left_t.1, bf16[8,8,512]{2,1,0:T(8,128)(2,1)} %right.1, f32[8,8,512]{2,1,0:T(8,128)} %first.3, f32[8,8,512]{2,1,0:T(8,128)} %second.3), custom_call_target="tpu_custom_call" | custom-call | tf_op jit(solution)/shard_map/state_halves/pallas_call | solution.py:212
  1.8 0.1 collective-permute-start
  1.9 1.6 %load_terms.1.loaded = bf16[8,72,4,512]{3,2,1,0:T(4,128)(2,1)S(1)} custom-call(bf16[8,8,8,4,512]{4,3,2,1,0:T(4,128)(2,1)} %bitcast.23, bf16[8,64,4,512]{3,2,1,0:T(4,128)(2,1)} %bitcast.24), custom_call_target="tpu_custom_call" | custom-call | bytes 4194304 | tf_op jit(solution)/shard_map/load_terms/pallas_call | solution.py:239
  3.5 0.0 collective-permute-done.given
  3.5 0.8 %pack_states.1 = bf16[8,72,4,512]{3,2,1,0:T(4,128)(2,1)S(1)} custom-call(s32[2,8]{1,0:T(2,128)} %slot_block.3, bf16[8,72,4,512]{3,2,1,0:T(4,128)(2,1)S(1)} %load_terms.1.loaded, bf16[8,32,512]{2,1,0:T(8,128)(2,1)S(1)} %get-tuple-element.14.keep, bf16[8,32,512]{2,1,0:T(8,128)(2,1)S(1)} %collective-permute-done.given), custom_call_target="tpu_custom_call", output_to_operand_aliasing={{}: (1, {})} | custom-call | tf_op jit(solution)/shard_map/pack_states/pallas_call | solution.py:282
  4.3 31.7 %all_to_all.20.received = bf16[8,72,4,512]{3,2,1,0:T(4,128)(2,1)S(1)} all-to-all(bf16[8,72,4,512]{3,2,1,0:T(4,128)(2,1)S(1)} %pack_states.1), channel_id=1, replica_groups={{0,3,12,15,48,51,60,63},{1,2,13,14,49,50,61,62},{4,7,8,11,52,55,56,59},..., dimensions={0} | all-to-all | bytes 4718592 | tf_op jit(solution)/shard_map/all_to_all | solution.py:43
  36.0 0.9 %relay.1 = bf16[8,24,4,512]{3,2,1,0:T(4,128)(2,1)S(1)} custom-call(bf16[8,72,4,512]{3,2,1,0:T(4,128)(2,1)S(1)} %all_to_all.20.received), custom_call_target="tpu_custom_call" | custom-call | tf_op jit(solution)/shard_map/relay/pallas_call | solution.py:322
  36.9 12.2 %all_to_all.21.received = bf16[8,24,4,512]{3,2,1,0:T(4,128)(2,1)S(1)} all-to-all(bf16[8,24,4,512]{3,2,1,0:T(4,128)(2,1)S(1)} %relay.1), channel_id=1, replica_groups={{0,1,4,5,16,17,20,21},{3,2,7,6,19,18,23,22},{12,13,8,9,28,29,24,25},{15..., dimensions={0} | all-to-all | bytes 1572864 | tf_op jit(solution)/shard_map/all_to_all | solution.py:43
  49.1 0.8 sum_terms.1
  49.9 0.2 copy.19
  50.1 0.1 collective-permute-start.2
  50.2 3.4 %all-to-all-start.2 = ((bf16[8,32,512]{2,1,0:T(8,128)(2,1)}), bf16[8,32,512]{2,1,0:T(8,128)(2,1)S(1)}, u32[]{:S(2)}, u32[]{:S(2)}) async-start(bf16[8,32,512]{2,1,0:T(8,128)(2,1)} %get-tuple-element.16), calls=%async_computation.2 | async-start | bytes 524288 | tf_op jit(solution)/shard_map/all_to_all | solution.py:43
  53.6 7.8 %all-to-all-done.2 = bf16[8,32,512]{2,1,0:T(8,128)(2,1)S(1)} async-done(((bf16[8,32,512]{2,1,0:T(8,128)(2,1)}), bf16[8,32,512]{2,1,0:T(8,128)(2,1)S(1)}, u32[]{:S(2)}, u32[]{:S(2)}) %all-to-all-start.2) | async-done | bytes 262176 | tf_op jit(solution)/shard_map/all_to_all | solution.py:43
  61.4 0.0 collective-permute-start.1
  61.4 0.0 collective-permute-done.2
  61.5 0.2 broadcast_select_fusion
  61.7 0.4 copy.20
  62.1 0.0 copy-start
  62.1 0.0 copy-start.1
  62.1 0.0 copy-start.2
  62.1 0.0 copy-start.3
  62.1 0.0 copy-start.4
  62.2 0.1 reshape.28.right
  62.3 0.7 collective-permute-done.1.swapped
  63.0 2.1 %block_chain.1 = bf16[512,512]{1,0:T(8,128)(2,1)S(1)} custom-call(bf16[256,512]{1,0:T(8,128)(2,1)S(1)} %bitcast.22, bf16[256,512]{1,0:T(8,128)(2,1)S(1)} %collective-permute-done.1.swapped, bf16[512,512]{1,0:T(8,128)(2,1)S(1)} %reshape.28.right, bf16[64,512]{1,0:T(8,128)(2,1)S(1)} %get-tuple-element.34.left_t, f32[64,512]{1,0:T(8,128)S(1)} %add_bitcast_fusion.first, ...), custom_call_target="tpu_custom_call" | custom-call | tf_op jit(solution)/shard_map/block_chain/pallas_call | solution.py:128
  65.1 17.5 %all_to_all.22 = bf16[64,8,512]{2,1,0:T(8,128)(2,1)S(1)} all-to-all(bf16[64,8,512]{2,1,0:T(8,128)(2,1)S(1)} %bitcast.20), channel_id=1, replica_groups={{0,1,4,5,16,17,20,21,3,2,7,6,19,18,23,22,12,13,8,9,28,29,24,25,15,14,11..., dimensions={0} | all-to-all | bytes 1048576 | tf_op jit(solution)/shard_map/all_to_all | solution.py:43
  82.6 0.0 copy-done
  82.6 0.0 copy-done.1
  82.6 0.0 copy-done.2
  82.6 0.0 copy-done.3
  82.6 0.0 copy-done.4
  82.6 1.6 %new_state.1 = (f32[8,8,512]{2,1,0:T(8,128)}, f32[8,8,512]{2,1,0:T(8,128)}, f32[8,8,512]{2,1,0:T(8,128)}, f32[8,8,512]{2,1,0:T(8,128)}, bf16[8,4,512]{2,1,0:T(4,128)(2,1)}) custom-call(s32[2,8]{1,0:T(2,128)S(1)} %copy-done.4, bf16[8,64,512]{2,1,0:T(8,128)(2,1)S(1)} %bitcast.19, f32[8,8,512]{2,1,0:T(8,128)S(1)} %copy-done.2, f32[8,8,512]{2,1,0:T(8,128)S(1)} %copy-done.3, ...), custom_call_target="tpu_custom_call" | custom-call | tf_op jit(solution)/shard_map/new_state/pallas_call | solution.py:174
  (3 shorter events, 0.1 us)
Async XLA Ops:
  1.8 1.7 %collective-permute-start = (bf16[8,32,512]{2,1,0:T(8,128)(2,1)S(1)}, bf16[8,32,512]{2,1,0:T(8,128)(2,1)S(1)}, u32[]{:S(2)}, u32[]{:S(2)}) collective-permute-start(bf16[8,32,512]{2,1,0:T(8,128)(2,1)S(1)} %get-tuple-element.15), channel_id=1, source_target_pairs={{0,64},{64,0},{1,65},{65,1},{2,66},{66,2},{3,67},{67,3},{4,68},{68... | collective-permute-start | bytes 786440 | tf_op jit(solution)/shard_map/ppermute | solution.py:47
  50.1 11.4 %collective-permute-start.2 = (bf16[64,2,4,512]{3,0,2,1:T(8,128)(2,1)S(1)}, bf16[64,2,4,512]{3,0,2,1:T(8,128)(2,1)S(1)}, u32[]{:S(2)}, u32[]{:S(2)}) collective-permute-start(bf16[64,2,4,512]{3,0,2,1:T(8,128)(2,1)S(1)} %copy.19), channel_id=1, source_target_pairs={{0,64},{64,0},{1,65},{65,1},{2,66},{66,2},{3,67},{67,3},{4,68},{68... | collective-permute-start | bytes 1572872 | tf_op jit(solution)/shard_map/ppermute | solution.py:47
  50.2 11.3 %all-to-all-start.2 = ((bf16[8,32,512]{2,1,0:T(8,128)(2,1)}), bf16[8,32,512]{2,1,0:T(8,128)(2,1)S(1)}, u32[]{:S(2)}, u32[]{:S(2)}) async-start(bf16[8,32,512]{2,1,0:T(8,128)(2,1)} %get-tuple-element.16), calls=%async_computation.2 | async-start | bytes 524288 | tf_op jit(solution)/shard_map/all_to_all | solution.py:43
  61.4 1.5 %collective-permute-start.1 = (bf16[256,512]{1,0:T(8,128)(2,1)S(1)}, bf16[256,512]{1,0:T(8,128)(2,1)S(1)}, u32[]{:S(2)}, u32[]{:S(2)}) collective-permute-start(bf16[256,512]{1,0:T(8,128)(2,1)S(1)} %bitcast.21), channel_id=1, source_target_pairs={{0,64},{64,0},{1,65},{65,1},{2,66},{66,2},{3,67},{67,3},{4,68},{68... | collective-permute-start | bytes 786440 | tf_op jit(solution)/shard_map/ppermute | solution.py:47
  62.1 20.5 %copy-start = (f32[8,8,512]{2,1,0:T(8,128)S(1)}, f32[8,8,512]{2,1,0:T(8,128)}, u32[]{:S(2)}) copy-start(f32[8,8,512]{2,1,0:T(8,128)} %first.3) | copy-start | bytes 393220
  62.1 20.5 %copy-start.1 = (f32[8,8,512]{2,1,0:T(8,128)S(1)}, f32[8,8,512]{2,1,0:T(8,128)}, u32[]{:S(2)}) copy-start(f32[8,8,512]{2,1,0:T(8,128)} %second.3) | copy-start | bytes 393220
  62.1 20.5 %copy-start.2 = (f32[8,8,512]{2,1,0:T(8,128)S(1)}, f32[8,8,512]{2,1,0:T(8,128)}, u32[]{:S(2)}) copy-start(f32[8,8,512]{2,1,0:T(8,128)} %gram_l.1) | copy-start | bytes 393220
  62.1 20.5 %copy-start.3 = (f32[8,8,512]{2,1,0:T(8,128)S(1)}, f32[8,8,512]{2,1,0:T(8,128)}, u32[]{:S(2)}) copy-start(f32[8,8,512]{2,1,0:T(8,128)} %gram_r.1) | copy-start | bytes 393220
  62.1 20.5 %copy-start.4 = (s32[2,8]{1,0:T(2,128)S(1)}, s32[2,8]{1,0:T(2,128)}, u32[]{:S(2)}) copy-start(s32[2,8]{1,0:T(2,128)} %slot_block.3) | copy-start | bytes 196
